TPU v7x, 32 devices: a whole 2x2x4 slice. The times are simulated.
32 devices in a mesh: lat: 8 (over y, x, core), chan: 4 (over z).
Axes of the slice: x: 2, y: 2, z: 4, core: 2. Of those that a mesh axis runs over, the one named last changes fastest.
Arguments:
- grid_field: bfloat16 [8, 2, 384, 1440], P('lat', None, 'chan'), may hold values from -6 to 6
- cotangent: bfloat16 [8, 2, 384, 1440], P('lat', None, 'chan'), may hold values from -6 to 6
- legendre: bfloat16 [40, 1361, 8], P('lat'), may hold values from -1.5 to 1.5
- spectral: float32 [384, 2, 720], P('chan'), may hold values from -3 to 3
- mixing: bfloat16 [384, 384], P(None, 'chan'), may hold values from -0.3125 to 0.3125
- pair_table: int32 [40], replicated, may hold values from 0 to 39, each once
Outputs:
- block_output: bfloat16 [8, 2, 384, 1440], P('lat', None, 'chan')
- grad_input: bfloat16 [8, 2, 384, 1440], P('lat', None, 'chan')
- grad_weights: float32 [384, 2, 720], P('chan')
- grad_mixing: float32 [384, 384], P(None, 'chan')
Inputs may be any that keep to these rules, and one draw needn't show every extreme that they name: `pair_table`: each pair p stands for the orders p and 79 - p, whose degree ranges together fill 1361 coefficients. Index i of lat owns the slots i * 5 to (i + 1) * 5 - 1.
All inputs are finite; a program needn't handle non-finite values.
Results may differ from a plain program's by a relative error of at most 0.0067.
Values may be sent and summed in bfloat16 or wider, within the bound.
A program may use at most 128 MiB of HBM per device.

v0:
```python
import math

import jax
import jax.numpy as jnp
from jax import lax
from jax.sharding import PartitionSpec as P


def dft_basis(orders, longitudes):
    lon_index = jnp.arange(longitudes, dtype=jnp.int32)
    turns = lon_index[:, None] * orders[None, :] % longitudes
    angles = turns.astype(jnp.float32) * (2.0 * math.pi / longitudes)
    norm_scale = 1.0 / math.sqrt(longitudes)
    basis = jnp.stack([jnp.cos(angles) * norm_scale, -jnp.sin(angles) * norm_scale], axis=1)
    return basis.astype(jnp.bfloat16)


def even_odd(spectrum):
    return jnp.stack(
        [spectrum[:, 0] + spectrum[:, 1], spectrum[:, 0] - spectrum[:, 1]], axis=1
    ).astype(jnp.bfloat16)


def local(grid_field, cotangent, legendre, spectral, mixing, pair_table):
    lat_count = lax.axis_size("lat")
    owned = legendre.shape[0]
    packed = legendre.shape[1]
    npairs = legendre.shape[2]
    degrees = spectral.shape[2]
    chan_width = grid_field.shape[2]
    longitudes = grid_field.shape[3]
    order_count = 2 * owned * lat_count
    slot_orders = jnp.stack([pair_table, order_count - 1 - pair_table], axis=1).reshape(-1)
    basis = dft_basis(slot_orders, longitudes)
    weight_m = jnp.where(slot_orders == 0, 1.0, 2.0).astype(jnp.float32)
    spec_x = jnp.einsum("khcj,jrm->khcrm", grid_field, basis, preferred_element_type=jnp.float32)
    spec_g = (
        jnp.einsum("khcj,jrm->khcrm", cotangent, basis, preferred_element_type=jnp.float32)
        * weight_m
    )
    recv_x, recv_g = (
        lax.all_to_all(even_odd(spec_x), "lat", split_axis=4, concat_axis=0, tiled=True),
        lax.all_to_all(even_odd(spec_g), "lat", split_axis=4, concat_axis=0, tiled=True),
    )
    owner_shape = (npairs, 2, chan_width, 2, owned, 2)
    recv_x = recv_x.reshape(owner_shape)
    recv_g = recv_g.reshape(owner_shape)
    slot_start = lax.axis_index("lat") * owned
    lower = lax.dynamic_slice_in_dim(pair_table, slot_start, owned)
    position = jnp.arange(packed, dtype=jnp.int32)[None, :]
    lower_col = lower[:, None]
    leading = position < degrees - lower_col
    degree = jnp.where(leading, lower_col + position, position - (degrees - order_count + 1))
    order = jnp.where(leading, lower_col, order_count - 1 - lower_col)
    half_pick = jnp.where(leading, 0, 1)
    parity = (degree + order) % 2
    two_index = jnp.arange(2, dtype=jnp.int32)
    selector = (
        (half_pick[:, None, None, :] == two_index[None, :, None, None])
        & (parity[:, None, None, :] == two_index[None, None, :, None])
    ).astype(jnp.float32)

    def analyse(received):
        variants = jnp.einsum(
            "pqk,kecrph->phercq", legendre, received, preferred_element_type=jnp.float32
        )
        return jnp.sum(variants * selector[:, :, :, None, None, :], axis=(1, 2))

    coeff_x = analyse(recv_x)
    coeff_g = analyse(recv_g)
    weight_rows = jnp.transpose(spectral, (1, 0, 2))
    weight_pad = jnp.concatenate(
        [weight_rows, jnp.zeros((2, chan_width, packed), jnp.float32)], axis=2
    )
    weight_tail = jnp.concatenate(
        [jnp.zeros((2, chan_width, degrees - order_count + 1), jnp.float32), weight_rows], axis=2
    )
    picked_lead = jax.vmap(
        lambda start_row: lax.dynamic_slice_in_dim(weight_pad, start_row, packed, 2)
    )(lower)
    picked = jnp.where(leading[:, None, None, :], picked_lead, weight_tail[None])
    real_w, imag_w = (picked[:, 0], picked[:, 1])
    real_x, imag_x = (coeff_x[:, 0], coeff_x[:, 1])
    real_g, imag_g = (coeff_g[:, 0], coeff_g[:, 1])
    filtered = jnp.stack(
        [real_w * real_x - imag_w * imag_x, real_w * imag_x + imag_w * real_x], axis=1
    ).astype(jnp.bfloat16)
    back_coeff = jnp.stack(
        [real_w * real_g + imag_w * imag_g, real_w * imag_g - imag_w * real_g], axis=1
    ).astype(jnp.bfloat16)
    grad_term = jnp.stack(
        [real_g * real_x + imag_g * imag_x, imag_g * real_x - real_g * imag_x], axis=1
    )
    grad_rows = jnp.zeros((2, chan_width, degrees + packed), jnp.float32)
    for slot in range(owned):
        head_part = jnp.where(leading[slot][None, None, :], grad_term[slot], 0.0)
        current = lax.dynamic_slice_in_dim(grad_rows, lower[slot], packed, 2)
        grad_rows = lax.dynamic_update_slice_in_dim(grad_rows, current + head_part, lower[slot], 2)
    tail_part = jnp.sum(jnp.where(leading[:, None, None, :], 0.0, grad_term), axis=0)
    grad_local = jnp.transpose(
        grad_rows[:, :, :degrees] + tail_part[:, :, degrees - order_count + 1 :], (1, 0, 2)
    )

    def synthesize(coeff):
        masked = (
            coeff[:, None, None].astype(jnp.float32) * selector[:, :, :, None, None, :]
        ).astype(jnp.bfloat16)
        both = jnp.einsum(
            "pqk,phercq->kecrph", legendre, masked, preferred_element_type=jnp.float32
        )
        return even_odd(both.reshape(npairs, 2, chan_width, 2, 2 * owned))

    row_y, row_dx = (
        lax.all_to_all(synthesize(filtered), "lat", split_axis=0, concat_axis=4, tiled=True),
        lax.all_to_all(synthesize(back_coeff), "lat", split_axis=0, concat_axis=4, tiled=True),
    )
    filtered_grid = jnp.einsum(
        "khcrm,jrm->khcj",
        row_y * weight_m.astype(jnp.bfloat16),
        basis,
        preferred_element_type=jnp.float32,
    )
    back_grid = jnp.einsum("khcrm,jrm->khcj", row_dx, basis, preferred_element_type=jnp.float32)
    field_full, cot_full, mixing_full = (
        lax.all_gather(grid_field, "chan", axis=2, tiled=True),
        lax.all_gather(cotangent, "chan", axis=2, tiled=True),
        lax.all_gather(mixing, "chan", axis=1, tiled=True),
    )
    mixing_own = lax.dynamic_slice_in_dim(
        mixing_full, lax.axis_index("chan") * chan_width, chan_width, 0
    )
    skip_path = jnp.einsum("khij,io->khoj", field_full, mixing, preferred_element_type=jnp.float32)
    back_skip = jnp.einsum(
        "khoj,io->khij", cot_full, mixing_own, preferred_element_type=jnp.float32
    )
    mixing_grad = jnp.einsum(
        "khij,khoj->io", field_full, cotangent, preferred_element_type=jnp.float32
    )
    block_output = (filtered_grid + skip_path).astype(jnp.bfloat16)
    grad_input = (back_grid + back_skip).astype(jnp.bfloat16)
    weight_sum, mixing_sum = lax.psum((grad_local, mixing_grad), "lat")
    grad_weights = weight_sum / math.sqrt(order_count)
    grad_mixing = mixing_sum / math.sqrt(2 * npairs * longitudes)
    return (block_output, grad_input, grad_weights, grad_mixing)


def solution(mesh):
    in_specs = (
        P("lat", None, "chan", None),
        P("lat", None, "chan", None),
        P("lat", None, None),
        P("chan", None, None),
        P(None, "chan"),
        P(),
    )
    out_specs = (
        P("lat", None, "chan", None),
        P("lat", None, "chan", None),
        P("chan", None, None),
        P(None, "chan"),
    )
    return jax.shard_map(local, mesh=mesh, in_specs=in_specs, out_specs=out_specs, check_vma=False)
```

profile of v0, /device:TPU:0, one launch (start us, length us, event | category | flops | bytes accessed | tf_op | source)
XLA Modules:
  0.0 258.7 jit_solution(5115653758928864037)
XLA Ops:
  7.2 2.6 copy.59
  12.0 2.2 multiply_convert_fusion.3
  14.3 1.6 fusion.16
  16.7 5.2 %all-to-all-start.2 = ((bf16[1,2,96,2,80]{2,1,3,0,4:T(2,128)(2,1)}), bf16[1,2,96,2,80]{2,1,3,0,4:T(2,128)(2,1)}, u32[]{:S(2)}, u32[]{:S(2)}) async-start(bf16[1,2,96,2,80]{2,1,3,0,4:T(2,128)(2,1)} %copy.61), calls=%async_computation.2 | async-start | bytes 163840 | tf_op jit(solution)/shard_map/all_to_all | solution.py:43
  21.9 1.4 copy.71
  28.0 13.5 %while.2 = (s32[]{:T(128)}, f32[2,96,2081]{2,1,0:T(8,128)S(1)}, s32[5,3]{0,1:T(4,128)S(1)}, f32[5,2,96,1361]{3,2,1,0:T(8,128)}) while((s32[]{:T(128)}, f32[2,96,2081]{2,1,0:T(8,128)S(1)}, s32[5,3]{0,1:T(4,128)S(1)}, f32[5,2,96,1361]{3,2,1,0:T(8,128)}) %tuple.52), condition=%wide.while_cond.clone, body=%wide.while_body.sunk.clone | while | flops 2 | bytes 2127705 | solution.py:79
  28.7 2.0 bitcast_dynamic-update-slice_fusion.3
  31.4 2.0 bitcast_dynamic-update-slice_fusion.3
  34.1 2.1 bitcast_dynamic-update-slice_fusion.3
  36.8 2.0 bitcast_dynamic-update-slice_fusion.3
  39.5 2.0 bitcast_dynamic-update-slice_fusion.3
  43.2 5.4 %broadcast_select_fusion = f32[5,2,96,1361]{3,2,1,0:T(8,128)} fusion(f32[5,2,96,1361]{3,2,1,0:T(8,128)} %get-tuple-element.11, f32[2,96,1361]{2,1,0:T(8,128)S(1)} %concatenate.39, pred[5,1361]{1,0:T(8,128)(4,1)S(1)} %iota_compare_fusion.2), kind=kLoop, calls=%fused_computation.33 | loop fusion | flops 1306560 | bytes 11504533 | tf_op jit(solution)/shard_map/jit(_where)/select_n | solution.py:81
  48.6 18.2 %all_gather.10 = bf16[384,384]{0,1:T(8,128)(2,1)} all-gather(bf16[384,96]{0,1:T(8,128)(2,1)S(1)} %copy-done.19), channel_id=1, replica_groups=mesh['lat'=8,'chan'=4] {'chan'}, dimensions={1}, use_global_device_ids=true | all-gather | bytes 368640 | tf_op jit(solution)/shard_map/all_gather | solution.py:127
  77.0 4.0 %all-to-all-start = ((bf16[1,2,96,2,80]{2,1,3,0,4:T(2,128)(2,1)}), bf16[1,2,96,2,80]{2,1,3,0,4:T(2,128)(2,1)S(1)}, u32[]{:S(2)}, u32[]{:S(2)}) async-start(bf16[1,2,96,2,80]{2,1,3,0,4:T(2,128)(2,1)} %copy.50), calls=%async_computation | async-start | bytes 163840 | tf_op jit(solution)/shard_map/all_to_all | solution.py:42
  81.0 6.7 %fusion = f32[5,2,96,1361]{3,2,1,0:T(8,128)} fusion(f32[5,2,2,1361]{3,1,2,0:T(2,128)S(1)} %and_convert_fusion, bf16[5,1361,8]{1,2,0:T(8,128)(2,1)S(1)} %copy-done, bf16[8,2,96,2,5,2]{2,1,3,5,4,0:T(2,128)(2,1)} %bitcast.75), kind=kOutput, calls=%fused_computation.3 | convolution fusion | flops 92765760 | bytes 5505440 | tf_op jit(solution)/shard_map/pqk,kecrph->phercq/dot_general | solution.py:64
  87.8 3.7 %fusion.1 = f32[5,2,96,1361]{3,2,1,0:T(8,128)S(1)} fusion(f32[5,2,2,1361]{3,1,2,0:T(2,128)S(1)} %and_convert_fusion, bf16[5,1361,8]{1,2,0:T(8,128)(2,1)S(1)} %copy-done, bf16[8,2,96,2,5,2]{2,1,3,5,4,0:T(2,128)(2,1)S(1)} %bitcast.179), kind=kOutput, calls=%fused_computation.5 | convolution fusion | flops 92765760 | bytes 5505440 | tf_op jit(solution)/shard_map/pqk,kecrph->phercq/dot_general | solution.py:64
  91.5 5.4 %add_convert_fusion = (bf16[5,1,96,1361]{3,2,1,0:T(8,128)(2,1)}, bf16[5,1,96,1361]{3,2,1,0:T(8,128)(2,1)}) fusion(f32[5,2,96,1361]{3,2,1,0:T(8,128)S(1)} %copy-done.6, f32[5,2,96,1361]{3,2,1,0:T(8,128)} %broadcast_select_fusion), kind=kLoop, calls=%fused_computation.30 | loop fusion | flops 5226240 | bytes 13065600 | tf_op jit(solution)/shard_map/convert.2
  96.9 2.7 %multiply_add_fusion = (f32[5,1,96,1361]{3,2,1,0:T(8,128)S(1)}, f32[5,1,96,1361]{3,2,1,0:T(8,128)S(1)}, bf16[5,1,96,1361]{3,2,1,0:T(8,128)(2,1)}, bf16[5,1,96,1361]{3,2,1,0:T(8,128)(2,1)}) fusion(f32[5,2,96,1361]{3,2,1,0:T(8,128)S(1)} %copy-done.6, f32[5,2,96,1361]{3,2,1,0:T(8,128)S(1)} %fusion.1, f32[5,2,96,1361]{3,2,1,0:T(8,128)S(1)} %bitcast.170), kind=kLoop, calls=%fused_computation.28 | loop fusion | flops 9145920 | bytes 23518080 | tf_op jit(solution)/shard_map/add | solution.py:92
  99.5 1.2 fusion.22
  101.4 1.3 broadcast_in_dim.145
  102.7 6.5 %dynamic_update_slice.15 = f32[2,96,2081]{2,1,0:T(8,128)} dynamic-update-slice(f32[2,96,2081]{2,1,0:T(8,128)} %broadcast_in_dim.145, f32[2,96,1361]{2,1,0:T(8,128)} %fusion.22, s32[]{:T(128)} %constant.26.clone.1, s32[]{:T(128)} %constant.26.clone.1, s32[]{:T(128)S(6)} %select_n.126) | dynamic-update-slice | bytes 2090500 | tf_op jit(solution)/shard_map/dynamic_update_slice | solution.py:98
  109.2 2.8 %fusion.26 = f32[2,96,1361]{2,1,0:T(8,128)} fusion(f32[5,1,96,1361]{3,2,1,0:T(8,128)S(1)} %get-tuple-element.41, f32[5,1,96,1361]{3,2,1,0:T(8,128)} %copy-done.1, f32[2,96,2081]{2,1,0:T(8,128)} %dynamic_update_slice.15, s32[]{:T(128)S(6)} %select_n.127, pred[1361]{0:T(1024)(128)(4,1)S(1)} %copy-done.24), kind=kLoop, calls=%fused_computation.56 | loop fusion | flops 783936 | bytes 7318101 | tf_op jit(solution)/shard_map/add | solution.py:98
  112.0 6.5 %dynamic_update_slice.16 = f32[2,96,2081]{2,1,0:T(8,128)} dynamic-update-slice(f32[2,96,2081]{2,1,0:T(8,128)} %dynamic_update_slice.15, f32[2,96,1361]{2,1,0:T(8,128)} %fusion.26, s32[]{:T(128)} %constant.26.clone.1, s32[]{:T(128)} %constant.26.clone.1, s32[]{:T(128)S(6)} %select_n.127) | dynamic-update-slice | bytes 2090500 | tf_op jit(solution)/shard_map/dynamic_update_slice | solution.py:98
  118.5 2.8 %fusion.30 = f32[2,96,1361]{2,1,0:T(8,128)} fusion(f32[5,1,96,1361]{3,2,1,0:T(8,128)S(1)} %get-tuple-element.41, f32[5,1,96,1361]{3,2,1,0:T(8,128)} %copy-done.1, f32[2,96,2081]{2,1,0:T(8,128)} %dynamic_update_slice.16, s32[]{:T(128)S(6)} %select_n.129, pred[1361]{0:T(1024)(128)(4,1)S(1)} %copy-done.23), kind=kLoop, calls=%fused_computation.60 | loop fusion | flops 783936 | bytes 7318101 | tf_op jit(solution)/shard_map/add | solution.py:98
  121.3 6.5 %dynamic_update_slice.17 = f32[2,96,2081]{2,1,0:T(8,128)} dynamic-update-slice(f32[2,96,2081]{2,1,0:T(8,128)} %dynamic_update_slice.16, f32[2,96,1361]{2,1,0:T(8,128)} %fusion.30, s32[]{:T(128)} %constant.26.clone.1, s32[]{:T(128)} %constant.26.clone.1, s32[]{:T(128)S(6)} %select_n.129) | dynamic-update-slice | bytes 2090500 | tf_op jit(solution)/shard_map/dynamic_update_slice | solution.py:98
  127.8 2.2 maximum_convert_fusion
  131.2 9.1 %multiply_convert_fusion = (bf16[5,2,2,2,96,1361]{5,4,1,3,2,0:T(8,128)(2,1)}, bf16[5,2,2,2,96,1361]{5,4,1,3,2,0:T(8,128)(2,1)}) fusion(f32[5,2,96,1361]{3,2,1,0:T(8,128)S(1)} %maximum_convert_fusion.1, f32[5,2,2,1361]{3,1,2,0:T(2,128)S(1)} %copy-done.18, f32[5,2,96,1361]{3,2,1,0:T(8,128)S(1)} %maximum_convert_fusion), kind=kLoop, calls=%fused_computation.6 | loop fusion | flops 20904960 | bytes 31466320 | tf_op jit(solution)/shard_map/convert_element_type | solution.py:107
  140.3 6.4 %fusion.2 = f32[5,2,2,2,96,8]{4,5,3,2,1,0:T(8,128)S(1)} fusion(bf16[5,2,2,2,96,1361]{5,4,1,3,2,0:T(8,128)(2,1)} %get-tuple-element.61, bf16[5,1361,8]{1,2,0:T(8,128)(2,1)S(1)} %copy-done), kind=kOutput, calls=%fused_computation.8 | convolution fusion | flops 83619840 | bytes 10684240 | tf_op jit(solution)/shard_map/pqk,phercq->kecrph/dot_general | solution.py:108
  146.7 1.3 fusion.34
  148.7 6.5 %dynamic_update_slice.18 = f32[2,96,2081]{2,1,0:T(8,128)} dynamic-update-slice(f32[2,96,2081]{2,1,0:T(8,128)} %dynamic_update_slice.17, f32[2,96,1361]{2,1,0:T(8,128)} %fusion.34, s32[]{:T(128)} %constant.26.clone.1, s32[]{:T(128)} %constant.26.clone.1, s32[]{:T(128)S(6)} %select_n.131) | dynamic-update-slice | bytes 2090500 | tf_op jit(solution)/shard_map/dynamic_update_slice | solution.py:98
  157.0 3.9 %all-to-all-start.3 = ((bf16[8,2,96,2,10]{2,3,4,1,0:T(2,128)(2,1)}), bf16[8,2,96,2,10]{2,3,4,1,0:T(2,128)(2,1)S(1)}, u32[]{:S(2)}, u32[]{:S(2)}) async-start(bf16[8,2,96,2,10]{2,3,4,1,0:T(2,128)(2,1)} %pad_maximum_fusion.5), calls=%async_computation.3 | async-start | bytes 163840 | tf_op jit(solution)/shard_map/all_to_all | solution.py:115
  160.9 6.4 %fusion.4 = f32[5,2,2,2,96,8]{4,5,3,2,1,0:T(8,128)S(1)} fusion(bf16[5,2,2,2,96,1361]{5,4,1,3,2,0:T(8,128)(2,1)} %get-tuple-element.62, bf16[5,1361,8]{1,2,0:T(8,128)(2,1)S(1)} %copy-done), kind=kOutput, calls=%fused_computation.10 | convolution fusion | flops 83619840 | bytes 10684240 | tf_op jit(solution)/shard_map/pqk,phercq->kecrph/dot_general | solution.py:108
  167.5 1.4 fusion.7
  169.0 1.3 fusion.38
  171.2 6.5 %dynamic_update_slice.19 = f32[2,96,2081]{2,1,0:T(8,128)} dynamic-update-slice(f32[2,96,2081]{2,1,0:T(8,128)} %dynamic_update_slice.18, f32[2,96,1361]{2,1,0:T(8,128)} %fusion.38, s32[]{:T(128)} %constant.26.clone.1, s32[]{:T(128)} %constant.26.clone.1, s32[]{:T(128)S(6)} %select_n.133) | dynamic-update-slice | bytes 2090500 | tf_op jit(solution)/shard_map/dynamic_update_slice | solution.py:98
  177.6 4.2 %all-to-all-start.1 = ((bf16[8,2,96,2,10]{2,3,4,1,0:T(2,128)(2,1)}), bf16[8,2,96,2,10]{2,3,4,1,0:T(2,128)(2,1)S(1)}, u32[]{:S(2)}, u32[]{:S(2)}) async-start(bf16[8,2,96,2,10]{2,3,4,1,0:T(2,128)(2,1)} %pad_maximum_fusion.3), calls=%async_computation.1 | async-start | bytes 163840 | tf_op jit(solution)/shard_map/all_to_all | solution.py:114
  181.9 2.1 fusion.39
  184.1 2.9 %all-to-all-done.1 = bf16[8,2,96,2,10]{2,3,4,1,0:T(2,128)(2,1)S(1)} async-done(((bf16[8,2,96,2,10]{2,3,4,1,0:T(2,128)(2,1)}), bf16[8,2,96,2,10]{2,3,4,1,0:T(2,128)(2,1)S(1)}, u32[]{:S(2)}, u32[]{:S(2)}) %all-to-all-start.1) | async-done | bytes 61472 | tf_op jit(solution)/shard_map/all_to_all | solution.py:114
  187.2 6.1 %copy.60 = bf16[1,2,384,1440]{2,3,1,0:T(8,128)(2,1)S(1)} copy(bf16[1,2,384,1440]{3,1,0,2:T(2,128)(2,1)} %all-gather.3.cloned.1.call-done) | data formatting | bytes 4423680 | tf_op jit(solution)/shard_map/all_gather | solution.py:125
  193.3 1.2 fusion.17
  194.6 6.8 %copy.72 = bf16[1,2,384,1440]{2,3,1,0:T(8,128)(2,1)} copy(bf16[1,2,384,1440]{3,1,0,2:T(2,128)(2,1)} %all-gather.5.cloned.1.call-done) | data formatting | bytes 4423680 | tf_op jit(solution)/shard_map/all_gather | solution.py:126
  201.4 2.7 %convolution_bitcast_fusion = f32[1,2,96,1440]{3,2,1,0:T(8,128)S(1)} fusion(bf16[1,2,384,1440]{2,3,1,0:T(8,128)(2,1)} %copy.72, bf16[384,384]{0,1:T(8,128)(2,1)} %all_gather.10, s32[]{:T(128)S(6)} %select_n.124), kind=kOutput, calls=%fused_computation.34 | convolution fusion | flops 212336640 | bytes 3416068 | tf_op jit(solution)/shard_map/khoj,io->khij/dot_general | solution.py:133
  204.1 1.2 fusion.11
  206.1 1.2 fusion.10
  207.3 40.9 %all-reduce.6.cloned.1.call-done = (f32[96,2,720]{2,0,1:T(8,128)}, f32[384,96]{0,1:T(8,128)}) async-done(((f32[96,2,720]{2,0,1:T(8,128)}, f32[384,96]{0,1:T(8,128)}), (f32[96,2,720]{2,0,1:T(8,128)}, f32[384,96]{0,1:T(8,128)})) %all-reduce.6.cloned.1.call-update) | async-done | bytes 700432 | tf_op jit(solution)/shard_map/psum | solution.py:141
  248.2 1.1 broadcast_multiply_fusion
  249.3 1.3 copy.73
  250.6 1.6 broadcast_multiply_fusion.1
  (121 shorter events, 19.7 us)
Async XLA Ops:
  7.2 73.9 %copy-start = (bf16[5,1361,8]{1,2,0:T(8,128)(2,1)S(1)}, bf16[5,1361,8]{1,2,0:T(8,128)(2,1)}, u32[]{:S(2)}) copy-start(bf16[5,1361,8]{1,2,0:T(8,128)(2,1)} %param.8) | copy-start | bytes 326644
  7.2 14.7 %copy-start.10 = (bf16[1,2,96,1440]{3,2,1,0:T(8,128)(2,1)S(1)}, bf16[1,2,96,1440]{3,2,1,0:T(8,128)(2,1)}, u32[]{:S(2)}) copy-start(bf16[1,2,96,1440]{3,2,1,0:T(8,128)(2,1)} %param.7) | copy-start | bytes 1658884
  7.2 180.0 %all-gather.3.cloned.1.call-start = ((), (), s32[]{:S(2)}) async-start(), calls=%async_computation.4 | async-start | bytes 2949120 | tf_op jit(solution)/shard_map/all_gather | solution.py:125
  9.8 14.2 %copy-start.15 = (bf16[1,2,96,1440]{3,2,1,0:T(8,128)(2,1)S(1)}, bf16[1,2,96,1440]{3,2,1,0:T(8,128)(2,1)}, u32[]{:S(2)}) copy-start(bf16[1,2,96,1440]{3,2,1,0:T(8,128)(2,1)} %param.6) | copy-start | bytes 1658884
  14.2 10.8 %copy-start.11 = (bf16[1440,1,80]{0,2,1:T(8,128)(2,1)}, bf16[1440,1,80]{0,2,1:T(8,128)(2,1)S(1)}, u32[]{:S(2)}) copy-start(bf16[1440,1,80]{0,2,1:T(8,128)(2,1)S(1)} %get-tuple-element.70) | copy-start | bytes 691204
  14.3 10.8 %copy-start.13 = (bf16[1440,1,80]{0,2,1:T(8,128)(2,1)}, bf16[1440,1,80]{0,2,1:T(8,128)(2,1)S(1)}, u32[]{:S(2)}) copy-start(bf16[1440,1,80]{0,2,1:T(8,128)(2,1)S(1)} %get-tuple-element.71) | copy-start | bytes 691204
  14.3 10.7 %copy-start.16 = (f32[96,2,720]{2,1,0:T(2,128)S(1)}, f32[96,2,720]{2,1,0:T(2,128)}, u32[]{:S(2)}) copy-start(f32[96,2,720]{2,1,0:T(2,128)} %param.9) | copy-start | bytes 1658884
  16.7 60.3 %all-to-all-start.2 = ((bf16[1,2,96,2,80]{2,1,3,0,4:T(2,128)(2,1)}), bf16[1,2,96,2,80]{2,1,3,0,4:T(2,128)(2,1)}, u32[]{:S(2)}, u32[]{:S(2)}) async-start(bf16[1,2,96,2,80]{2,1,3,0,4:T(2,128)(2,1)} %copy.61), calls=%async_computation.2 | async-start | bytes 163840 | tf_op jit(solution)/shard_map/all_to_all | solution.py:43
  21.8 172.7 %all-gather.5.cloned.1.call-start = ((), (), s32[]{:S(2)}) async-start(), calls=%async_computation.5 | async-start | bytes 2949120 | tf_op jit(solution)/shard_map/all_gather | solution.py:126
  25.0 0.7 copy-start.27
  25.7 2.3 copy-start.21
  26.3 1.7 copy-start.26
  43.1 44.6 %copy-start.17 = (f32[5,2,2,1361]{3,1,2,0:T(2,128)}, f32[5,2,2,1361]{3,1,2,0:T(2,128)S(1)}, u32[]{:S(2)}) copy-start(f32[5,2,2,1361]{3,1,2,0:T(2,128)S(1)} %and_convert_fusion) | copy-start | bytes 326644
  43.2 5.4 %copy-start.19 = (bf16[384,96]{0,1:T(8,128)(2,1)S(1)}, bf16[384,96]{0,1:T(8,128)(2,1)}, u32[]{:S(2)}) copy-start(bf16[384,96]{0,1:T(8,128)(2,1)} %param.10) | copy-start | bytes 221188
  77.0 10.8 %all-to-all-start = ((bf16[1,2,96,2,80]{2,1,3,0,4:T(2,128)(2,1)}), bf16[1,2,96,2,80]{2,1,3,0,4:T(2,128)(2,1)S(1)}, u32[]{:S(2)}, u32[]{:S(2)}) async-start(bf16[1,2,96,2,80]{2,1,3,0,4:T(2,128)(2,1)} %copy.50), calls=%async_computation | async-start | bytes 163840 | tf_op jit(solution)/shard_map/all_to_all | solution.py:42
  87.8 3.7 %copy-start.6 = (f32[5,2,96,1361]{3,2,1,0:T(8,128)S(1)}, f32[5,2,96,1361]{3,2,1,0:T(8,128)}, u32[]{:S(2)}) copy-start(f32[5,2,96,1361]{3,2,1,0:T(8,128)} %fusion) | copy-start | bytes 15678724
  87.8 9.1 %slice-start = ((s8[5406720]{0:T(1024)(128)(4,1)}), s8[1212416]{0:T(1024)(128)(4,1)S(1)}, s32[]{:S(2)}) async-start(s8[5406720]{0:T(1024)(128)(4,1)} %bitcast.169), calls=%async_computation.7 | async-start | bytes 2424832
  91.5 5.4 %slice-start.1 = ((s8[5406720]{0:T(1024)(128)(4,1)}), s8[4194304]{0:T(1024)(128)(4,1)S(1)}, s32[]{:S(2)}) async-start(s8[5406720]{0:T(1024)(128)(4,1)} %bitcast.169), calls=%async_computation.8 | async-start | bytes 8388608
  96.9 2.7 %copy-start.25 = (pred[1361]{0:T(1024)(128)(4,1)S(1)}, pred[1361]{0:T(1024)(128)(4,1)}, u32[]{:S(2)}) copy-start(pred[1361]{0:T(1024)(128)(4,1)} %get-tuple-element.27) | copy-start | bytes 4087
  99.5 1.8 copy-start.1
  101.4 7.8 %copy-start.24 = (pred[1361]{0:T(1024)(128)(4,1)S(1)}, pred[1361]{0:T(1024)(128)(4,1)}, u32[]{:S(2)}) copy-start(pred[1361]{0:T(1024)(128)(4,1)} %get-tuple-element.26) | copy-start | bytes 4087
  109.2 9.3 %copy-start.23 = (pred[1361]{0:T(1024)(128)(4,1)S(1)}, pred[1361]{0:T(1024)(128)(4,1)}, u32[]{:S(2)}) copy-start(pred[1361]{0:T(1024)(128)(4,1)} %get-tuple-element.25) | copy-start | bytes 4087
  127.8 2.2 copy-start.7
  127.8 2.5 copy-start.8
  130.3 0.9 copy-start.18
  140.3 6.4 %copy-start.2 = (f32[5,1,96,1361]{3,2,1,0:T(8,128)S(1)}, f32[5,1,96,1361]{3,2,1,0:T(8,128)}, u32[]{:S(2)}) copy-start(f32[5,1,96,1361]{3,2,1,0:T(8,128)} %copy-done.1) | copy-start | bytes 7839364
  140.3 6.4 %copy-start.4 = (f32[2,96,2081]{2,1,0:T(8,128)S(1)}, f32[2,96,2081]{2,1,0:T(8,128)}, u32[]{:S(2)}) copy-start(f32[2,96,2081]{2,1,0:T(8,128)} %dynamic_update_slice.17) | copy-start | bytes 4794628
  140.3 6.5 %copy-start.22 = (pred[1361]{0:T(1024)(128)(4,1)S(1)}, pred[1361]{0:T(1024)(128)(4,1)}, u32[]{:S(2)}) copy-start(pred[1361]{0:T(1024)(128)(4,1)} %get-tuple-element.28) | copy-start | bytes 4087
  157.0 20.7 %all-to-all-start.3 = ((bf16[8,2,96,2,10]{2,3,4,1,0:T(2,128)(2,1)}), bf16[8,2,96,2,10]{2,3,4,1,0:T(2,128)(2,1)S(1)}, u32[]{:S(2)}, u32[]{:S(2)}) async-start(bf16[8,2,96,2,10]{2,3,4,1,0:T(2,128)(2,1)} %pad_maximum_fusion.5), calls=%async_computation.3 | async-start | bytes 163840 | tf_op jit(solution)/shard_map/all_to_all | solution.py:115
  160.9 6.6 %copy-start.3 = (f32[5,1,96,1361]{3,2,1,0:T(8,128)S(1)}, f32[5,1,96,1361]{3,2,1,0:T(8,128)}, u32[]{:S(2)}) copy-start(f32[5,1,96,1361]{3,2,1,0:T(8,128)} %copy-done.1) | copy-start | bytes 7839364
  167.5 1.5 copy-start.5
  170.4 11.5 %copy-start.9 = (f32[2,96,1361]{2,1,0:T(8,128)S(1)}, f32[2,96,1361]{2,1,0:T(8,128)}, u32[]{:S(2)}) copy-start(f32[2,96,1361]{2,1,0:T(8,128)} %fusion.7) | copy-start | bytes 3135748
  170.4 16.6 %copy-start.28 = (bf16[80]{0:T(256)(128)(2,1)S(1)}, bf16[80]{0:T(256)(128)(2,1)}, u32[]{:S(2)}) copy-start(bf16[80]{0:T(256)(128)(2,1)} %get-tuple-element.69) | copy-start | bytes 484
  177.6 9.3 %all-to-all-start.1 = ((bf16[8,2,96,2,10]{2,3,4,1,0:T(2,128)(2,1)}), bf16[8,2,96,2,10]{2,3,4,1,0:T(2,128)(2,1)S(1)}, u32[]{:S(2)}, u32[]{:S(2)}) async-start(bf16[8,2,96,2,10]{2,3,4,1,0:T(2,128)(2,1)} %pad_maximum_fusion.3), calls=%async_computation.1 | async-start | bytes 163840 | tf_op jit(solution)/shard_map/all_to_all | solution.py:114
  181.8 66.4 %all-reduce.6.cloned.1.call-start = ((), (), s32[]{:S(2)}) async-start(), calls=%async_computation.6 | async-start | bytes 1474560 | tf_op jit(solution)/shard_map/psum | solution.py:141
  201.4 2.7 %copy-start.12 = (bf16[1440,1,80]{0,2,1:T(8,128)(2,1)S(1)}, bf16[1440,1,80]{0,2,1:T(8,128)(2,1)}, u32[]{:S(2)}) copy-start(bf16[1440,1,80]{0,2,1:T(8,128)(2,1)} %copy-done.11) | copy-start | bytes 691204
  201.4 2.7 %copy-start.14 = (bf16[1440,1,80]{0,2,1:T(8,128)(2,1)S(1)}, bf16[1440,1,80]{0,2,1:T(8,128)(2,1)}, u32[]{:S(2)}) copy-start(bf16[1440,1,80]{0,2,1:T(8,128)(2,1)} %copy-done.13) | copy-start | bytes 691204
  201.4 3.9 %copy-start.20 = (bf16[384,96]{0,1:T(8,128)(2,1)S(1)}, bf16[384,96]{0,1:T(8,128)(2,1)}, u32[]{:S(2)}) copy-start(bf16[384,96]{0,1:T(8,128)(2,1)} %param.10) | copy-start | bytes 221188
Sparse Core Ops, SparseCore 0:
  10.2 57.8 all-gather.2
  70.2 49.2 all-gather.4
  194.7 53.4 all-reduce.5
where the time goes:
time: 261 us; the launch traced here: 259 us
  local copies, waits for them, and re-layouts  71.4 us (27%)
  other arithmetic  51.1 us (20%)
  waiting for transfers between devices  43.9 us (17%)
  matrix products  33 us (13%)
  between operations  23.6 us (9%)
  blocking collectives  18.2 us (7%)
  starting transfers between devices  17.5 us (7%)
    psum x1, waiting for transfers between devices, local(): weight_sum, mixing_sum = lax.psum((grad_local, mixing_grad), 'lat')  40.9 us
    dynamic_update_slice x5, local copies, waits for them, and re-layouts, local(): lax.dynamic_update_slice_in_dim(grad_rows, current + head_part, lower[slo...  32.4 us
    all_gather x1, blocking collectives, local(): lax.all_gather(mixing, 'chan', axis=1, tiled=True)  18.2 us
    gather x15, local copies, waits for them, and re-layouts  13.4 us
    dot_general x2, matrix products, synthesize(): jnp.einsum('pqk,phercq->kecrph', legendre, masked, preferred_element_type...  12.9 us
    dot_general x2, matrix products, analyse(): jnp.einsum('pqk,kecrph->phercq', legendre, received, preferred_element_ty...  10.4 us
    another operation x6, other arithmetic  9.65 us
    convert_element_type x1, other arithmetic, synthesize(): masked = (coeff[:, None, None].astype(jnp.float32) * selector[:, :, :, No...  9.07 us
  transfers between devices with their start and end apart: 7, of which 2 were waited for; matrix products, arithmetic and copies ran while one was open for 57% of the time, Pallas kernels for 0%

commit v1 on v0

--- a/solution.py
+++ b/solution.py
@@ -75,9 +75,9 @@
     weight_tail = jnp.concatenate(
         [jnp.zeros((2, chan_width, degrees - order_count + 1), jnp.float32), weight_rows], axis=2
     )
-    picked_lead = jax.vmap(
-        lambda start_row: lax.dynamic_slice_in_dim(weight_pad, start_row, packed, 2)
-    )(lower)
+    picked_lead = jnp.stack(
+        [lax.dynamic_slice_in_dim(weight_pad, lower[slot], packed, 2) for slot in range(owned)]
+    )
     picked = jnp.where(leading[:, None, None, :], picked_lead, weight_tail[None])
     real_w, imag_w = (picked[:, 0], picked[:, 1])
     real_x, imag_x = (coeff_x[:, 0], coeff_x[:, 1])

time: 261 us -> 244 us (0.935)
  local copies, waits for them, and re-layouts: 71.4 us -> 60.8 us
  other arithmetic: 51.1 us -> 45.8 us
    gather x15 -> x0, local copies, waits for them, and re-layouts: 13.4 us -> none
    dynamic_slice x0 -> x1, local copies, waits for them, and re-layouts: none -> 3.86 us  [local(): lax.dynamic_slice_in_dim(weight_pad, lower[slot], packed, 2)]
    select_n x1, other arithmetic: 5.4 us -> 2.78 us  [local(): jnp.where(leading[:, None, None, :], picked_lead, weight_tail[None])]
    unnamed x66 -> x54, local copies, waits for them, and re-layouts: 7.2 us -> 6.75 us
  transfers between devices with their start and end apart: 7 -> 7, of which waited for: 2 -> 2; matrix products, arithmetic and copies ran while one was open for 57% -> 54% of each run, Pallas kernels for 0% -> 0%
where the time goes in v1:
time: 244 us; the launch traced here: 242 us
  local copies, waits for them, and re-layouts  60.8 us (25%)
  other arithmetic  45.8 us (19%)
  waiting for transfers between devices  44.2 us (18%)
  matrix products  31.6 us (13%)
  between operations  23.8 us (10%)
  blocking collectives  17.9 us (7%)
  starting transfers between devices  17.7 us (7%)
    psum x1, waiting for transfers between devices, local(): weight_sum, mixing_sum = lax.psum((grad_local, mixing_grad), 'lat')  41.2 us
    dynamic_update_slice x5, local copies, waits for them, and re-layouts, local(): lax.dynamic_update_slice_in_dim(grad_rows, current + head_part, lower[slo...  32.4 us
    all_gather x1, blocking collectives, local(): lax.all_gather(mixing, 'chan', axis=1, tiled=True)  17.9 us
    dot_general x2, matrix products, synthesize(): jnp.einsum('pqk,phercq->kecrph', legendre, masked, preferred_element_type...  12.9 us
    dot_general x2, matrix products, analyse(): jnp.einsum('pqk,kecrph->phercq', legendre, received, preferred_element_ty...  9.7 us
    convert_element_type x1, other arithmetic, synthesize(): masked = (coeff[:, None, None].astype(jnp.float32) * selector[:, :, :, No...  9.06 us
    another operation x6, other arithmetic  9 us
    add x4, other arithmetic, local(): current + head_part  8.28 us
  transfers between devices with their start and end apart: 7, of which 2 were waited for; matrix products, arithmetic and copies ran while one was open for 54% of the time, Pallas kernels for 0%

profile of v1, /device:TPU:0, one launch (start us, length us, event | category | flops | bytes accessed | tf_op | source)
XLA Modules:
  0.0 241.8 jit_solution(9440944002188104553)
XLA Ops:
  7.2 2.6 %copy.56 = bf16[1,2,96,1440]{3,1,0,2:T(2,128)(2,1)} copy(bf16[1,2,96,1440]{3,2,1,0:T(8,128)(2,1)} %param.6) | data formatting | bytes 1105920 | tf_op args[0]
  9.8 0.7 subtract_bitcast_fusion
  11.9 2.2 multiply_convert_fusion.3
  14.2 1.6 fusion.16
  16.6 5.2 %all-to-all-start.2 = ((bf16[1,2,96,2,80]{2,1,3,0,4:T(2,128)(2,1)}), bf16[1,2,96,2,80]{2,1,3,0,4:T(2,128)(2,1)S(1)}, u32[]{:S(2)}, u32[]{:S(2)}) async-start(bf16[1,2,96,2,80]{2,1,3,0,4:T(2,128)(2,1)} %copy.58), calls=%async_computation.2 | async-start | bytes 163840 | tf_op jit(solution)/shard_map/all_to_all | solution.py:43
  21.9 1.4 copy.68
  34.2 3.9 %pad_dynamic-slice_fusion = (f32[2,96,1361]{2,0,1:T(2,128)S(1)}, f32[2,96,1361]{2,0,1:T(2,128)S(1)}, f32[2,96,1361]{2,0,1:T(2,128)S(1)}, f32[2,96,1361]{2,0,1:T(2,128)S(1)}, f32[2,96,1361]{2,0,1:T(2,128)S(1)}) fusion(s32[]{:T(128)S(6)} %select_n.122, f32[2,96,720]{2,0,1:T(2,128)S(1)} %bitcast.169, s32[]{:T(128)S(6)} %select_n.119, s32[]{:T(128)S(6)} %select_n.120, ...), kind=kLoop, calls=%fused_computation.40 | loop fusion | bytes 5779220 | tf_op jit(solution)/shard_map/dynamic_slice | solution.py:79
  38.9 2.8 %broadcast_select_fusion = f32[5,2,96,1361]{3,2,1,0:T(8,128)} fusion(f32[5,2,96,1361]{3,2,1,0:T(8,128)S(1)} %bitcast_dynamic-update-slice_fusion, f32[2,96,1361]{2,1,0:T(8,128)S(1)} %concatenate.35.clone, pred[5,1361]{1,0:T(8,128)(4,1)S(1)} %iota_compare_fusion.2), kind=kLoop, calls=%fused_computation.31 | loop fusion | flops 1306560 | bytes 11504533 | tf_op jit(solution)/shard_map/jit(_where)/select_n | solution.py:81
  41.9 17.9 %all_gather.10 = bf16[384,384]{0,1:T(8,128)(2,1)} all-gather(bf16[384,96]{0,1:T(8,128)(2,1)S(1)} %copy-done.17), channel_id=1, replica_groups=mesh['lat'=8,'chan'=4] {'chan'}, dimensions={1}, use_global_device_ids=true | all-gather | bytes 368640 | tf_op jit(solution)/shard_map/all_gather | solution.py:127
  60.6 4.1 %all-to-all-start = ((bf16[1,2,96,2,80]{2,1,3,0,4:T(2,128)(2,1)}), bf16[1,2,96,2,80]{2,1,3,0,4:T(2,128)(2,1)S(1)}, u32[]{:S(2)}, u32[]{:S(2)}) async-start(bf16[1,2,96,2,80]{2,1,3,0,4:T(2,128)(2,1)} %copy.47), calls=%async_computation | async-start | bytes 163840 | tf_op jit(solution)/shard_map/all_to_all | solution.py:42
  64.7 6.0 %fusion = f32[5,2,96,1361]{3,2,1,0:T(8,128)} fusion(f32[5,2,2,1361]{3,1,2,0:T(2,128)S(1)} %and_convert_fusion, bf16[5,1361,8]{1,2,0:T(8,128)(2,1)S(1)} %copy-done, bf16[8,2,96,2,5,2]{2,1,3,5,4,0:T(2,128)(2,1)S(1)} %bitcast.176), kind=kOutput, calls=%fused_computation.1 | convolution fusion | flops 92765760 | bytes 5505440 | tf_op jit(solution)/shard_map/pqk,kecrph->phercq/dot_general | solution.py:64
  70.7 3.7 %fusion.1 = f32[5,2,96,1361]{3,2,1,0:T(8,128)S(1)} fusion(f32[5,2,2,1361]{3,1,2,0:T(2,128)S(1)} %and_convert_fusion, bf16[5,1361,8]{1,2,0:T(8,128)(2,1)S(1)} %copy-done, bf16[8,2,96,2,5,2]{2,1,3,5,4,0:T(2,128)(2,1)S(1)} %bitcast.177), kind=kOutput, calls=%fused_computation.3 | convolution fusion | flops 92765760 | bytes 5505440 | tf_op jit(solution)/shard_map/pqk,kecrph->phercq/dot_general | solution.py:64
  74.4 5.7 %add_convert_fusion = (bf16[5,1,96,1361]{3,2,1,0:T(8,128)(2,1)}, bf16[5,1,96,1361]{3,2,1,0:T(8,128)(2,1)}) fusion(f32[5,2,96,1361]{3,2,1,0:T(8,128)S(1)} %copy-done.6, f32[5,2,96,1361]{3,2,1,0:T(8,128)} %broadcast_select_fusion), kind=kLoop, calls=%fused_computation.28 | loop fusion | flops 5226240 | bytes 13065600 | tf_op jit(solution)/shard_map/convert.2
  80.1 2.6 %multiply_add_fusion = (f32[5,1,96,1361]{3,2,1,0:T(8,128)S(1)}, f32[5,1,96,1361]{3,2,1,0:T(8,128)S(1)}, bf16[5,1,96,1361]{3,2,1,0:T(8,128)(2,1)}, bf16[5,1,96,1361]{3,2,1,0:T(8,128)(2,1)}) fusion(f32[5,2,96,1361]{3,2,1,0:T(8,128)S(1)} %copy-done.6, f32[5,2,96,1361]{3,2,1,0:T(8,128)S(1)} %fusion.1, f32[5,2,96,1361]{3,2,1,0:T(8,128)S(1)} %bitcast.167), kind=kLoop, calls=%fused_computation.26 | loop fusion | flops 9145920 | bytes 23518080 | tf_op jit(solution)/shard_map/add | solution.py:92
  82.7 1.2 fusion.22
  84.6 1.3 broadcast_in_dim.141
  85.9 6.5 %dynamic_update_slice.15 = f32[2,96,2081]{2,1,0:T(8,128)} dynamic-update-slice(f32[2,96,2081]{2,1,0:T(8,128)} %broadcast_in_dim.141, f32[2,96,1361]{2,1,0:T(8,128)} %fusion.22, s32[]{:T(128)} %constant.26.clone.1, s32[]{:T(128)} %constant.26.clone.1, s32[]{:T(128)S(6)} %select_n.118) | dynamic-update-slice | bytes 2090500 | tf_op jit(solution)/shard_map/dynamic_update_slice | solution.py:98
  92.4 2.8 %fusion.26 = f32[2,96,1361]{2,1,0:T(8,128)} fusion(f32[5,1,96,1361]{3,2,1,0:T(8,128)S(1)} %get-tuple-element.17, f32[5,1,96,1361]{3,2,1,0:T(8,128)} %copy-done.1, f32[2,96,2081]{2,1,0:T(8,128)} %dynamic_update_slice.15, s32[]{:T(128)S(6)} %select_n.119, pred[1361]{0:T(1024)(128)(4,1)S(1)} %get-tuple-element.10), kind=kLoop, calls=%fused_computation.59 | loop fusion | flops 783936 | bytes 7318101 | tf_op jit(solution)/shard_map/add | solution.py:98
  95.2 6.5 %dynamic_update_slice.16 = f32[2,96,2081]{2,1,0:T(8,128)} dynamic-update-slice(f32[2,96,2081]{2,1,0:T(8,128)} %dynamic_update_slice.15, f32[2,96,1361]{2,1,0:T(8,128)} %fusion.26, s32[]{:T(128)} %constant.26.clone.1, s32[]{:T(128)} %constant.26.clone.1, s32[]{:T(128)S(6)} %select_n.119) | dynamic-update-slice | bytes 2090500 | tf_op jit(solution)/shard_map/dynamic_update_slice | solution.py:98
  101.7 2.8 %fusion.30 = f32[2,96,1361]{2,1,0:T(8,128)} fusion(f32[5,1,96,1361]{3,2,1,0:T(8,128)S(1)} %get-tuple-element.17, f32[5,1,96,1361]{3,2,1,0:T(8,128)} %copy-done.1, f32[2,96,2081]{2,1,0:T(8,128)} %dynamic_update_slice.16, s32[]{:T(128)S(6)} %select_n.120, pred[1361]{0:T(1024)(128)(4,1)S(1)} %get-tuple-element.9), kind=kLoop, calls=%fused_computation.63 | loop fusion | flops 783936 | bytes 7318101 | tf_op jit(solution)/shard_map/add | solution.py:98
  104.5 6.5 %dynamic_update_slice.17 = f32[2,96,2081]{2,1,0:T(8,128)} dynamic-update-slice(f32[2,96,2081]{2,1,0:T(8,128)} %dynamic_update_slice.16, f32[2,96,1361]{2,1,0:T(8,128)} %fusion.30, s32[]{:T(128)} %constant.26.clone.1, s32[]{:T(128)} %constant.26.clone.1, s32[]{:T(128)S(6)} %select_n.120) | dynamic-update-slice | bytes 2090500 | tf_op jit(solution)/shard_map/dynamic_update_slice | solution.py:98
  110.9 2.2 maximum_convert_fusion
  113.9 9.1 %multiply_convert_fusion = (bf16[5,2,2,2,96,1361]{5,4,1,3,2,0:T(8,128)(2,1)}, bf16[5,2,2,2,96,1361]{5,4,1,3,2,0:T(8,128)(2,1)}) fusion(f32[5,2,96,1361]{3,2,1,0:T(8,128)S(1)} %maximum_convert_fusion.1, f32[5,2,2,1361]{3,1,2,0:T(2,128)S(1)} %and_convert_fusion, f32[5,2,96,1361]{3,2,1,0:T(8,128)S(1)} %maximum_convert_fusion), kind=kLoop, calls=%fused_computation.4 | loop fusion | flops 20904960 | bytes 31466320 | tf_op jit(solution)/shard_map/convert_element_type | solution.py:107
  122.9 6.4 %fusion.2 = f32[5,2,2,2,96,8]{4,5,3,2,1,0:T(8,128)S(1)} fusion(bf16[5,2,2,2,96,1361]{5,4,1,3,2,0:T(8,128)(2,1)} %get-tuple-element.42, bf16[5,1361,8]{1,2,0:T(8,128)(2,1)S(1)} %copy-done), kind=kOutput, calls=%fused_computation.6 | convolution fusion | flops 83619840 | bytes 10684240 | tf_op jit(solution)/shard_map/pqk,phercq->kecrph/dot_general | solution.py:108
  129.4 1.3 fusion.34
  131.4 6.5 %dynamic_update_slice.18 = f32[2,96,2081]{2,1,0:T(8,128)} dynamic-update-slice(f32[2,96,2081]{2,1,0:T(8,128)} %dynamic_update_slice.17, f32[2,96,1361]{2,1,0:T(8,128)} %fusion.34, s32[]{:T(128)} %constant.26.clone.1, s32[]{:T(128)} %constant.26.clone.1, s32[]{:T(128)S(6)} %select_n.121) | dynamic-update-slice | bytes 2090500 | tf_op jit(solution)/shard_map/dynamic_update_slice | solution.py:98
  137.8 1.0 add_convert_fusion.2
  138.8 0.8 pad_maximum_fusion.5
  139.6 4.2 %all-to-all-start.3 = ((bf16[8,2,96,2,10]{2,3,4,1,0:T(2,128)(2,1)}), bf16[8,2,96,2,10]{2,3,4,1,0:T(2,128)(2,1)S(1)}, u32[]{:S(2)}, u32[]{:S(2)}) async-start(bf16[8,2,96,2,10]{2,3,4,1,0:T(2,128)(2,1)} %pad_maximum_fusion.5), calls=%async_computation.3 | async-start | bytes 163840 | tf_op jit(solution)/shard_map/all_to_all | solution.py:115
  143.7 6.4 %fusion.4 = f32[5,2,2,2,96,8]{4,5,3,2,1,0:T(8,128)S(1)} fusion(bf16[5,2,2,2,96,1361]{5,4,1,3,2,0:T(8,128)(2,1)} %get-tuple-element.43, bf16[5,1361,8]{1,2,0:T(8,128)(2,1)S(1)} %copy-done), kind=kOutput, calls=%fused_computation.8 | convolution fusion | flops 83619840 | bytes 10684240 | tf_op jit(solution)/shard_map/pqk,phercq->kecrph/dot_general | solution.py:108
  150.3 1.4 fusion.7
  151.9 1.3 fusion.38
  153.2 0.8 pad_maximum_fusion.3
  154.0 6.5 %dynamic_update_slice.19 = f32[2,96,2081]{2,1,0:T(8,128)} dynamic-update-slice(f32[2,96,2081]{2,1,0:T(8,128)} %dynamic_update_slice.18, f32[2,96,1361]{2,1,0:T(8,128)} %fusion.38, s32[]{:T(128)} %constant.26.clone.1, s32[]{:T(128)} %constant.26.clone.1, s32[]{:T(128)S(6)} %select_n.122) | dynamic-update-slice | bytes 2090500 | tf_op jit(solution)/shard_map/dynamic_update_slice | solution.py:98
  160.5 4.2 %all-to-all-start.1 = ((bf16[8,2,96,2,10]{2,3,4,1,0:T(2,128)(2,1)}), bf16[8,2,96,2,10]{2,3,4,1,0:T(2,128)(2,1)S(1)}, u32[]{:S(2)}, u32[]{:S(2)}) async-start(bf16[8,2,96,2,10]{2,3,4,1,0:T(2,128)(2,1)} %pad_maximum_fusion.3), calls=%async_computation.1 | async-start | bytes 163840 | tf_op jit(solution)/shard_map/all_to_all | solution.py:114
  164.7 2.1 fusion.39
  166.9 2.9 %all-to-all-done.1 = bf16[8,2,96,2,10]{2,3,4,1,0:T(2,128)(2,1)S(1)} async-done(((bf16[8,2,96,2,10]{2,3,4,1,0:T(2,128)(2,1)}), bf16[8,2,96,2,10]{2,3,4,1,0:T(2,128)(2,1)S(1)}, u32[]{:S(2)}, u32[]{:S(2)}) %all-to-all-start.1) | async-done | bytes 61472 | tf_op jit(solution)/shard_map/all_to_all | solution.py:114
  170.0 6.1 %copy.57 = bf16[1,2,384,1440]{2,3,1,0:T(8,128)(2,1)S(1)} copy(bf16[1,2,384,1440]{3,1,0,2:T(2,128)(2,1)} %all-gather.3.cloned.1.call-done) | data formatting | bytes 4423680 | tf_op jit(solution)/shard_map/all_gather | solution.py:125
  176.1 1.2 fusion.17
  177.4 6.9 %copy.69 = bf16[1,2,384,1440]{2,3,1,0:T(8,128)(2,1)} copy(bf16[1,2,384,1440]{3,1,0,2:T(2,128)(2,1)} %all-gather.5.cloned.1.call-done) | data formatting | bytes 4423680 | tf_op jit(solution)/shard_map/all_gather | solution.py:126
  184.3 2.7 %convolution_bitcast_fusion = f32[1,2,96,1440]{3,2,1,0:T(8,128)S(1)} fusion(bf16[1,2,384,1440]{2,3,1,0:T(8,128)(2,1)} %copy.69, bf16[384,384]{0,1:T(8,128)(2,1)} %all_gather.10, s32[]{:T(128)S(6)} %select_n.130), kind=kOutput, calls=%fused_computation.32 | convolution fusion | flops 212336640 | bytes 3416068 | tf_op jit(solution)/shard_map/khoj,io->khij/dot_general | solution.py:133
  187.0 1.2 fusion.11
  188.1 0.8 convolution_bitcast_fusion.2
  188.9 1.2 fusion.10
  190.1 41.2 %all-reduce.5.cloned.1.call-done = (f32[96,2,720]{2,0,1:T(8,128)}, f32[384,96]{0,1:T(8,128)}) async-done(((f32[96,2,720]{2,0,1:T(8,128)}, f32[384,96]{0,1:T(8,128)}), (f32[96,2,720]{2,0,1:T(8,128)}, f32[384,96]{0,1:T(8,128)})) %all-reduce.5.cloned.1.call-update) | async-done | bytes 700432 | tf_op jit(solution)/shard_map/psum | solution.py:141
  231.3 1.1 broadcast_multiply_fusion
  232.5 1.3 copy.70
  233.7 1.6 broadcast_multiply_fusion.1
  (92 shorter events, 7.8 us)
Async XLA Ops:
  7.2 57.5 %copy-start = (bf16[5,1361,8]{1,2,0:T(8,128)(2,1)S(1)}, bf16[5,1361,8]{1,2,0:T(8,128)(2,1)}, u32[]{:S(2)}) copy-start(bf16[5,1361,8]{1,2,0:T(8,128)(2,1)} %param.8) | copy-start | bytes 326644
  7.2 14.7 %copy-start.11 = (bf16[1,2,96,1440]{3,2,1,0:T(8,128)(2,1)S(1)}, bf16[1,2,96,1440]{3,2,1,0:T(8,128)(2,1)}, u32[]{:S(2)}) copy-start(bf16[1,2,96,1440]{3,2,1,0:T(8,128)(2,1)} %param.7) | copy-start | bytes 1658884
  7.2 162.8 %all-gather.3.cloned.1.call-start = ((), (), s32[]{:S(2)}) async-start(), calls=%async_computation.4 | async-start | bytes 2949120 | tf_op jit(solution)/shard_map/all_gather | solution.py:125
  9.8 13.5 %copy-start.19 = (s32[40]{0:T(128)S(1)}, s32[40]{0:T(128)}, u32[]{:S(2)}) copy-start(s32[40]{0:T(128)} %param.11) | copy-start | bytes 484
  9.8 20.7 %copy-start.16 = (bf16[1,2,96,1440]{3,2,1,0:T(8,128)(2,1)S(1)}, bf16[1,2,96,1440]{3,2,1,0:T(8,128)(2,1)}, u32[]{:S(2)}) copy-start(bf16[1,2,96,1440]{3,2,1,0:T(8,128)(2,1)} %param.6) | copy-start | bytes 1658884
  14.2 16.7 %copy-start.12 = (bf16[1440,1,80]{0,2,1:T(8,128)(2,1)}, bf16[1440,1,80]{0,2,1:T(8,128)(2,1)S(1)}, u32[]{:S(2)}) copy-start(bf16[1440,1,80]{0,2,1:T(8,128)(2,1)S(1)} %get-tuple-element.51) | copy-start | bytes 691204
  14.2 16.7 %copy-start.14 = (bf16[1440,1,80]{0,2,1:T(8,128)(2,1)}, bf16[1440,1,80]{0,2,1:T(8,128)(2,1)S(1)}, u32[]{:S(2)}) copy-start(bf16[1440,1,80]{0,2,1:T(8,128)(2,1)S(1)} %get-tuple-element.52) | copy-start | bytes 691204
  14.2 16.7 %copy-start.10 = (f32[96,2,720]{2,1,0:T(2,128)S(1)}, f32[96,2,720]{2,1,0:T(2,128)}, u32[]{:S(2)}) copy-start(f32[96,2,720]{2,1,0:T(2,128)} %param.9) | copy-start | bytes 1658884
  16.6 44.0 %all-to-all-start.2 = ((bf16[1,2,96,2,80]{2,1,3,0,4:T(2,128)(2,1)}), bf16[1,2,96,2,80]{2,1,3,0,4:T(2,128)(2,1)S(1)}, u32[]{:S(2)}, u32[]{:S(2)}) async-start(bf16[1,2,96,2,80]{2,1,3,0,4:T(2,128)(2,1)} %copy.58), calls=%async_computation.2 | async-start | bytes 163840 | tf_op jit(solution)/shard_map/all_to_all | solution.py:43
  21.8 155.6 %all-gather.5.cloned.1.call-start = ((), (), s32[]{:S(2)}) async-start(), calls=%async_computation.5 | async-start | bytes 2949120 | tf_op jit(solution)/shard_map/all_gather | solution.py:126
  38.9 3.1 %copy-start.17 = (bf16[384,96]{0,1:T(8,128)(2,1)S(1)}, bf16[384,96]{0,1:T(8,128)(2,1)}, u32[]{:S(2)}) copy-start(bf16[384,96]{0,1:T(8,128)(2,1)} %param.10) | copy-start | bytes 221188
  60.6 10.1 %all-to-all-start = ((bf16[1,2,96,2,80]{2,1,3,0,4:T(2,128)(2,1)}), bf16[1,2,96,2,80]{2,1,3,0,4:T(2,128)(2,1)S(1)}, u32[]{:S(2)}, u32[]{:S(2)}) async-start(bf16[1,2,96,2,80]{2,1,3,0,4:T(2,128)(2,1)} %copy.47), calls=%async_computation | async-start | bytes 163840 | tf_op jit(solution)/shard_map/all_to_all | solution.py:42
  70.7 3.7 %copy-start.6 = (f32[5,2,96,1361]{3,2,1,0:T(8,128)S(1)}, f32[5,2,96,1361]{3,2,1,0:T(8,128)}, u32[]{:S(2)}) copy-start(f32[5,2,96,1361]{3,2,1,0:T(8,128)} %fusion) | copy-start | bytes 15678724
  70.7 9.4 %slice-start = ((s8[5406720]{0:T(1024)(128)(4,1)}), s8[1212416]{0:T(1024)(128)(4,1)S(1)}, s32[]{:S(2)}) async-start(s8[5406720]{0:T(1024)(128)(4,1)} %bitcast.166), calls=%async_computation.7 | async-start | bytes 2424832
  74.4 5.7 %slice-start.1 = ((s8[5406720]{0:T(1024)(128)(4,1)}), s8[4194304]{0:T(1024)(128)(4,1)S(1)}, s32[]{:S(2)}) async-start(s8[5406720]{0:T(1024)(128)(4,1)} %bitcast.166), calls=%async_computation.8 | async-start | bytes 8388608
  82.7 1.8 copy-start.1
  110.9 2.2 copy-start.7
  110.9 2.5 %copy-start.8 = (bf16[5,1,96,1361]{3,2,1,0:T(8,128)(2,1)S(1)}, bf16[5,1,96,1361]{3,2,1,0:T(8,128)(2,1)}, u32[]{:S(2)}) copy-start(bf16[5,1,96,1361]{3,2,1,0:T(8,128)(2,1)} %get-tuple-element.20) | copy-start | bytes 3919684
  122.9 6.4 %copy-start.2 = (f32[5,1,96,1361]{3,2,1,0:T(8,128)S(1)}, f32[5,1,96,1361]{3,2,1,0:T(8,128)}, u32[]{:S(2)}) copy-start(f32[5,1,96,1361]{3,2,1,0:T(8,128)} %copy-done.1) | copy-start | bytes 7839364
  122.9 6.4 %copy-start.4 = (f32[2,96,2081]{2,1,0:T(8,128)S(1)}, f32[2,96,2081]{2,1,0:T(8,128)}, u32[]{:S(2)}) copy-start(f32[2,96,2081]{2,1,0:T(8,128)} %dynamic_update_slice.17) | copy-start | bytes 4794628
  139.6 20.9 %all-to-all-start.3 = ((bf16[8,2,96,2,10]{2,3,4,1,0:T(2,128)(2,1)}), bf16[8,2,96,2,10]{2,3,4,1,0:T(2,128)(2,1)S(1)}, u32[]{:S(2)}, u32[]{:S(2)}) async-start(bf16[8,2,96,2,10]{2,3,4,1,0:T(2,128)(2,1)} %pad_maximum_fusion.5), calls=%async_computation.3 | async-start | bytes 163840 | tf_op jit(solution)/shard_map/all_to_all | solution.py:115
  143.7 6.6 %copy-start.3 = (f32[5,1,96,1361]{3,2,1,0:T(8,128)S(1)}, f32[5,1,96,1361]{3,2,1,0:T(8,128)}, u32[]{:S(2)}) copy-start(f32[5,1,96,1361]{3,2,1,0:T(8,128)} %copy-done.1) | copy-start | bytes 7839364
  150.3 1.5 copy-start.5
  153.2 11.5 %copy-start.9 = (f32[2,96,1361]{2,1,0:T(8,128)S(1)}, f32[2,96,1361]{2,1,0:T(8,128)}, u32[]{:S(2)}) copy-start(f32[2,96,1361]{2,1,0:T(8,128)} %fusion.7) | copy-start | bytes 3135748
  153.2 16.6 %copy-start.20 = (bf16[80]{0:T(256)(128)(2,1)S(1)}, bf16[80]{0:T(256)(128)(2,1)}, u32[]{:S(2)}) copy-start(bf16[80]{0:T(256)(128)(2,1)} %get-tuple-element.45) | copy-start | bytes 484
  160.5 9.3 %all-to-all-start.1 = ((bf16[8,2,96,2,10]{2,3,4,1,0:T(2,128)(2,1)}), bf16[8,2,96,2,10]{2,3,4,1,0:T(2,128)(2,1)S(1)}, u32[]{:S(2)}, u32[]{:S(2)}) async-start(bf16[8,2,96,2,10]{2,3,4,1,0:T(2,128)(2,1)} %pad_maximum_fusion.3), calls=%async_computation.1 | async-start | bytes 163840 | tf_op jit(solution)/shard_map/all_to_all | solution.py:114
  164.6 66.7 %all-reduce.5.cloned.1.call-start = ((), (), s32[]{:S(2)}) async-start(), calls=%async_computation.6 | async-start | bytes 1474560 | tf_op jit(solution)/shard_map/psum | solution.py:141
  184.3 2.7 %copy-start.13 = (bf16[1440,1,80]{0,2,1:T(8,128)(2,1)S(1)}, bf16[1440,1,80]{0,2,1:T(8,128)(2,1)}, u32[]{:S(2)}) copy-start(bf16[1440,1,80]{0,2,1:T(8,128)(2,1)} %copy-done.12) | copy-start | bytes 691204
  184.3 2.7 %copy-start.15 = (bf16[1440,1,80]{0,2,1:T(8,128)(2,1)S(1)}, bf16[1440,1,80]{0,2,1:T(8,128)(2,1)}, u32[]{:S(2)}) copy-start(bf16[1440,1,80]{0,2,1:T(8,128)(2,1)} %copy-done.14) | copy-start | bytes 691204
  184.3 3.9 %copy-start.18 = (bf16[384,96]{0,1:T(8,128)(2,1)S(1)}, bf16[384,96]{0,1:T(8,128)(2,1)}, u32[]{:S(2)}) copy-start(bf16[384,96]{0,1:T(8,128)(2,1)} %param.10) | copy-start | bytes 221188
Sparse Core Ops, SparseCore 0:
  10.2 57.7 all-gather.2
  70.1 49.2 all-gather.4
  177.5 53.8 all-reduce.4

commit v2 on v1

v2 whole, which is shorter than its diff:
```python
import functools
import math

import jax
import jax.numpy as jnp
from jax import lax
from jax.experimental import pallas as pl
from jax.experimental.pallas import tpu as pltpu
from jax.sharding import PartitionSpec as P


def dft_basis(orders, longitudes):
    lon_index = jnp.arange(longitudes, dtype=jnp.int32)
    turns = orders[:, None] * lon_index[None, :] % longitudes
    angles = turns.astype(jnp.float32) * (2.0 * math.pi / longitudes)
    norm_scale = 1.0 / math.sqrt(longitudes)
    basis = jnp.stack([jnp.cos(angles) * norm_scale, -jnp.sin(angles) * norm_scale], axis=0)
    return basis.astype(jnp.bfloat16)


def owner_kernel(
    degrees, tail_shift, chunk, lower_ref, leg_ref, recv_ref, lead_ref, tail_ref,
    synth_ref, grad_ref, coeff_ref, head_acc, tail_acc,
):
    slot = pl.program_id(0)
    lower = lower_ref[slot]
    qpad = leg_ref.shape[2]
    half_rows = leg_ref.shape[1] // 2

    @pl.when(slot == 0)
    def _():
        head_acc[...] = jnp.zeros_like(head_acc)
        tail_acc[...] = jnp.zeros_like(tail_acc)

    for start in range(0, qpad, chunk):
        rows = pl.ds(start, chunk)
        leg_t = leg_ref[0, :, start : start + chunk].astype(jnp.float32).T.astype(jnp.bfloat16)

        def analyse(part):
            return jnp.dot(leg_t, recv_ref[0, part], preferred_element_type=jnp.float32)

        x0, x1, g0, g1 = [analyse(part) for part in range(4)]
        position = start + lax.broadcasted_iota(jnp.int32, x0.shape, 0)
        leading = position < degrees - lower
        lead_rows = pl.ds(lower + start, chunk)
        w0 = jnp.where(leading, lead_ref[0, lead_rows, :], tail_ref[0, rows, :])
        w1 = jnp.where(leading, lead_ref[1, lead_rows, :], tail_ref[1, rows, :])
        coeff_ref[0, rows, :] = (w0 * x0 - w1 * x1).astype(jnp.bfloat16)
        coeff_ref[1, rows, :] = (w0 * x1 + w1 * x0).astype(jnp.bfloat16)
        coeff_ref[2, rows, :] = (w0 * g0 + w1 * g1).astype(jnp.bfloat16)
        coeff_ref[3, rows, :] = (w0 * g1 - w1 * g0).astype(jnp.bfloat16)
        for part, term in enumerate((g0 * x0 + g1 * x1, g1 * x0 - g0 * x1)):
            head_acc[part, lead_rows, :] += jnp.where(leading, term, 0.0)
            tail_acc[part, rows, :] += jnp.where(leading, 0.0, term)

    for part in range(4):
        both = jnp.dot(leg_ref[0], coeff_ref[part], preferred_element_type=jnp.float32)
        even, odd = both[:half_rows], both[half_rows:]
        synth_ref[0, part, :half_rows] = (even + odd).astype(jnp.bfloat16)
        synth_ref[0, part, half_rows:] = (even - odd).astype(jnp.bfloat16)

    @pl.when(slot == pl.num_programs(0) - 1)
    def _():
        for part in range(2):
            grad_ref[part] = (
                head_acc[part, :degrees, :] + tail_acc[part, tail_shift : tail_shift + degrees, :]
            )


def owner_stage(lower, leg_masked, received, spectral, order_count):
    owned, rows, qpad = leg_masked.shape
    width = received.shape[3]
    degrees = spectral.shape[2]
    tail_shift = degrees - order_count + 1
    weight_rows = jnp.transpose(spectral, (1, 2, 0))
    lead = jnp.pad(weight_rows, ((0, 0), (0, qpad), (0, 0)))
    tail = jnp.pad(weight_rows, ((0, 0), (tail_shift, qpad - tail_shift - degrees), (0, 0)))
    per_slot = lambda s: (s, 0, 0)
    return pl.pallas_call(
        functools.partial(owner_kernel, degrees, tail_shift, 128),
        grid=(owned,),
        out_shape=(
            jax.ShapeDtypeStruct((owned, 4, rows, width), jnp.bfloat16),
            jax.ShapeDtypeStruct((2, degrees, width), jnp.float32),
        ),
        in_specs=[
            pl.BlockSpec(memory_space=pltpu.SMEM),
            pl.BlockSpec((1, rows, qpad), per_slot),
            pl.BlockSpec((1, 4, rows, width), lambda s: (s, 0, 0, 0)),
            pl.BlockSpec(lead.shape, lambda s: (0, 0, 0)),
            pl.BlockSpec(tail.shape, lambda s: (0, 0, 0)),
        ],
        out_specs=(
            pl.BlockSpec((1, 4, rows, width), lambda s: (s, 0, 0, 0)),
            pl.BlockSpec((2, degrees, width), lambda s: (0, 0, 0)),
        ),
        scratch_shapes=[
            pltpu.VMEM((4, qpad, width), jnp.bfloat16),
            pltpu.VMEM(lead.shape, jnp.float32),
            pltpu.VMEM(tail.shape, jnp.float32),
        ],
        compiler_params=pltpu.CompilerParams(vmem_limit_bytes=32 * 2**20),
        cost_estimate=pl.CostEstimate(
            flops=owned * 16 * rows * qpad * width, bytes_accessed=2**24, transcendentals=0
        ),
    )(lower, leg_masked, received, lead, tail)


def lat_sum(array):
    lat_count = lax.axis_size("lat")
    groups, rows, columns = array.shape
    share = -(-rows // (8 * lat_count)) * 8
    padded = jnp.pad(array, ((0, 0), (0, share * lat_count - rows), (0, 0)))
    parts = padded.reshape(groups, lat_count, share, columns).transpose(1, 0, 2, 3)
    mine = jnp.sum(lax.all_to_all(parts, "lat", 0, 0, tiled=True), axis=0)
    every = lax.all_to_all(
        jnp.broadcast_to(mine[None], (lat_count, *mine.shape)), "lat", 0, 0, tiled=True
    )
    return every.transpose(1, 0, 2, 3).reshape(groups, -1, columns)[:, :rows]


def local(grid_field, cotangent, legendre, spectral, mixing, pair_table):
    lat_count = lax.axis_size("lat")
    owned, packed, npairs = legendre.shape
    degrees = spectral.shape[2]
    chan_width = grid_field.shape[2]
    longitudes = grid_field.shape[3]
    order_count = 2 * owned * lat_count
    field_full = lax.all_gather(grid_field[0], "chan", axis=0, tiled=False)
    cot_full = lax.all_gather(cotangent[0], "chan", axis=0, tiled=False)
    mixing_full = lax.all_gather(mixing, "chan", axis=0, tiled=False)
    slot_orders = jnp.stack([pair_table, order_count - 1 - pair_table], axis=1).reshape(-1)
    basis = dft_basis(slot_orders, longitudes)
    weight_m = jnp.where(slot_orders == 0, 1.0, 2.0).astype(jnp.float32)

    def transform(field):
        spec = jnp.einsum("rmj,hcj->hrmc", basis, field[0], preferred_element_type=jnp.float32)
        return spec

    def parity_parts(spec):
        return jnp.stack([spec[0] + spec[1], spec[0] - spec[1]], axis=0).astype(jnp.bfloat16)

    even_x = parity_parts(transform(grid_field))
    even_g = parity_parts(transform(cotangent) * weight_m[None, None, :, None])
    spectra = jnp.stack([even_x, even_g], axis=0)
    spectra = spectra.reshape(2, 2, 2, lat_count, owned, 2, chan_width)
    sent = jnp.transpose(spectra, (3, 4, 0, 2, 1, 5, 6))
    received = lax.all_to_all(sent, "lat", split_axis=0, concat_axis=0, tiled=True)
    received = jnp.transpose(received, (1, 2, 3, 4, 5, 0, 6)).reshape(
        owned, 4, 4 * npairs, chan_width
    )

    slot_start = lax.axis_index("lat") * owned
    lower = lax.dynamic_slice_in_dim(pair_table, slot_start, owned)
    qpad = -(-packed // 128) * 128
    position = jnp.arange(qpad, dtype=jnp.int32)[None, :]
    lower_col = lower[:, None]
    leading = position < degrees - lower_col
    degree = jnp.where(leading, lower_col + position, position - (degrees - order_count + 1))
    order = jnp.where(leading, lower_col, order_count - 1 - lower_col)
    half_pick = jnp.where(leading, 0, 1)
    parity = (degree + order) % 2
    group = 2 * parity + half_pick
    leg_rows = jnp.pad(
        jnp.transpose(legendre, (0, 2, 1)), ((0, 0), (0, 0), (0, qpad - packed))
    )
    chosen = group[:, None, None, :] == jnp.arange(4, dtype=jnp.int32)[None, :, None, None]
    leg_masked = jnp.where(chosen, leg_rows[:, None], jnp.zeros((), jnp.bfloat16)).reshape(
        owned, 4 * npairs, qpad
    )

    synth, grad_local = owner_stage(lower, leg_masked, received, spectral, order_count)
    synth = synth.reshape(owned, 2, 2, 2, 2, npairs, chan_width)
    back = jnp.transpose(synth, (5, 0, 1, 2, 3, 4, 6))
    rows = lax.all_to_all(back, "lat", split_axis=0, concat_axis=0, tiled=True)
    rows = jnp.transpose(rows, (2, 4, 3, 0, 1, 5, 6)).reshape(
        2, 2, 2, order_count, chan_width
    )
    row_y = rows[0] * weight_m.astype(jnp.bfloat16)[None, None, :, None]
    row_dx = rows[1]
    weight_sum = lat_sum(grad_local)

    filtered_grid = jnp.einsum(
        "hrmc,rmj->hcj", row_y, basis, preferred_element_type=jnp.float32
    )
    back_grid = jnp.einsum("hrmc,rmj->hcj", row_dx, basis, preferred_element_type=jnp.float32)
    chan_count = lax.axis_size("chan")
    mixing_own = lax.dynamic_slice_in_dim(
        mixing_full, lax.axis_index("chan") * chan_width, chan_width, 1
    )
    mixing_parts = mixing.reshape(chan_count, chan_width, chan_width)
    skip_path = jnp.einsum(
        "zhij,zio->hoj", field_full, mixing_parts, preferred_element_type=jnp.float32
    )
    back_skip = jnp.einsum(
        "zhoj,zio->hij", cot_full, mixing_own, preferred_element_type=jnp.float32
    )
    mixing_grad = jnp.einsum(
        "zhij,hoj->zio", field_full, cotangent[0], preferred_element_type=jnp.float32
    ).reshape(1, chan_count * chan_width, chan_width)
    block_output = (filtered_grid + skip_path).astype(jnp.bfloat16)[None]
    grad_input = (back_grid + back_skip).astype(jnp.bfloat16)[None]
    mixing_sum = lat_sum(mixing_grad)[0]
    grad_weights = jnp.transpose(weight_sum, (2, 0, 1)) / math.sqrt(order_count)
    grad_mixing = mixing_sum / math.sqrt(2 * npairs * longitudes)
    return (block_output, grad_input, grad_weights, grad_mixing)


def solution(mesh):
    in_specs = (
        P("lat", None, "chan", None),
        P("lat", None, "chan", None),
        P("lat", None, None),
        P("chan", None, None),
        P(None, "chan"),
        P(),
    )
    out_specs = (
        P("lat", None, "chan", None),
        P("lat", None, "chan", None),
        P("chan", None, None),
        P(None, "chan"),
    )
    return jax.shard_map(local, mesh=mesh, in_specs=in_specs, out_specs=out_specs, check_vma=False)
```

time: 244 us -> 141 us (0.58)
  local copies, waits for them, and re-layouts: 60.8 us -> 13.1 us
  other arithmetic: 45.8 us -> 5.97 us
  matrix products: 31.6 us -> 11.5 us
  between operations: 23.8 us -> 14.4 us
  Pallas kernels: 0 us -> 9.18 us
  starting transfers between devices: 17.7 us -> 23.7 us
    psum x1 -> x0, waiting for transfers between devices: 41.2 us -> none  [local(): weight_sum, mixing_sum = lax.psum((grad_local, mixing_grad), 'lat')]
    dynamic_update_slice x5 -> x0, local copies, waits for them, and re-layouts: 32.4 us -> none  [local(): lax.dynamic_update_slice_in_dim(grad_rows, current + head_part, lower[slo...]
    all_to_all x4 -> x6, waiting for transfers between devices: 2.88 us -> 25.4 us  [the longest x2 11.7 us: lat_sum(): mine = jnp.sum(lax.all_to_all(parts, 'lat', 0, 0, tiled=True), axis=0)]
    dot_general x11 -> x7, matrix products: 31.6 us -> 11.5 us  [the longest x1 3.28 us: local(): jnp.einsum('zhij,hoj->zio', field_full, cotangent[0], preferred_element_t...]
    all_gather x2, waiting for transfers between devices: 0.04 us -> 17.8 us  [the longest x1 17.8 us: local(): cot_full = lax.all_gather(cotangent[0], 'chan', axis=0, tiled=False)]
    all_gather x2 -> x1, local copies, waits for them, and re-layouts: 13 us -> 0.92 us  [local(): mixing_full = lax.all_gather(mixing, 'chan', axis=0, tiled=False)]
    convert_element_type x4 -> x1, other arithmetic: 11.7 us -> 0.01 us  [local(): row_y = rows[0] * weight_m.astype(jnp.bfloat16)[None, None, :, None]]
    add x5 -> x1, other arithmetic: 10.9 us -> 0.1 us  [local(): group = 2 * parity + half_pick]
  transfers between devices with their start and end apart: 7 -> 8, of which waited for: 2 -> 5; matrix products, arithmetic and copies ran while one was open for 54% -> 19% of each run, Pallas kernels for 0% -> 7%
where the time goes in v2:
time: 141 us; the launch traced here: 140 us
  waiting for transfers between devices  44.6 us (32%)
  starting transfers between devices  23.7 us (17%)
  blocking collectives  17.8 us (13%)
  between operations  14.4 us (10%)
  local copies, waits for them, and re-layouts  13.1 us (9%)
  matrix products  11.5 us (8%)
  Pallas kernels  9.18 us (7%)
  other arithmetic  5.97 us (4%)
    all_gather x1, waiting for transfers between devices, local(): cot_full = lax.all_gather(cotangent[0], 'chan', axis=0, tiled=False)  17.8 us
    all_gather x1, blocking collectives, local(): mixing_full = lax.all_gather(mixing, 'chan', axis=0, tiled=False)  17.8 us
    all_to_all x2, waiting for transfers between devices, lat_sum(): mine = jnp.sum(lax.all_to_all(parts, 'lat', 0, 0, tiled=True), axis=0)  11.7 us
    pallas_call x1, Pallas kernels, owner_stage(): pl.pallas_call(functools.partial(owner_kernel, degrees, tail_shift, 128),...  9.18 us
    all_to_all x2, starting transfers between devices, lat_sum(): mine = jnp.sum(lax.all_to_all(parts, 'lat', 0, 0, tiled=True), axis=0)  7.62 us
    all_to_all x2, starting transfers between devices, lat_sum(): lax.all_to_all(jnp.broadcast_to(mine[None], (lat_count, *mine.shape)), 'l...  7.44 us
    all_to_all x1, waiting for transfers between devices, local(): rows = lax.all_to_all(back, 'lat', split_axis=0, concat_axis=0, tiled=True)  5.64 us
    all_to_all x1, starting transfers between devices, local(): lax.all_to_all(sent, 'lat', split_axis=0, concat_axis=0, tiled=True)  5.17 us
  transfers between devices with their start and end apart: 8, of which 5 were waited for; matrix products, arithmetic and copies ran while one was open for 19% of the time, Pallas kernels for 7%

profile of v2, /device:TPU:0, one launch (start us, length us, event | category | flops | bytes accessed | tf_op | source)
XLA Modules:
  0.0 140.3 jit_solution(10070514237901839524)
XLA Ops:
  7.2 0.7 all-gather.4.cloned.1.call-update
  7.9 0.7 subtract_bitcast_fusion
  8.6 0.7 pad_add_fusion
  9.3 0.1 mul.98
  9.5 2.3 %multiply_convert_fusion.1 = (bf16[1,80,1440]{2,1,0:T(8,128)(2,1)S(1)}, bf16[1,80,1440]{2,1,0:T(8,128)(2,1)S(1)}) fusion(s32[80]{0:T(128)S(1)} %mul.98), kind=kLoop, calls=%fused_computation.29 | loop fusion | flops 1612800 | bytes 461120 | tf_op jit(solution)/shard_map/convert.8
  11.8 1.6 %fusion.6 = f32[2,2,80,96]{3,2,0,1:T(8,128)S(1)} fusion(bf16[1,2,96,1440]{3,2,1,0:T(8,128)(2,1)} %param.7, f32[80]{0:T(128)S(1)} %get-tuple-element.29, bf16[1,80,1440]{2,1,0:T(8,128)(2,1)S(1)} %get-tuple-element.31, bf16[1,80,1440]{2,1,0:T(8,128)(2,1)S(1)} %get-tuple-element.30), kind=kOutput, calls=%fused_computation.13 | convolution fusion | flops 89425920 | bytes 1136960 | tf_op jit(solution)/shard_map/rmj,hcj->hrmc/dot_general | solution.py:137
  13.5 0.4 convolution_bitcast_fusion.5
  13.9 0.9 copy_bitcast_fusion.1
  14.8 5.2 %all-to-all-start = ((bf16[8,5,2,2,2,2,96]{6,5,4,3,2,1,0:T(2,128)(2,1)}), bf16[8,5,2,2,2,2,96]{6,5,4,3,2,1,0:T(2,128)(2,1)S(1)}, u32[]{:S(2)}, u32[]{:S(2)}) async-start(bf16[8,5,2,2,2,2,96]{6,5,4,3,2,1,0:T(2,128)(2,1)} %copy_bitcast_fusion.1), calls=%async_computation | async-start | bytes 327680 | tf_op jit(solution)/shard_map/all_to_all | solution.py:148
  20.0 0.7 all-gather.6.cloned.1.call-update
  20.8 0.1 fusion.27
  21.0 0.2 select_bitcast_fusion.leg_ref
  21.2 0.3 copy.61
  21.4 0.1 pad.17.lead_ref
  21.6 1.3 pad.18.tail_ref
  22.8 3.0 %all-to-all-done = bf16[8,5,2,2,2,2,96]{6,5,4,3,2,1,0:T(2,128)(2,1)S(1)} async-done(((bf16[8,5,2,2,2,2,96]{6,5,4,3,2,1,0:T(2,128)(2,1)}), bf16[8,5,2,2,2,2,96]{6,5,4,3,2,1,0:T(2,128)(2,1)S(1)}, u32[]{:S(2)}, u32[]{:S(2)}) %all-to-all-start) | async-done | bytes 122912 | tf_op jit(solution)/shard_map/all_to_all | solution.py:148
  25.9 1.4 copy-done
  27.3 9.2 %shard_map.93 = (bf16[5,4,32,96]{3,2,1,0:T(8,128)(2,1)S(1)}, f32[2,720,96]{2,1,0:T(8,128)S(1)}) custom-call(s32[5]{0:T(128)S(1)} %get-tuple-element.21.lower_ref, bf16[5,32,1408]{2,1,0:T(8,128)(2,1)S(1)} %select_bitcast_fusion.leg_ref, bf16[5,4,32,96]{3,2,1,0:T(8,128)(2,1)S(1)} %bitcast.116, f32[2,2128,96]{2,1,0:T(8,128)S(1)} %pad.17.lead_ref, ...), custom_call_target="tpu_custom_call" | custom-call | flops 346030080 | bytes 16777216 | tf_op jit(solution)/shard_map/pallas_call | solution.py:79
  36.5 1.0 copy.93
  37.5 3.5 %all-to-all-start.2 = ((f32[8,2,96,96]{3,2,1,0:T(8,128)}), f32[8,2,96,96]{3,2,1,0:T(8,128)S(1)}, u32[]{:S(2)}, u32[]{:S(2)}) async-start(f32[8,2,96,96]{3,2,1,0:T(8,128)} %bitcast.114), calls=%async_computation.2 | async-start | bytes 1572864 | tf_op jit(solution)/shard_map/all_to_all | solution.py:115
  41.1 0.8 copy.94
  41.8 11.7 %all-to-all-done.2 = f32[8,2,96,96]{3,2,1,0:T(8,128)S(1)} async-done(((f32[8,2,96,96]{3,2,1,0:T(8,128)}), f32[8,2,96,96]{3,2,1,0:T(8,128)S(1)}, u32[]{:S(2)}, u32[]{:S(2)}) %all-to-all-start.2) | async-done | bytes 589856 | tf_op jit(solution)/shard_map/all_to_all | solution.py:115
  53.6 3.4 %all-to-all-start.1 = ((bf16[8,5,2,2,2,2,96]{6,5,4,3,2,1,0:T(2,128)(2,1)}), bf16[8,5,2,2,2,2,96]{6,5,4,3,2,1,0:T(2,128)(2,1)S(1)}, u32[]{:S(2)}, u32[]{:S(2)}) async-start(bf16[8,5,2,2,2,2,96]{6,5,4,3,2,1,0:T(2,128)(2,1)} %bitcast.115), calls=%async_computation.1 | async-start | bytes 327680 | tf_op jit(solution)/shard_map/all_to_all | solution.py:175
  57.0 0.1 copy.71
  57.1 5.6 %all-to-all-done.1 = bf16[8,5,2,2,2,2,96]{6,5,4,3,2,1,0:T(2,128)(2,1)S(1)} async-done(((bf16[8,5,2,2,2,2,96]{6,5,4,3,2,1,0:T(2,128)(2,1)}), bf16[8,5,2,2,2,2,96]{6,5,4,3,2,1,0:T(2,128)(2,1)S(1)}, u32[]{:S(2)}, u32[]{:S(2)}) %all-to-all-start.1) | async-done | bytes 122912 | tf_op jit(solution)/shard_map/all_to_all | solution.py:175
  62.8 1.1 broadcast_in_dim.89
  63.9 3.5 %all-to-all-start.3 = ((f32[8,2,96,96]{2,1,3,0:T(2,128)}), f32[8,2,96,96]{2,1,3,0:T(2,128)S(1)}, u32[]{:S(2)}, u32[]{:S(2)}) async-start(f32[8,2,96,96]{2,1,3,0:T(2,128)} %broadcast_in_dim.89), calls=%async_computation.3 | async-start | bytes 1572864 | tf_op jit(solution)/shard_map/all_to_all | solution.py:116
  67.5 0.8 reshape.342
  68.2 17.8 %all-gather = bf16[1536,96]{0,1:T(8,128)(2,1)S(1)} all-gather(bf16[384,96]{0,1:T(8,128)(2,1)S(1)} %copy-done.11), channel_id=2, replica_groups=mesh['lat'=8,'chan'=4] {'chan'}, dimensions={0}, use_global_device_ids=true | all-gather | bytes 368640 | tf_op jit(solution)/shard_map/all_gather | solution.py:131
  86.0 0.9 copy.67
  86.9 0.1 fusion.31
  87.0 0.7 copy.66
  87.7 0.7 copy.63
  88.4 0.5 copy.72
  88.9 0.3 reshape.344
  89.2 1.3 copy.74
  90.5 3.3 %convolution_bitcast_fusion.4 = f32[8,1,48,96]{3,2,1,0:T(8,128)} fusion(bf16[8,48,2,1440]{3,1,0,2:T(8,128)(2,1)} %bitcast.118, bf16[1,2,96,1440]{3,2,1,0:T(8,128)(2,1)S(1)} %copy-done.2), kind=kOutput, calls=%fused_computation.10 | convolution fusion | flops 212336640 | bytes 2912256 | tf_op jit(solution)/shard_map/zhij,hoj->zio/dot_general | solution.py:198
  93.8 4.1 %all-to-all-start.4 = ((f32[8,1,48,96]{3,2,1,0:T(8,128)}), f32[8,1,48,96]{3,2,1,0:T(8,128)}, u32[]{:S(2)}, u32[]{:S(2)}) async-start(f32[8,1,48,96]{3,2,1,0:T(8,128)} %convolution_bitcast_fusion.4), calls=%async_computation.4 | async-start | bytes 393216 | tf_op jit(solution)/shard_map/all_to_all | solution.py:115
  97.9 1.5 %convolution_bitcast_fusion.2 = f32[2,96,1440]{2,1,0:T(8,128)S(1)} fusion(bf16[4,2,96,1440]{3,2,0,1:T(8,128)(2,1)S(1)} %copy-done.1, bf16[4,96,96]{1,0,2:T(4,128)(2,1)} %reshape.342), kind=kOutput, calls=%fused_computation.3 | convolution fusion | flops 212336640 | bytes 3391488 | tf_op jit(solution)/shard_map/zhij,zio->hoj/dot_general | solution.py:192
  99.4 17.8 %all-gather.6.cloned.1.call-done = bf16[4,2,96,1440]{3,2,0,1:T(8,128)(2,1)} async-done(((bf16[1,2,96,1440]{3,2,0,1:T(8,128)(2,1)}), bf16[4,2,96,1440]{3,2,0,1:T(8,128)(2,1)}) %all-gather.6.cloned.1.call-update) | async-done | bytes 2211856 | tf_op jit(solution)/shard_map/all_gather | solution.py:130
  117.3 2.3 %convolution_bitcast_fusion = f32[2,96,1440]{2,1,0:T(8,128)S(1)} fusion(bf16[4,2,96,1440]{3,2,0,1:T(8,128)(2,1)} %all-gather.6.cloned.1.call-done, bf16[4,384,96]{2,1,0:T(8,128)(2,1)} %bitcast.127, s32[]{:T(128)S(6)} %select_n.86), kind=kOutput, calls=%fused_computation | convolution fusion | flops 212336640 | bytes 3563524 | tf_op jit(solution)/shard_map/zhoj,zio->hij/dot_general | solution.py:195
  119.6 1.2 fusion.5
  120.9 0.9 reduce_sum.19
  121.8 0.7 broadcast_in_dim.90
  122.5 3.9 %all-to-all-start.5 = ((f32[8,1,48,96]{3,2,1,0:T(8,128)}), f32[8,1,48,96]{3,2,1,0:T(8,128)S(1)}, u32[]{:S(2)}, u32[]{:S(2)}) async-start(f32[8,1,48,96]{3,2,1,0:T(8,128)} %broadcast_in_dim.90), calls=%async_computation.5 | async-start | bytes 393216 | tf_op jit(solution)/shard_map/all_to_all | solution.py:116
  126.4 1.2 fusion.4
  127.6 5.1 %all-to-all-done.5 = f32[8,1,48,96]{3,2,1,0:T(8,128)S(1)} async-done(((f32[8,1,48,96]{3,2,1,0:T(8,128)}), f32[8,1,48,96]{3,2,1,0:T(8,128)S(1)}, u32[]{:S(2)}, u32[]{:S(2)}) %all-to-all-start.5) | async-done | bytes 147488 | tf_op jit(solution)/shard_map/all_to_all | solution.py:116
  132.7 0.8 copy.75
  (46 shorter events, 0.6 us)
Async XLA Ops:
  7.2 6.3 %copy-start.7 = (bf16[1,2,96,1440]{3,2,1,0:T(8,128)(2,1)S(1)}, bf16[1,2,96,1440]{3,2,1,0:T(8,128)(2,1)}, u32[]{:S(2)}) copy-start(bf16[1,2,96,1440]{3,2,1,0:T(8,128)(2,1)} %param.6) | copy-start | bytes 1658884
  7.2 83.3 %all-gather.4.cloned.1.call-start = ((), (), s32[]{:S(2)}) async-start(), calls=%async_computation.6 | async-start | bytes 2949120 | tf_op jit(solution)/shard_map/all_gather | solution.py:129
  11.7 1.7 %copy-start.3 = (bf16[1,80,1440]{2,1,0:T(8,128)(2,1)}, bf16[1,80,1440]{2,1,0:T(8,128)(2,1)S(1)}, u32[]{:S(2)}) copy-start(bf16[1,80,1440]{2,1,0:T(8,128)(2,1)S(1)} %get-tuple-element.30) | copy-start | bytes 691204
  11.7 2.1 %copy-start.5 = (bf16[1,80,1440]{2,1,0:T(8,128)(2,1)}, bf16[1,80,1440]{2,1,0:T(8,128)(2,1)S(1)}, u32[]{:S(2)}) copy-start(bf16[1,80,1440]{2,1,0:T(8,128)(2,1)S(1)} %get-tuple-element.31) | copy-start | bytes 691204
  11.8 9.0 %copy-start.13 = (s32[40]{0:T(128)S(1)}, s32[40]{0:T(128)}, u32[]{:S(2)}) copy-start(s32[40]{0:T(128)} %param.11) | copy-start | bytes 484
  11.8 9.1 %copy-start.12 = (bf16[5,1361,8]{1,2,0:T(8,128)(2,1)S(1)}, bf16[5,1361,8]{1,2,0:T(8,128)(2,1)}, u32[]{:S(2)}) copy-start(bf16[5,1361,8]{1,2,0:T(8,128)(2,1)} %param.8) | copy-start | bytes 326644
  13.4 7.7 %copy-start.8 = (f32[96,2,720]{2,1,0:T(2,128)S(1)}, f32[96,2,720]{2,1,0:T(2,128)}, u32[]{:S(2)}) copy-start(f32[96,2,720]{2,1,0:T(2,128)} %param.9) | copy-start | bytes 1658884
  14.8 11.1 %all-to-all-start = ((bf16[8,5,2,2,2,2,96]{6,5,4,3,2,1,0:T(2,128)(2,1)}), bf16[8,5,2,2,2,2,96]{6,5,4,3,2,1,0:T(2,128)(2,1)S(1)}, u32[]{:S(2)}, u32[]{:S(2)}) async-start(bf16[8,5,2,2,2,2,96]{6,5,4,3,2,1,0:T(2,128)(2,1)} %copy_bitcast_fusion.1), calls=%async_computation | async-start | bytes 327680 | tf_op jit(solution)/shard_map/all_to_all | solution.py:148
  20.0 97.3 %all-gather.6.cloned.1.call-start = ((), (), s32[]{:S(2)}) async-start(), calls=%async_computation.7 | async-start | bytes 2949120 | tf_op jit(solution)/shard_map/all_gather | solution.py:130
  25.9 1.4 copy-start
  37.5 16.1 %all-to-all-start.2 = ((f32[8,2,96,96]{3,2,1,0:T(8,128)}), f32[8,2,96,96]{3,2,1,0:T(8,128)S(1)}, u32[]{:S(2)}, u32[]{:S(2)}) async-start(f32[8,2,96,96]{3,2,1,0:T(8,128)} %bitcast.114), calls=%async_computation.2 | async-start | bytes 1572864 | tf_op jit(solution)/shard_map/all_to_all | solution.py:115
  41.0 26.4 %copy-start.11 = (bf16[384,96]{0,1:T(8,128)(2,1)S(1)}, bf16[384,96]{0,1:T(8,128)(2,1)}, u32[]{:S(2)}) copy-start(bf16[384,96]{0,1:T(8,128)(2,1)} %param.10) | copy-start | bytes 221188
  53.6 9.2 %all-to-all-start.1 = ((bf16[8,5,2,2,2,2,96]{6,5,4,3,2,1,0:T(2,128)(2,1)}), bf16[8,5,2,2,2,2,96]{6,5,4,3,2,1,0:T(2,128)(2,1)S(1)}, u32[]{:S(2)}, u32[]{:S(2)}) async-start(bf16[8,5,2,2,2,2,96]{6,5,4,3,2,1,0:T(2,128)(2,1)} %bitcast.115), calls=%async_computation.1 | async-start | bytes 327680 | tf_op jit(solution)/shard_map/all_to_all | solution.py:175
  63.9 24.5 %all-to-all-start.3 = ((f32[8,2,96,96]{2,1,3,0:T(2,128)}), f32[8,2,96,96]{2,1,3,0:T(2,128)S(1)}, u32[]{:S(2)}, u32[]{:S(2)}) async-start(f32[8,2,96,96]{2,1,3,0:T(2,128)} %broadcast_in_dim.89), calls=%async_computation.3 | async-start | bytes 1572864 | tf_op jit(solution)/shard_map/all_to_all | solution.py:116
  88.9 1.6 %copy-start.2 = (bf16[1,2,96,1440]{3,2,1,0:T(8,128)(2,1)S(1)}, bf16[1,2,96,1440]{3,2,1,0:T(8,128)(2,1)}, u32[]{:S(2)}) copy-start(bf16[1,2,96,1440]{3,2,1,0:T(8,128)(2,1)} %param.7) | copy-start | bytes 1658884
  90.5 7.4 %copy-start.1 = (bf16[4,2,96,1440]{3,2,0,1:T(8,128)(2,1)S(1)}, bf16[4,2,96,1440]{3,2,0,1:T(8,128)(2,1)}, u32[]{:S(2)}) copy-start(bf16[4,2,96,1440]{3,2,0,1:T(8,128)(2,1)} %all-gather.4.cloned.1.call-done) | copy-start | bytes 6635524
  93.8 27.1 %all-to-all-start.4 = ((f32[8,1,48,96]{3,2,1,0:T(8,128)}), f32[8,1,48,96]{3,2,1,0:T(8,128)}, u32[]{:S(2)}, u32[]{:S(2)}) async-start(f32[8,1,48,96]{3,2,1,0:T(8,128)} %convolution_bitcast_fusion.4), calls=%async_computation.4 | async-start | bytes 393216 | tf_op jit(solution)/shard_map/all_to_all | solution.py:115
  99.4 20.2 %copy-start.4 = (bf16[1,80,1440]{2,1,0:T(8,128)(2,1)S(1)}, bf16[1,80,1440]{2,1,0:T(8,128)(2,1)}, u32[]{:S(2)}) copy-start(bf16[1,80,1440]{2,1,0:T(8,128)(2,1)} %copy-done.3) | copy-start | bytes 691204
  99.4 20.2 %copy-start.6 = (bf16[1,80,1440]{2,1,0:T(8,128)(2,1)S(1)}, bf16[1,80,1440]{2,1,0:T(8,128)(2,1)}, u32[]{:S(2)}) copy-start(bf16[1,80,1440]{2,1,0:T(8,128)(2,1)} %copy-done.5) | copy-start | bytes 691204
  99.4 20.2 %copy-start.10 = (bf16[1,2,2,8,5,2,96]{6,5,4,3,2,1,0:T(2,128)(2,1)S(1)}, bf16[1,2,2,8,5,2,96]{6,5,4,3,2,1,0:T(2,128)(2,1)}, u32[]{:S(2)}) copy-start(bf16[1,2,2,8,5,2,96]{6,5,4,3,2,1,0:T(2,128)(2,1)} %copy.63) | copy-start | bytes 184324
  119.6 6.8 %copy-start.9 = (bf16[1,2,2,8,5,2,96]{6,5,4,3,2,1,0:T(2,128)(2,1)S(1)}, bf16[1,2,2,8,5,2,96]{6,5,4,3,2,1,0:T(2,128)(2,1)}, u32[]{:S(2)}) copy-start(bf16[1,2,2,8,5,2,96]{6,5,4,3,2,1,0:T(2,128)(2,1)} %copy.66) | copy-start | bytes 184324
  122.5 10.1 %all-to-all-start.5 = ((f32[8,1,48,96]{3,2,1,0:T(8,128)}), f32[8,1,48,96]{3,2,1,0:T(8,128)S(1)}, u32[]{:S(2)}, u32[]{:S(2)}) async-start(f32[8,1,48,96]{3,2,1,0:T(8,128)} %broadcast_in_dim.90), calls=%async_computation.5 | async-start | bytes 393216 | tf_op jit(solution)/shard_map/all_to_all | solution.py:116
Sparse Core Ops, SparseCore 0:
  9.6 53.1 all-gather.3
  64.4 52.8 all-gather.5

commit v3 on v2

--- a/solution.py
+++ b/solution.py
@@ -106,17 +106,38 @@
     )(lower, leg_masked, received, lead, tail)
 
 
-def lat_sum(array):
+def exchange(blocks):
+    count = lax.axis_size("chan")
+    me = lax.axis_index("chan")
+    pick = lambda index: lax.dynamic_index_in_dim(blocks, lax.rem(index, count), 0, keepdims=True)
+    arrived = [pick(me)]
+    for step in range(1, count):
+        pairs = [(source, (source - step) % count) for source in range(count)]
+        arrived.append(lax.ppermute(pick(me + count - step), "chan", pairs))
+    twice = jnp.concatenate(arrived + arrived[:-1], axis=0)
+    return lax.dynamic_slice_in_dim(twice, lax.rem(count - me, count), count, 0)
+
+
+def scattered_rows(array):
     lat_count = lax.axis_size("lat")
     groups, rows, columns = array.shape
     share = -(-rows // (8 * lat_count)) * 8
     padded = jnp.pad(array, ((0, 0), (0, share * lat_count - rows), (0, 0)))
-    parts = padded.reshape(groups, lat_count, share, columns).transpose(1, 0, 2, 3)
-    mine = jnp.sum(lax.all_to_all(parts, "lat", 0, 0, tiled=True), axis=0)
-    every = lax.all_to_all(
-        jnp.broadcast_to(mine[None], (lat_count, *mine.shape)), "lat", 0, 0, tiled=True
-    )
-    return every.transpose(1, 0, 2, 3).reshape(groups, -1, columns)[:, :rows]
+    return padded.reshape(groups, lat_count, share, columns).transpose(1, 0, 2, 3)
+
+
+def scatter_sum(array, axis):
+    return jnp.sum(lax.all_to_all(array, axis, 0, 0, tiled=True), axis=0)
+
+
+def spread(array, axis):
+    everywhere = jnp.broadcast_to(array[None], (lax.axis_size(axis), *array.shape))
+    return lax.all_to_all(everywhere, axis, 0, 0, tiled=True)
+
+
+def joined_rows(shares, rows):
+    every = shares.transpose(1, 0, 2, 3)
+    return every.reshape(every.shape[0], -1, every.shape[3])[:, :rows]
 
 
 def local(grid_field, cotangent, legendre, spectral, mixing, pair_table):
@@ -126,9 +147,14 @@
     chan_width = grid_field.shape[2]
     longitudes = grid_field.shape[3]
     order_count = 2 * owned * lat_count
-    field_full = lax.all_gather(grid_field[0], "chan", axis=0, tiled=False)
-    cot_full = lax.all_gather(cotangent[0], "chan", axis=0, tiled=False)
-    mixing_full = lax.all_gather(mixing, "chan", axis=0, tiled=False)
+    chan_count = lax.axis_size("chan")
+    pieces = chan_count // 2
+    span = longitudes // pieces
+    both_fields = jnp.stack([grid_field[0], cotangent[0]], axis=0)
+    cut = both_fields.reshape(2, 2, chan_width, pieces, span).transpose(1, 3, 0, 2, 4)
+    sliced = exchange(cut.reshape(chan_count, 2, chan_width, span))
+    mixing_blocks = exchange(jnp.broadcast_to(mixing[None], (chan_count, *mixing.shape)))
+    mixing_full = mixing_blocks.transpose(1, 0, 2).reshape(mixing.shape[0], -1)
     slot_orders = jnp.stack([pair_table, order_count - 1 - pair_table], axis=1).reshape(-1)
     basis = dft_basis(slot_orders, longitudes)
     weight_m = jnp.where(slot_orders == 0, 1.0, 2.0).astype(jnp.float32)
@@ -178,29 +204,39 @@
     )
     row_y = rows[0] * weight_m.astype(jnp.bfloat16)[None, None, :, None]
     row_dx = rows[1]
-    weight_sum = lat_sum(grad_local)
-
     filtered_grid = jnp.einsum(
         "hrmc,rmj->hcj", row_y, basis, preferred_element_type=jnp.float32
     )
     back_grid = jnp.einsum("hrmc,rmj->hcj", row_dx, basis, preferred_element_type=jnp.float32)
-    chan_count = lax.axis_size("chan")
-    mixing_own = lax.dynamic_slice_in_dim(
-        mixing_full, lax.axis_index("chan") * chan_width, chan_width, 1
-    )
-    mixing_parts = mixing.reshape(chan_count, chan_width, chan_width)
-    skip_path = jnp.einsum(
-        "zhij,zio->hoj", field_full, mixing_parts, preferred_element_type=jnp.float32
-    )
-    back_skip = jnp.einsum(
-        "zhoj,zio->hij", cot_full, mixing_own, preferred_element_type=jnp.float32
-    )
-    mixing_grad = jnp.einsum(
-        "zhij,hoj->zio", field_full, cotangent[0], preferred_element_type=jnp.float32
-    ).reshape(1, chan_count * chan_width, chan_width)
-    block_output = (filtered_grid + skip_path).astype(jnp.bfloat16)[None]
-    grad_input = (back_grid + back_skip).astype(jnp.bfloat16)[None]
-    mixing_sum = lat_sum(mixing_grad)[0]
+    channels = chan_count * chan_width
+    field_slice = sliced[:, 0].reshape(channels, span)
+    cot_slice = sliced[:, 1].reshape(channels, span)
+    mixing_grad = jnp.einsum("ij,oj->io", field_slice, cot_slice, preferred_element_type=jnp.float32)
+    skip_slice = jnp.einsum("io,ij->oj", mixing_full, field_slice, preferred_element_type=jnp.float32)
+    back_slice = jnp.einsum("io,oj->ij", mixing_full, cot_slice, preferred_element_type=jnp.float32)
+    mixed = jnp.stack(
+        [
+            skip_slice.astype(jnp.bfloat16).reshape(chan_count, chan_width, span),
+            back_slice.astype(jnp.bfloat16).reshape(chan_count, chan_width, span),
+        ],
+        axis=1,
+    )
+    home = exchange(mixed)
+    home = home.reshape(2, pieces, 2, chan_width, span).transpose(2, 0, 3, 1, 4)
+    home = home.reshape(2, 2, chan_width, longitudes).astype(jnp.float32)
+    block_output = (filtered_grid + home[0]).astype(jnp.bfloat16)[None]
+    grad_input = (back_grid + home[1]).astype(jnp.bfloat16)[None]
+
+    mixing_share = scatter_sum(scattered_rows(mixing_grad[None])[:, 0], "lat")
+    by_owner = mixing_share.reshape(-1, chan_count, chan_width).transpose(1, 0, 2)
+    mixing_share = jnp.sum(exchange(by_owner), axis=0)
+    weight_share = scatter_sum(scattered_rows(grad_local), "lat")
+    weight_rows = weight_share.shape[1]
+    shares = jnp.concatenate([weight_share.reshape(-1, chan_width), mixing_share], axis=0)
+    shares = spread(shares, "lat")
+    weight_shares = shares[:, : 2 * weight_rows].reshape(-1, 2, weight_rows, chan_width)
+    weight_sum = joined_rows(weight_shares, degrees)
+    mixing_sum = joined_rows(shares[:, None, 2 * weight_rows :], channels)[0]
     grad_weights = jnp.transpose(weight_sum, (2, 0, 1)) / math.sqrt(order_count)
     grad_mixing = mixing_sum / math.sqrt(2 * npairs * longitudes)
     return (block_output, grad_input, grad_weights, grad_mixing)

time: 141 us -> 137 us (0.972)
  local copies, waits for them, and re-layouts: 13.1 us -> 52.4 us
  waiting for transfers between devices: 44.6 us -> 17.2 us
  blocking collectives: 17.8 us -> 0 us
  starting transfers between devices: 23.7 us -> 38.5 us
  between operations: 14.4 us -> 1.17 us
  matrix products: 11.5 us -> 7.87 us
  other arithmetic: 5.97 us -> 9.6 us
    unnamed x31 -> x50, local copies, waits for them, and re-layouts: 3.78 us -> 24.3 us
    ppermute x0 -> x12, starting transfers between devices: none -> 18.9 us  [exchange(): arrived.append(lax.ppermute(pick(me + count - step), 'chan', pairs))]
    all_gather x2 -> x0, waiting for transfers between devices: 17.8 us -> none  [the longest x1 17.8 us: local(): cot_full = lax.all_gather(cotangent[0], 'chan', axis=0, tiled=False)]
    all_gather x1 -> x0, blocking collectives: 17.8 us -> none  [local(): mixing_full = lax.all_gather(mixing, 'chan', axis=0, tiled=False)]
    ppermute x0 -> x12, waiting for transfers between devices: none -> 11.3 us  [exchange(): arrived.append(lax.ppermute(pick(me + count - step), 'chan', pairs))]
    all_to_all x4 -> x3, waiting for transfers between devices: 16.8 us -> 5.87 us  [the longest x2 5.87 us: scatter_sum(): return jnp.sum(lax.all_to_all(array, axis, 0, 0, tiled=True), axis=0)]
    slice x0 -> x5, local copies, waits for them, and re-layouts: none -> 6.83 us  [the longest x1 3.24 us: local(): block_output = (filtered_grid + home[0]).astype(jnp.bfloat16)[None]]
    all_to_all x1, waiting for transfers between devices: 5.64 us -> 0.01 us  [local(): rows = lax.all_to_all(back, 'lat', split_axis=0, concat_axis=0, tiled=True)]
  transfers between devices with their start and end apart: 8 -> 17, of which waited for: 5 -> 4; matrix products, arithmetic and copies ran while one was open for 19% -> 47% of each run, Pallas kernels for 7% -> 7%
where the time goes in v3:
time: 137 us; the launch traced here: 136 us
  local copies, waits for them, and re-layouts  52.4 us (38%)
  starting transfers between devices  38.5 us (28%)
  waiting for transfers between devices  17.2 us (13%)
  other arithmetic  9.6 us (7%)
  Pallas kernels  9 us (7%)
  matrix products  7.87 us (6%)
    unnamed x50, local copies, waits for them, and re-layouts  24.3 us
    ppermute x12, starting transfers between devices, exchange(): arrived.append(lax.ppermute(pick(me + count - step), 'chan', pairs))  18.9 us
    ppermute x12, waiting for transfers between devices, exchange(): arrived.append(lax.ppermute(pick(me + count - step), 'chan', pairs))  11.3 us
    pallas_call x1, Pallas kernels, owner_stage(): pl.pallas_call(functools.partial(owner_kernel, degrees, tail_shift, 128),...  9 us
    all_to_all x2, starting transfers between devices, scatter_sum(): return jnp.sum(lax.all_to_all(array, axis, 0, 0, tiled=True), axis=0)  7.74 us
    all_to_all x2, waiting for transfers between devices, scatter_sum(): return jnp.sum(lax.all_to_all(array, axis, 0, 0, tiled=True), axis=0)  5.87 us
    concatenate x4, local copies, waits for them, and re-layouts, exchange(): twice = jnp.concatenate(arrived + arrived[:-1], axis=0)  4.89 us
    all_to_all x1, starting transfers between devices, local(): rows = lax.all_to_all(back, 'lat', split_axis=0, concat_axis=0, tiled=True)  4.2 us
  transfers between devices with their start and end apart: 17, of which 4 were waited for; matrix products, arithmetic and copies ran while one was open for 47% of the time, Pallas kernels for 7%

profile of v3, /device:TPU:0, one launch (start us, length us, event | category | flops | bytes accessed | tf_op | source)
XLA Modules:
  0.0 135.6 jit_solution(5942808451742182626)
XLA Ops:
  0.6 3.1 %collective-permute-start.2 = (bf16[1,384,96]{1,2,0:T(8,128)(2,1)}, bf16[1,384,96]{1,2,0:T(8,128)(2,1)}, u32[]{:S(2)}, u32[]{:S(2)}) collective-permute-start(bf16[1,384,96]{1,2,0:T(8,128)(2,1)} %bitcast.144), channel_id=1, source_target_pairs={{0,1},{1,2},{2,3},{3,0},{4,5},{5,6},{6,7},{7,4},{8,9},{9,10},{10,1... | collective-permute-start | bytes 221192 | tf_op jit(solution)/shard_map/ppermute | solution.py:116
  3.7 2.6 %collective-permute-start.1 = (bf16[1,384,96]{1,2,0:T(8,128)(2,1)}, bf16[1,384,96]{1,2,0:T(8,128)(2,1)}, u32[]{:S(2)}, u32[]{:S(2)}) collective-permute-start(bf16[1,384,96]{1,2,0:T(8,128)(2,1)} %bitcast.145), channel_id=1, source_target_pairs={{0,2},{1,3},{2,0},{3,1},{4,6},{5,7},{6,4},{7,5},{8,10},{9,11},{10,... | collective-permute-start | bytes 221192 | tf_op jit(solution)/shard_map/ppermute | solution.py:116
  6.3 1.3 collective-permute-start
  9.2 2.3 %multiply_convert_fusion.1 = (bf16[1,80,1440]{2,1,0:T(8,128)(2,1)S(1)}, bf16[1,80,1440]{2,1,0:T(8,128)(2,1)S(1)}) fusion(s32[80]{0:T(128)S(1)} %mul.95), kind=kLoop, calls=%fused_computation.37 | loop fusion | flops 1612800 | bytes 461120 | tf_op jit(solution)/shard_map/convert.10
  11.5 1.6 %fusion.6 = f32[2,2,80,96]{3,2,0,1:T(8,128)S(1)} fusion(bf16[1,2,96,1440]{3,2,1,0:T(8,128)(2,1)} %param.7, f32[80]{0:T(128)S(1)} %get-tuple-element.61, bf16[1,80,1440]{2,1,0:T(8,128)(2,1)S(1)} %get-tuple-element.63, bf16[1,80,1440]{2,1,0:T(8,128)(2,1)S(1)} %get-tuple-element.62), kind=kOutput, calls=%fused_computation.22 | convolution fusion | flops 89425920 | bytes 1136960 | tf_op jit(solution)/shard_map/rmj,hcj->hrmc/dot_general | solution.py:163
  14.5 3.7 %all-to-all-start = ((bf16[8,5,2,2,2,2,96]{6,5,4,3,2,1,0:T(2,128)(2,1)}), bf16[8,5,2,2,2,2,96]{6,5,4,3,2,1,0:T(2,128)(2,1)S(1)}, u32[]{:S(2)}, u32[]{:S(2)}) async-start(bf16[8,5,2,2,2,2,96]{6,5,4,3,2,1,0:T(2,128)(2,1)} %copy_bitcast_fusion.1), calls=%async_computation | async-start | bytes 327680 | tf_op jit(solution)/shard_map/all_to_all | solution.py:174
  18.3 1.3 reshape.366
  23.3 1.2 pad.18.tail_ref
  24.7 2.9 %collective-permute-start.3 = (bf16[1,2,96,720]{3,2,0,1:T(8,128)(2,1)}, bf16[1,2,96,720]{3,2,0,1:T(8,128)(2,1)}, u32[]{:S(2)}, u32[]{:S(2)}) collective-permute-start(bf16[1,2,96,720]{3,2,0,1:T(8,128)(2,1)} %get-tuple-element.49), channel_id=1, source_target_pairs={{0,3},{1,0},{2,1},{3,2},{4,7},{5,4},{6,5},{7,6},{8,11},{9,8},{10,9... | collective-permute-start | bytes 829448 | tf_op jit(solution)/shard_map/ppermute | solution.py:116
  27.6 1.5 %constant_dynamic-update-slice_fusion.5 = bf16[7,384,96]{1,2,0:T(8,128)(2,1)} fusion(bf16[7,384,96]{1,2,0:T(8,128)(2,1)} %constant_dynamic-update-slice_fusion.6, bf16[1,384,96]{1,2,0:T(8,128)(2,1)} %collective-permute-done), kind=kLoop, calls=%fused_computation.69 | loop fusion | bytes 147456
  29.1 1.5 %constant_dynamic-update-slice_fusion.4 = bf16[7,384,96]{1,2,0:T(8,128)(2,1)} fusion(bf16[7,384,96]{1,2,0:T(8,128)(2,1)} %constant_dynamic-update-slice_fusion.5, bf16[1,384,96]{1,2,0:T(8,128)(2,1)} %collective-permute-done.1), kind=kLoop, calls=%fused_computation.68 | loop fusion | bytes 147456
  30.6 1.5 %constant_dynamic-update-slice_fusion.3 = bf16[7,384,96]{1,2,0:T(8,128)(2,1)} fusion(bf16[7,384,96]{1,2,0:T(8,128)(2,1)} %constant_dynamic-update-slice_fusion.4, bf16[1,384,96]{1,2,0:T(8,128)(2,1)} %collective-permute-done.2), kind=kLoop, calls=%fused_computation.67 | loop fusion | bytes 147456
  32.1 1.5 %constant_dynamic-update-slice_fusion.2 = bf16[7,384,96]{1,2,0:T(8,128)(2,1)} fusion(bf16[7,384,96]{1,2,0:T(8,128)(2,1)} %constant_dynamic-update-slice_fusion.3, bf16[384,96]{0,1:T(8,128)(2,1)} %param.10), kind=kLoop, calls=%fused_computation.66 | loop fusion | bytes 147456
  33.7 1.5 %constant_dynamic-update-slice_fusion.1 = bf16[7,384,96]{1,2,0:T(8,128)(2,1)} fusion(bf16[7,384,96]{1,2,0:T(8,128)(2,1)} %constant_dynamic-update-slice_fusion.2, bf16[1,384,96]{1,2,0:T(8,128)(2,1)} %collective-permute-done), kind=kLoop, calls=%fused_computation.65 | loop fusion | bytes 147456
  35.2 1.5 %constant_dynamic-update-slice_fusion = bf16[7,384,96]{1,2,0:T(8,128)(2,1)} fusion(bf16[7,384,96]{1,2,0:T(8,128)(2,1)} %constant_dynamic-update-slice_fusion.1, bf16[1,384,96]{1,2,0:T(8,128)(2,1)} %collective-permute-done.1), kind=kLoop, calls=%fused_computation.64 | loop fusion | bytes 147456 | tf_op jit(solution)/shard_map/concatenate | solution.py:117
  36.7 1.7 %constant_dynamic-slice_fusion.9 = bf16[4,384,96]{1,2,0:T(8,128)(2,1)} fusion(bf16[7,384,96]{1,2,0:T(8,128)(2,1)} %constant_dynamic-update-slice_fusion, s32[]{:T(128)S(6)} %select_n.116), kind=kLoop, calls=%fused_computation.105 | loop fusion | bytes 589828 | tf_op jit(solution)/shard_map/dynamic_slice | solution.py:118
  38.5 1.4 copy-done
  39.8 9.0 %shard_map.93 = (bf16[5,4,32,96]{3,2,1,0:T(8,128)(2,1)S(1)}, f32[2,720,96]{2,1,0:T(8,128)S(1)}) custom-call(s32[5]{0:T(128)S(1)} %get-tuple-element.37.lower_ref, bf16[5,32,1408]{2,1,0:T(8,128)(2,1)S(1)} %select_bitcast_fusion.leg_ref, bf16[5,4,32,96]{3,2,1,0:T(8,128)(2,1)S(1)} %bitcast.118, f32[2,2128,96]{2,1,0:T(8,128)S(1)} %pad.17.lead_ref, ...), custom_call_target="tpu_custom_call" | custom-call | flops 346030080 | bytes 16777216 | tf_op jit(solution)/shard_map/pallas_call | solution.py:79
  49.6 4.2 %all-to-all-start.1 = ((bf16[8,5,2,2,2,2,96]{6,5,4,3,2,1,0:T(2,128)(2,1)}), bf16[8,5,2,2,2,2,96]{6,5,4,3,2,1,0:T(2,128)(2,1)}, u32[]{:S(2)}, u32[]{:S(2)}) async-start(bf16[8,5,2,2,2,2,96]{6,5,4,3,2,1,0:T(2,128)(2,1)} %bitcast.114), calls=%async_computation.1 | async-start | bytes 327680 | tf_op jit(solution)/shard_map/all_to_all | solution.py:201
  54.8 1.7 %constant_dynamic-update-slice_fusion.11 = bf16[7,2,96,720]{3,2,0,1:T(8,128)(2,1)} fusion(bf16[7,2,96,720]{3,2,0,1:T(8,128)(2,1)} %get-tuple-element.47, bf16[1,2,96,720]{3,2,0,1:T(8,128)(2,1)} %collective-permute-done.3), kind=kLoop, calls=%fused_computation.75 | loop fusion | bytes 589824
  56.6 1.7 %constant_dynamic-update-slice_fusion.10 = bf16[7,2,96,720]{3,2,0,1:T(8,128)(2,1)} fusion(bf16[7,2,96,720]{3,2,0,1:T(8,128)(2,1)} %constant_dynamic-update-slice_fusion.11, bf16[1,2,96,720]{3,2,0,1:T(8,128)(2,1)} %collective-permute-done.4), kind=kLoop, calls=%fused_computation.74 | loop fusion | bytes 589824
  58.2 1.7 %constant_dynamic-update-slice_fusion.9 = bf16[7,2,96,720]{3,2,0,1:T(8,128)(2,1)} fusion(bf16[7,2,96,720]{3,2,0,1:T(8,128)(2,1)} %constant_dynamic-update-slice_fusion.10, bf16[1,2,96,720]{3,2,0,1:T(8,128)(2,1)} %collective-permute-done.5), kind=kLoop, calls=%fused_computation.73 | loop fusion | bytes 589824
  59.9 1.8 %dynamic-slice_dynamic-update-slice_fusion.1 = bf16[7,2,96,720]{3,2,0,1:T(8,128)(2,1)} fusion(bf16[7,2,96,720]{3,2,0,1:T(8,128)(2,1)} %constant_dynamic-update-slice_fusion.9, bf16[4,2,96,720]{3,2,0,1:T(8,128)(2,1)} %bitcast.124, s32[]{:T(128)S(6)} %select_n.117), kind=kLoop, calls=%fused_computation.48 | loop fusion | bytes 589828
  61.7 1.7 %constant_dynamic-update-slice_fusion.8 = bf16[7,2,96,720]{3,2,0,1:T(8,128)(2,1)} fusion(bf16[7,2,96,720]{3,2,0,1:T(8,128)(2,1)} %dynamic-slice_dynamic-update-slice_fusion.1, bf16[1,2,96,720]{3,2,0,1:T(8,128)(2,1)} %collective-permute-done.3), kind=kLoop, calls=%fused_computation.72 | loop fusion | bytes 589824
  63.4 1.7 %constant_dynamic-update-slice_fusion.7 = bf16[7,2,96,720]{3,2,0,1:T(8,128)(2,1)} fusion(bf16[7,2,96,720]{3,2,0,1:T(8,128)(2,1)} %constant_dynamic-update-slice_fusion.8, bf16[1,2,96,720]{3,2,0,1:T(8,128)(2,1)} %collective-permute-done.4), kind=kLoop, calls=%fused_computation.71 | loop fusion | bytes 589824 | tf_op jit(solution)/shard_map/concatenate | solution.py:117
  65.1 1.3 constant_dynamic-slice_fusion
  68.1 1.1 fusion.19
  69.2 1.2 collective-permute-start.6
  70.4 4.2 %all-to-all-start.2 = ((f32[8,2,96,96]{3,2,1,0:T(8,128)}), f32[8,2,96,96]{3,2,1,0:T(8,128)S(1)}, u32[]{:S(2)}, u32[]{:S(2)}) async-start(f32[8,2,96,96]{3,2,1,0:T(8,128)} %bitcast.113), calls=%async_computation.2 | async-start | bytes 1572864 | tf_op jit(solution)/shard_map/all_to_all | solution.py:130
  77.3 2.0 %collective-permute-start.7 = (bf16[1,2,96,720]{3,2,0,1:T(8,128)(2,1)}, bf16[1,2,96,720]{3,2,0,1:T(8,128)(2,1)}, u32[]{:S(2)}, u32[]{:S(2)}) collective-permute-start(bf16[1,2,96,720]{3,2,0,1:T(8,128)(2,1)} %get-tuple-element.45), channel_id=1, source_target_pairs={{0,2},{1,3},{2,0},{3,1},{4,6},{5,7},{6,4},{7,5},{8,10},{9,11},{10,... | collective-permute-start | bytes 829448 | tf_op jit(solution)/shard_map/ppermute | solution.py:116
  79.3 1.3 fusion.31
  81.4 5.9 %all-to-all-done.2 = f32[8,2,96,96]{3,2,1,0:T(8,128)S(1)} async-done(((f32[8,2,96,96]{3,2,1,0:T(8,128)}), f32[8,2,96,96]{3,2,1,0:T(8,128)S(1)}, u32[]{:S(2)}, u32[]{:S(2)}) %all-to-all-start.2) | async-done | bytes 589856 | tf_op jit(solution)/shard_map/all_to_all | solution.py:130
  87.2 3.5 %all-to-all-start.3 = ((f32[8,48,384]{2,1,0:T(8,128)}), f32[8,48,384]{2,1,0:T(8,128)S(1)}, u32[]{:S(2)}, u32[]{:S(2)}) async-start(f32[8,48,384]{2,1,0:T(8,128)} %fusion.31), calls=%async_computation.3 | async-start | bytes 1179648 | tf_op jit(solution)/shard_map/all_to_all | solution.py:130
  90.8 9.5 %collective-permute-done.7 = bf16[1,2,96,720]{3,2,0,1:T(8,128)(2,1)} collective-permute-done((bf16[1,2,96,720]{3,2,0,1:T(8,128)(2,1)}, bf16[1,2,96,720]{3,2,0,1:T(8,128)(2,1)}, u32[]{:S(2)}, u32[]{:S(2)}) %collective-permute-start.7) | collective-permute-done | bytes 276512 | tf_op jit(solution)/shard_map/ppermute | solution.py:116
  100.2 1.7 %constant_dynamic-update-slice_fusion.16 = bf16[7,2,96,720]{3,2,0,1:T(8,128)(2,1)} fusion(bf16[7,2,96,720]{3,2,0,1:T(8,128)(2,1)} %constant_dynamic-update-slice_fusion.17, bf16[1,2,96,720]{3,2,0,1:T(8,128)(2,1)} %collective-permute-done.7), kind=kLoop, calls=%fused_computation.80 | loop fusion | bytes 589824
  101.9 1.7 %constant_dynamic-update-slice_fusion.15 = bf16[7,2,96,720]{3,2,0,1:T(8,128)(2,1)} fusion(bf16[7,2,96,720]{3,2,0,1:T(8,128)(2,1)} %constant_dynamic-update-slice_fusion.16, bf16[1,2,96,720]{3,2,0,1:T(8,128)(2,1)} %collective-permute-done.8), kind=kLoop, calls=%fused_computation.79 | loop fusion | bytes 589824
  105.1 1.7 %constant_dynamic-update-slice_fusion.12 = bf16[7,2,96,720]{3,2,0,1:T(8,128)(2,1)} fusion(bf16[7,2,96,720]{3,2,0,1:T(8,128)(2,1)} %constant_dynamic-update-slice_fusion.13, bf16[1,2,96,720]{3,2,0,1:T(8,128)(2,1)} %collective-permute-done.7), kind=kLoop, calls=%fused_computation.76 | loop fusion | bytes 589824 | tf_op jit(solution)/shard_map/concatenate | solution.py:117
  107.2 1.2 collective-permute-start.11
  108.4 2.7 %collective-permute-start.9 = (f32[1,48,96]{2,1,0:T(8,128)S(1)}, f32[1,48,96]{2,1,0:T(8,128)S(1)}, u32[]{:S(2)}, u32[]{:S(2)}) collective-permute-start(f32[1,48,96]{2,1,0:T(8,128)S(1)} %bitcast.156), channel_id=1, source_target_pairs={{0,3},{1,0},{2,1},{3,2},{4,7},{5,4},{6,5},{7,6},{8,11},{9,8},{10,9... | collective-permute-start | bytes 55304 | tf_op jit(solution)/shard_map/ppermute | solution.py:116
  111.1 1.5 %collective-permute-done.9 = f32[1,48,96]{2,1,0:T(8,128)S(1)} collective-permute-done((f32[1,48,96]{2,1,0:T(8,128)S(1)}, f32[1,48,96]{2,1,0:T(8,128)S(1)}, u32[]{:S(2)}, u32[]{:S(2)}) %collective-permute-start.9) | collective-permute-done | bytes 18464 | tf_op jit(solution)/shard_map/ppermute | solution.py:116
  114.0 3.8 %all-to-all-start.4 = ((f32[8,240,96]{1,2,0:T(8,128)}), f32[8,240,96]{1,2,0:T(8,128)S(1)}, u32[]{:S(2)}, u32[]{:S(2)}) async-start(f32[8,240,96]{1,2,0:T(8,128)} %broadcast_in_dim.91), calls=%async_computation.4 | async-start | bytes 1572864 | tf_op jit(solution)/shard_map/all_to_all | solution.py:135
  117.9 1.5 %dynamic-slice_convert_fusion = f32[4,2,96,720]{3,2,0,1:T(8,128)S(1)} fusion(bf16[7,2,96,720]{3,2,0,1:T(8,128)(2,1)} %constant_dynamic-update-slice_fusion.12, s32[]{:T(128)S(6)} %select_n.116), kind=kLoop, calls=%fused_computation.19 | loop fusion | flops 552960 | bytes 3317764 | tf_op jit(solution)/shard_map/convert_element_type | solution.py:226
  119.5 1.2 fusion.29
  122.7 3.2 %copy.158 = f32[1,2,96,2,720]{4,3,2,1,0:T(2,128)} copy(f32[1,2,96,2,720]{4,2,0,3,1:T(8,128)} %get-tuple-element.39) | data formatting | bytes 2211840 | tf_op jit(solution)/shard_map/slice | solution.py:227
  125.9 2.4 %squeeze.29 = f32[2,96,1440]{2,1,0:T(8,128)S(1)} reshape(f32[1,2,96,2,720]{4,3,2,1,0:T(2,128)} %copy.158) | data formatting | bytes 2211840 | tf_op jit(solution)/shard_map/squeeze | solution.py:227
  128.3 2.2 %fusion.4 = bf16[1,2,96,1440]{3,2,1,0:T(8,128)(2,1)} fusion(f32[2,96,1440]{2,1,0:T(8,128)S(1)} %squeeze.31, bf16[2,2,80,96]{3,2,1,0:T(8,128)(2,1)} %bitcast.143, bf16[1,80,1440]{2,1,0:T(8,128)(2,1)} %copy-done.5, bf16[1,80,1440]{2,1,0:T(8,128)(2,1)S(1)} %copy-done.4), kind=kOutput, calls=%fused_computation.6 | convolution fusion | flops 89256960 | bytes 2181120 | tf_op jit(solution)/shard_map/hrmc,rmj->hcj/dot_general | solution.py:210
  130.5 1.2 fusion.5
  134.5 1.1 fusion.7
  (104 shorter events, 21.6 us)
Async XLA Ops:
  0.6 12.5 %copy-start.8 = (bf16[1,2,96,1440]{3,2,1,0:T(8,128)(2,1)S(1)}, bf16[1,2,96,1440]{3,2,1,0:T(8,128)(2,1)}, u32[]{:S(2)}) copy-start(bf16[1,2,96,1440]{3,2,1,0:T(8,128)(2,1)} %param.6) | copy-start | bytes 1658884
  0.6 30.0 %collective-permute-start.2 = (bf16[1,384,96]{1,2,0:T(8,128)(2,1)}, bf16[1,384,96]{1,2,0:T(8,128)(2,1)}, u32[]{:S(2)}, u32[]{:S(2)}) collective-permute-start(bf16[1,384,96]{1,2,0:T(8,128)(2,1)} %bitcast.144), channel_id=1, source_target_pairs={{0,1},{1,2},{2,3},{3,0},{4,5},{5,6},{6,7},{7,4},{8,9},{9,10},{10,1... | collective-permute-start | bytes 221192 | tf_op jit(solution)/shard_map/ppermute | solution.py:116
  3.7 25.4 %collective-permute-start.1 = (bf16[1,384,96]{1,2,0:T(8,128)(2,1)}, bf16[1,384,96]{1,2,0:T(8,128)(2,1)}, u32[]{:S(2)}, u32[]{:S(2)}) collective-permute-start(bf16[1,384,96]{1,2,0:T(8,128)(2,1)} %bitcast.145), channel_id=1, source_target_pairs={{0,2},{1,3},{2,0},{3,1},{4,6},{5,7},{6,4},{7,5},{8,10},{9,11},{10,... | collective-permute-start | bytes 221192 | tf_op jit(solution)/shard_map/ppermute | solution.py:116
  6.3 18.4 %collective-permute-start = (bf16[1,384,96]{1,2,0:T(8,128)(2,1)}, bf16[1,384,96]{1,2,0:T(8,128)(2,1)}, u32[]{:S(2)}, u32[]{:S(2)}) collective-permute-start(bf16[1,384,96]{1,2,0:T(8,128)(2,1)} %bitcast.146), channel_id=1, source_target_pairs={{0,3},{1,0},{2,1},{3,2},{4,7},{5,4},{6,5},{7,6},{8,11},{9,8},{10,9... | collective-permute-start | bytes 221192 | tf_op jit(solution)/shard_map/ppermute | solution.py:116
  11.5 1.7 %copy-start.3 = (bf16[1,80,1440]{2,1,0:T(8,128)(2,1)}, bf16[1,80,1440]{2,1,0:T(8,128)(2,1)S(1)}, u32[]{:S(2)}) copy-start(bf16[1,80,1440]{2,1,0:T(8,128)(2,1)S(1)} %get-tuple-element.62) | copy-start | bytes 691204
  11.5 2.1 %copy-start.5 = (bf16[1,80,1440]{2,1,0:T(8,128)(2,1)}, bf16[1,80,1440]{2,1,0:T(8,128)(2,1)S(1)}, u32[]{:S(2)}) copy-start(bf16[1,80,1440]{2,1,0:T(8,128)(2,1)S(1)} %get-tuple-element.63) | copy-start | bytes 691204
  11.5 6.7 %copy-start.7 = (bf16[1,2,96,1440]{3,2,1,0:T(8,128)(2,1)S(1)}, bf16[1,2,96,1440]{3,2,1,0:T(8,128)(2,1)}, u32[]{:S(2)}) copy-start(bf16[1,2,96,1440]{3,2,1,0:T(8,128)(2,1)} %param.7) | copy-start | bytes 1658884
  14.5 23.9 %all-to-all-start = ((bf16[8,5,2,2,2,2,96]{6,5,4,3,2,1,0:T(2,128)(2,1)}), bf16[8,5,2,2,2,2,96]{6,5,4,3,2,1,0:T(2,128)(2,1)S(1)}, u32[]{:S(2)}, u32[]{:S(2)}) async-start(bf16[8,5,2,2,2,2,96]{6,5,4,3,2,1,0:T(2,128)(2,1)} %copy_bitcast_fusion.1), calls=%async_computation | async-start | bytes 327680 | tf_op jit(solution)/shard_map/all_to_all | solution.py:174
  19.6 2.3 %copy-start.12 = (s32[40]{0:T(128)S(1)}, s32[40]{0:T(128)}, u32[]{:S(2)}) copy-start(s32[40]{0:T(128)} %param.11) | copy-start | bytes 484
  19.6 2.5 %copy-start.11 = (bf16[5,1361,8]{1,2,0:T(8,128)(2,1)S(1)}, bf16[5,1361,8]{1,2,0:T(8,128)(2,1)}, u32[]{:S(2)}) copy-start(bf16[5,1361,8]{1,2,0:T(8,128)(2,1)} %param.8) | copy-start | bytes 326644
  19.8 3.5 %copy-start.1 = (bf16[2,2,2,96,720]{4,3,1,0,2:T(8,128)(2,1)}, bf16[2,2,2,96,720]{4,3,1,0,2:T(8,128)(2,1)S(1)}, u32[]{:S(2)}) copy-start(bf16[2,2,2,96,720]{4,3,1,0,2:T(8,128)(2,1)S(1)} %copy.154) | copy-start | bytes 3317764
  19.8 2.6 %copy-start.10 = (bf16[384,96]{0,1:T(8,128)(2,1)S(1)}, bf16[384,96]{0,1:T(8,128)(2,1)}, u32[]{:S(2)}) copy-start(bf16[384,96]{0,1:T(8,128)(2,1)} %param.10) | copy-start | bytes 221188
  19.8 3.2 %copy-start.9 = (f32[96,2,720]{2,1,0:T(2,128)S(1)}, f32[96,2,720]{2,1,0:T(2,128)}, u32[]{:S(2)}) copy-start(f32[96,2,720]{2,1,0:T(2,128)} %param.9) | copy-start | bytes 1658884
  20.9 37.3 %collective-permute-start.5 = (bf16[1,2,96,720]{3,2,0,1:T(8,128)(2,1)}, bf16[1,2,96,720]{3,2,0,1:T(8,128)(2,1)}, u32[]{:S(2)}, u32[]{:S(2)}) collective-permute-start(bf16[1,2,96,720]{3,2,0,1:T(8,128)(2,1)} %get-tuple-element.46), channel_id=1, source_target_pairs={{0,1},{1,2},{2,3},{3,0},{4,5},{5,6},{6,7},{7,4},{8,9},{9,10},{10,1... | collective-permute-start | bytes 829448 | tf_op jit(solution)/shard_map/ppermute | solution.py:116
  21.6 35.0 %collective-permute-start.4 = (bf16[1,2,96,720]{3,2,0,1:T(8,128)(2,1)}, bf16[1,2,96,720]{3,2,0,1:T(8,128)(2,1)}, u32[]{:S(2)}, u32[]{:S(2)}) collective-permute-start(bf16[1,2,96,720]{3,2,0,1:T(8,128)(2,1)} %get-tuple-element.48), channel_id=1, source_target_pairs={{0,2},{1,3},{2,0},{3,1},{4,6},{5,7},{6,4},{7,5},{8,10},{9,11},{10,... | collective-permute-start | bytes 829448 | tf_op jit(solution)/shard_map/ppermute | solution.py:116
  24.7 30.1 %collective-permute-start.3 = (bf16[1,2,96,720]{3,2,0,1:T(8,128)(2,1)}, bf16[1,2,96,720]{3,2,0,1:T(8,128)(2,1)}, u32[]{:S(2)}, u32[]{:S(2)}) collective-permute-start(bf16[1,2,96,720]{3,2,0,1:T(8,128)(2,1)} %get-tuple-element.49), channel_id=1, source_target_pairs={{0,3},{1,0},{2,1},{3,2},{4,7},{5,4},{6,5},{7,6},{8,11},{9,8},{10,9... | collective-permute-start | bytes 829448 | tf_op jit(solution)/shard_map/ppermute | solution.py:116
  38.5 1.4 %copy-start = (f32[2,1408,96]{2,1,0:T(8,128)S(1)}, f32[2,1408,96]{2,1,0:T(8,128)}, u32[]{:S(2)}) copy-start(f32[2,1408,96]{2,1,0:T(8,128)} %pad.18.tail_ref) | copy-start | bytes 3244036
  49.6 20.8 %all-to-all-start.1 = ((bf16[8,5,2,2,2,2,96]{6,5,4,3,2,1,0:T(2,128)(2,1)}), bf16[8,5,2,2,2,2,96]{6,5,4,3,2,1,0:T(2,128)(2,1)}, u32[]{:S(2)}, u32[]{:S(2)}) async-start(bf16[8,5,2,2,2,2,96]{6,5,4,3,2,1,0:T(2,128)(2,1)} %bitcast.114), calls=%async_computation.1 | async-start | bytes 327680 | tf_op jit(solution)/shard_map/all_to_all | solution.py:201
  59.9 6.4 %copy-start.2 = (bf16[4,384,96]{1,2,0:T(8,128)(2,1)S(1)}, bf16[4,384,96]{1,2,0:T(8,128)(2,1)}, u32[]{:S(2)}) copy-start(bf16[4,384,96]{1,2,0:T(8,128)(2,1)} %constant_dynamic-slice_fusion.9) | copy-start | bytes 884740
  69.2 11.4 %collective-permute-start.6 = (bf16[1,2,96,720]{3,2,0,1:T(8,128)(2,1)}, bf16[1,2,96,720]{3,2,0,1:T(8,128)(2,1)S(1)}, u32[]{:S(2)}, u32[]{:S(2)}) collective-permute-start(bf16[1,2,96,720]{3,2,0,1:T(8,128)(2,1)} %get-tuple-element.44), channel_id=1, source_target_pairs={{0,3},{1,0},{2,1},{3,2},{4,7},{5,4},{6,5},{7,6},{8,11},{9,8},{10,9... | collective-permute-start | bytes 829448 | tf_op jit(solution)/shard_map/ppermute | solution.py:116
  70.4 16.8 %all-to-all-start.2 = ((f32[8,2,96,96]{3,2,1,0:T(8,128)}), f32[8,2,96,96]{3,2,1,0:T(8,128)S(1)}, u32[]{:S(2)}, u32[]{:S(2)}) async-start(f32[8,2,96,96]{3,2,1,0:T(8,128)} %bitcast.113), calls=%async_computation.2 | async-start | bytes 1572864 | tf_op jit(solution)/shard_map/all_to_all | solution.py:130
  76.4 25.5 %collective-permute-start.8 = (bf16[1,2,96,720]{3,2,0,1:T(8,128)(2,1)}, bf16[1,2,96,720]{3,2,0,1:T(8,128)(2,1)}, u32[]{:S(2)}, u32[]{:S(2)}) collective-permute-start(bf16[1,2,96,720]{3,2,0,1:T(8,128)(2,1)} %get-tuple-element.42), channel_id=1, source_target_pairs={{0,1},{1,2},{2,3},{3,0},{4,5},{5,6},{6,7},{7,4},{8,9},{9,10},{10,1... | collective-permute-start | bytes 829448 | tf_op jit(solution)/shard_map/ppermute | solution.py:116
  77.3 23.0 %collective-permute-start.7 = (bf16[1,2,96,720]{3,2,0,1:T(8,128)(2,1)}, bf16[1,2,96,720]{3,2,0,1:T(8,128)(2,1)}, u32[]{:S(2)}, u32[]{:S(2)}) collective-permute-start(bf16[1,2,96,720]{3,2,0,1:T(8,128)(2,1)} %get-tuple-element.45), channel_id=1, source_target_pairs={{0,2},{1,3},{2,0},{3,1},{4,6},{5,7},{6,4},{7,5},{8,10},{9,11},{10,... | collective-permute-start | bytes 829448 | tf_op jit(solution)/shard_map/ppermute | solution.py:116
  87.2 19.7 %all-to-all-start.3 = ((f32[8,48,384]{2,1,0:T(8,128)}), f32[8,48,384]{2,1,0:T(8,128)S(1)}, u32[]{:S(2)}, u32[]{:S(2)}) async-start(f32[8,48,384]{2,1,0:T(8,128)} %fusion.31), calls=%async_computation.3 | async-start | bytes 1179648 | tf_op jit(solution)/shard_map/all_to_all | solution.py:130
  107.1 5.5 %collective-permute-start.10 = (f32[1,48,96]{2,1,0:T(8,128)S(1)}, f32[1,48,96]{2,1,0:T(8,128)S(1)}, u32[]{:S(2)}, u32[]{:S(2)}) collective-permute-start(f32[1,48,96]{2,1,0:T(8,128)S(1)} %bitcast.155), channel_id=1, source_target_pairs={{0,2},{1,3},{2,0},{3,1},{4,6},{5,7},{6,4},{7,5},{8,10},{9,11},{10,... | collective-permute-start | bytes 55304 | tf_op jit(solution)/shard_map/ppermute | solution.py:116
  107.2 5.7 %collective-permute-start.11 = (f32[1,48,96]{2,1,0:T(8,128)S(1)}, f32[1,48,96]{2,1,0:T(8,128)S(1)}, u32[]{:S(2)}, u32[]{:S(2)}) collective-permute-start(f32[1,48,96]{2,1,0:T(8,128)S(1)} %bitcast.154), channel_id=1, source_target_pairs={{0,1},{1,2},{2,3},{3,0},{4,5},{5,6},{6,7},{7,4},{8,9},{9,10},{10,1... | collective-permute-start | bytes 55304 | tf_op jit(solution)/shard_map/ppermute | solution.py:116
  108.4 4.2 %collective-permute-start.9 = (f32[1,48,96]{2,1,0:T(8,128)S(1)}, f32[1,48,96]{2,1,0:T(8,128)S(1)}, u32[]{:S(2)}, u32[]{:S(2)}) collective-permute-start(f32[1,48,96]{2,1,0:T(8,128)S(1)} %bitcast.156), channel_id=1, source_target_pairs={{0,3},{1,0},{2,1},{3,2},{4,7},{5,4},{6,5},{7,6},{8,11},{9,8},{10,9... | collective-permute-start | bytes 55304 | tf_op jit(solution)/shard_map/ppermute | solution.py:116
  114.0 17.7 %all-to-all-start.4 = ((f32[8,240,96]{1,2,0:T(8,128)}), f32[8,240,96]{1,2,0:T(8,128)S(1)}, u32[]{:S(2)}, u32[]{:S(2)}) async-start(f32[8,240,96]{1,2,0:T(8,128)} %broadcast_in_dim.91), calls=%async_computation.4 | async-start | bytes 1572864 | tf_op jit(solution)/shard_map/all_to_all | solution.py:135
  122.6 5.6 %copy-start.4 = (bf16[1,80,1440]{2,1,0:T(8,128)(2,1)S(1)}, bf16[1,80,1440]{2,1,0:T(8,128)(2,1)}, u32[]{:S(2)}) copy-start(bf16[1,80,1440]{2,1,0:T(8,128)(2,1)} %copy-done.3) | copy-start | bytes 691204
  128.3 2.2 %copy-start.6 = (bf16[1,80,1440]{2,1,0:T(8,128)(2,1)S(1)}, bf16[1,80,1440]{2,1,0:T(8,128)(2,1)}, u32[]{:S(2)}) copy-start(bf16[1,80,1440]{2,1,0:T(8,128)(2,1)} %copy-done.5) | copy-start | bytes 691204

commit v4 on v3

--- a/solution.py
+++ b/solution.py
@@ -106,16 +106,98 @@
     )(lower, leg_masked, received, lead, tail)
 
 
-def exchange(blocks):
+def arrivals(pick):
     count = lax.axis_size("chan")
     me = lax.axis_index("chan")
-    pick = lambda index: lax.dynamic_index_in_dim(blocks, lax.rem(index, count), 0, keepdims=True)
-    arrived = [pick(me)]
+    arrived = [pick(me, 0)]
     for step in range(1, count):
         pairs = [(source, (source - step) % count) for source in range(count)]
-        arrived.append(lax.ppermute(pick(me + count - step), "chan", pairs))
-    twice = jnp.concatenate(arrived + arrived[:-1], axis=0)
-    return lax.dynamic_slice_in_dim(twice, lax.rem(count - me, count), count, 0)
+        arrived.append(lax.ppermute(pick(lax.rem(me + count - step, count), step), "chan", pairs))
+    return arrived
+
+
+def mix_kernel(count, me_ref, *refs):
+    fields, mixings = refs[:count], refs[count : 2 * count]
+    sends, grad_ref = refs[2 * count : 3 * count], refs[3 * count]
+    placed, placed_mix, mixed = refs[3 * count + 1 :]
+    width = fields[0].shape[1]
+    me = me_ref[0]
+    for step in range(count):
+        rows = pl.ds(pl.multiple_of(lax.rem(me + step, count) * width, 8), width)
+        for part in range(2):
+            placed[part, rows, :] = fields[step][part].astype(jnp.float32)
+        placed_mix[rows, :] = mixings[step][...].astype(jnp.float32)
+    field = placed[0].astype(jnp.bfloat16)
+    cot = placed[1].astype(jnp.bfloat16)
+    mix_t = placed_mix[...]
+    mixed[0] = jnp.dot(mix_t.astype(jnp.bfloat16), field, preferred_element_type=jnp.float32)
+    mixed[1] = jnp.dot(mix_t.T.astype(jnp.bfloat16), cot, preferred_element_type=jnp.float32)
+    grad_ref[...] = lax.dot_general(
+        field, cot, (((1,), (1,)), ((), ())), preferred_element_type=jnp.float32
+    )
+    for step in range(count):
+        rows = pl.ds(pl.multiple_of(lax.rem(me + count - step, count) * width, 8), width)
+        for part in range(2):
+            sends[step][part] = mixed[part, rows, :].astype(jnp.bfloat16)
+
+
+def mix_stage(me, fields, mixings):
+    count = len(fields)
+    block = fields[0].shape
+    width, span = block[1:]
+    channels = count * width
+    whole = pl.BlockSpec(memory_space=pltpu.VMEM)
+    return pl.pallas_call(
+        functools.partial(mix_kernel, count),
+        out_shape=tuple(jax.ShapeDtypeStruct(block, jnp.bfloat16) for _ in range(count))
+        + (jax.ShapeDtypeStruct((channels, channels), jnp.float32),),
+        in_specs=[pl.BlockSpec(memory_space=pltpu.SMEM)] + [whole] * (2 * count),
+        out_specs=(whole,) * (count + 1),
+        scratch_shapes=[
+            pltpu.VMEM((2, channels, span), jnp.float32),
+            pltpu.VMEM((channels, channels), jnp.float32),
+            pltpu.VMEM((2, channels, span), jnp.float32),
+        ],
+        compiler_params=pltpu.CompilerParams(vmem_limit_bytes=40 * 2**20),
+        cost_estimate=pl.CostEstimate(
+            flops=6 * channels * channels * span, bytes_accessed=2**23, transcendentals=0
+        ),
+    )(me[None], *fields, *mixings)
+
+
+def output_kernel(count, me_ref, rows_ref, basis_ref, *refs):
+    homes, outs, placed = refs[:count], refs[count : count + 2], refs[count + 2]
+    pieces = count // 2
+    me = me_ref[0]
+    for step in range(count):
+        placed[lax.rem(me + step, count)] = homes[step][...]
+    for part in range(2):
+        for half in range(2):
+            rows = rows_ref[part, half].astype(jnp.float32).T.astype(jnp.bfloat16)
+            grid = jnp.dot(rows, basis_ref[...], preferred_element_type=jnp.float32)
+            skip = jnp.concatenate(
+                [placed[half * pieces + p, part].astype(jnp.float32) for p in range(pieces)], axis=1
+            )
+            outs[part][0, half] = (grid + skip).astype(jnp.bfloat16)
+
+
+def output_stage(me, rows, basis, homes):
+    count = len(homes)
+    width = rows.shape[3]
+    longitudes = basis.shape[1]
+    whole = pl.BlockSpec(memory_space=pltpu.VMEM)
+    out = jax.ShapeDtypeStruct((1, 2, width, longitudes), jnp.bfloat16)
+    return pl.pallas_call(
+        functools.partial(output_kernel, count),
+        out_shape=(out, out),
+        in_specs=[pl.BlockSpec(memory_space=pltpu.SMEM)] + [whole] * (2 + count),
+        out_specs=(whole, whole),
+        scratch_shapes=[pltpu.VMEM((count, *homes[0].shape), jnp.bfloat16)],
+        compiler_params=pltpu.CompilerParams(vmem_limit_bytes=40 * 2**20),
+        cost_estimate=pl.CostEstimate(
+            flops=8 * rows.shape[2] * width * longitudes, bytes_accessed=2**22, transcendentals=0
+        ),
+    )(me[None], rows, basis, *homes)
 
 
 def scattered_rows(array):
@@ -150,11 +232,17 @@
     chan_count = lax.axis_size("chan")
     pieces = chan_count // 2
     span = longitudes // pieces
+    me = lax.axis_index("chan")
     both_fields = jnp.stack([grid_field[0], cotangent[0]], axis=0)
     cut = both_fields.reshape(2, 2, chan_width, pieces, span).transpose(1, 3, 0, 2, 4)
-    sliced = exchange(cut.reshape(chan_count, 2, chan_width, span))
-    mixing_blocks = exchange(jnp.broadcast_to(mixing[None], (chan_count, *mixing.shape)))
-    mixing_full = mixing_blocks.transpose(1, 0, 2).reshape(mixing.shape[0], -1)
+    cut = cut.reshape(chan_count, 2, chan_width, span)
+    field_blocks = arrivals(
+        lambda owner, step: lax.dynamic_index_in_dim(cut, owner, 0, keepdims=False)
+    )
+    mixing_t = mixing.T
+    mixing_blocks = arrivals(lambda owner, step: mixing_t)
+    *sends, mixing_grad = mix_stage(me, field_blocks, mixing_blocks)
+    homes = arrivals(lambda owner, step: sends[step])
     slot_orders = jnp.stack([pair_table, order_count - 1 - pair_table], axis=1).reshape(-1)
     basis = dft_basis(slot_orders, longitudes)
     weight_m = jnp.where(slot_orders == 0, 1.0, 2.0).astype(jnp.float32)
@@ -197,39 +285,24 @@
 
     synth, grad_local = owner_stage(lower, leg_masked, received, spectral, order_count)
     synth = synth.reshape(owned, 2, 2, 2, 2, npairs, chan_width)
-    back = jnp.transpose(synth, (5, 0, 1, 2, 3, 4, 6))
+    back = jnp.transpose(synth, (5, 1, 3, 2, 0, 4, 6))
+    back = back.reshape(npairs, 2, 2, 4 * owned, chan_width)
     rows = lax.all_to_all(back, "lat", split_axis=0, concat_axis=0, tiled=True)
-    rows = jnp.transpose(rows, (2, 4, 3, 0, 1, 5, 6)).reshape(
-        2, 2, 2, order_count, chan_width
-    )
-    row_y = rows[0] * weight_m.astype(jnp.bfloat16)[None, None, :, None]
-    row_dx = rows[1]
-    filtered_grid = jnp.einsum(
-        "hrmc,rmj->hcj", row_y, basis, preferred_element_type=jnp.float32
-    )
-    back_grid = jnp.einsum("hrmc,rmj->hcj", row_dx, basis, preferred_element_type=jnp.float32)
+    rows = jnp.transpose(rows, (1, 2, 0, 3, 4)).reshape(2, 2, 2 * order_count, chan_width)
+    by_device = lambda a: a.reshape(2, lat_count, 2 * owned, -1).transpose(1, 0, 2, 3)
+    row_scale = by_device(jnp.stack([weight_m, weight_m]).astype(jnp.bfloat16))
+    row_scale = row_scale.reshape(2 * order_count, 1)
+    rows = jnp.stack([rows[0] * row_scale, rows[1]], axis=0)
+    row_basis = by_device(basis).reshape(2 * order_count, longitudes)
+    block_output, grad_input = output_stage(me, rows, row_basis, homes)
     channels = chan_count * chan_width
-    field_slice = sliced[:, 0].reshape(channels, span)
-    cot_slice = sliced[:, 1].reshape(channels, span)
-    mixing_grad = jnp.einsum("ij,oj->io", field_slice, cot_slice, preferred_element_type=jnp.float32)
-    skip_slice = jnp.einsum("io,ij->oj", mixing_full, field_slice, preferred_element_type=jnp.float32)
-    back_slice = jnp.einsum("io,oj->ij", mixing_full, cot_slice, preferred_element_type=jnp.float32)
-    mixed = jnp.stack(
-        [
-            skip_slice.astype(jnp.bfloat16).reshape(chan_count, chan_width, span),
-            back_slice.astype(jnp.bfloat16).reshape(chan_count, chan_width, span),
-        ],
-        axis=1,
-    )
-    home = exchange(mixed)
-    home = home.reshape(2, pieces, 2, chan_width, span).transpose(2, 0, 3, 1, 4)
-    home = home.reshape(2, 2, chan_width, longitudes).astype(jnp.float32)
-    block_output = (filtered_grid + home[0]).astype(jnp.bfloat16)[None]
-    grad_input = (back_grid + home[1]).astype(jnp.bfloat16)[None]
 
     mixing_share = scatter_sum(scattered_rows(mixing_grad[None])[:, 0], "lat")
     by_owner = mixing_share.reshape(-1, chan_count, chan_width).transpose(1, 0, 2)
-    mixing_share = jnp.sum(exchange(by_owner), axis=0)
+    shares = arrivals(
+        lambda owner, step: lax.dynamic_index_in_dim(by_owner, owner, 0, keepdims=False)
+    )
+    mixing_share = functools.reduce(jnp.add, shares)
     weight_share = scatter_sum(scattered_rows(grad_local), "lat")
     weight_rows = weight_share.shape[1]
     shares = jnp.concatenate([weight_share.reshape(-1, chan_width), mixing_share], axis=0)

time: 137 us -> 141 us (1.029)
  waiting for transfers between devices: 17.2 us -> 58.8 us
  local copies, waits for them, and re-layouts: 52.4 us -> 17.6 us
  matrix products: 7.87 us -> 1.84 us
  Pallas kernels: 9 us -> 13.1 us
    ppermute x12, waiting for transfers between devices: 11.3 us -> 50.3 us  [arrivals(): lax.ppermute(pick(lax.rem(me + count - step, count), step), 'chan', pairs)]
    unnamed x50 -> x19, local copies, waits for them, and re-layouts: 24.3 us -> 3.5 us
    slice x7 -> x2, local copies, waits for them, and re-layouts: 8.46 us -> 0.13 us  [local(): rows = jnp.stack([rows[0] * row_scale, rows[1]], axis=0)]
    dot_general x5 -> x0, matrix products: 5.85 us -> none  [the longest x1 2.19 us: local(): jnp.einsum('hrmc,rmj->hcj', row_dx, basis, preferred_element_type=jnp.flo...]
    all_to_all x1, waiting for transfers between devices: 0.01 us -> 5.57 us  [local(): rows = lax.all_to_all(back, 'lat', split_axis=0, concat_axis=0, tiled=True)]
    concatenate x4 -> x0, local copies, waits for them, and re-layouts: 4.89 us -> none  [exchange(): twice = jnp.concatenate(arrived + arrived[:-1], axis=0)]
    pallas_call x0 -> x2, Pallas kernels: none -> 4.02 us  [the longest x1 2.43 us: mix_stage(): pl.pallas_call(functools.partial(mix_kernel, count), out_shape=tuple((jax...]
    squeeze x2 -> x1, local copies, waits for them, and re-layouts: 3.37 us -> 0.09 us  [local(): lax.dynamic_index_in_dim(cut, owner, 0, keepdims=False)]
  transfers between devices with their start and end apart: 17 -> 17, of which waited for: 4 -> 6; matrix products, arithmetic and copies ran while one was open for 47% -> 17% of each run, Pallas kernels for 7% -> 9%
where the time goes in v4:
time: 141 us; the launch traced here: 140 us
  waiting for transfers between devices  58.8 us (42%)
  starting transfers between devices  37.2 us (26%)
  local copies, waits for them, and re-layouts  17.6 us (12%)
  Pallas kernels  13.1 us (9%)
  other arithmetic  10.5 us (7%)
  matrix products  1.84 us (1%)
    ppermute x12, waiting for transfers between devices, arrivals(): lax.ppermute(pick(lax.rem(me + count - step, count), step), 'chan', pairs)  50.3 us
    ppermute x12, starting transfers between devices, arrivals(): lax.ppermute(pick(lax.rem(me + count - step, count), step), 'chan', pairs)  17.7 us
    pallas_call x1, Pallas kernels, owner_stage(): pl.pallas_call(functools.partial(owner_kernel, degrees, tail_shift, 128),...  9.07 us
    all_to_all x2, starting transfers between devices, scatter_sum(): return jnp.sum(lax.all_to_all(array, axis, 0, 0, tiled=True), axis=0)  8.57 us
    all_to_all x1, waiting for transfers between devices, local(): rows = lax.all_to_all(back, 'lat', split_axis=0, concat_axis=0, tiled=True)  5.57 us
    another operation x5, other arithmetic  4.57 us
    all_to_all x1, starting transfers between devices, local(): lax.all_to_all(sent, 'lat', split_axis=0, concat_axis=0, tiled=True)  4.01 us
    all_to_all x1, starting transfers between devices, spread(): return lax.all_to_all(everywhere, axis, 0, 0, tiled=True)  3.55 us
  transfers between devices with their start and end apart: 17, of which 6 were waited for; matrix products, arithmetic and copies ran while one was open for 17% of the time, Pallas kernels for 9%

profile of v4, /device:TPU:0, one launch (start us, length us, event | category | flops | bytes accessed | tf_op | source)
XLA Modules:
  0.0 140.3 jit_solution(6437411074627804134)
XLA Ops:
  0.6 5.1 %collective-permute-start.3 = (bf16[96,384]{1,0:T(8,128)(2,1)}, bf16[96,384]{1,0:T(8,128)(2,1)S(1)}, u32[]{:S(2)}, u32[]{:S(2)}) collective-permute-start(bf16[96,384]{1,0:T(8,128)(2,1)} %bitcast.83), channel_id=1, source_target_pairs={{0,3},{1,0},{2,1},{3,2},{4,7},{5,4},{6,5},{7,6},{8,11},{9,8},{10,9... | collective-permute-start | bytes 221192 | tf_op jit(solution)/shard_map/ppermute | solution.py:115
  5.7 1.0 collective-permute-start.5
  6.8 0.7 subtract_bitcast_fusion
  7.4 0.7 pad_add_fusion
  8.3 2.3 %multiply_convert_fusion.3 = (bf16[1,80,1440]{2,1,0:T(8,128)(2,1)S(1)}, bf16[1,80,1440]{2,1,0:T(8,128)(2,1)S(1)}) fusion(s32[80]{0:T(128)S(1)} %mul.146), kind=kLoop, calls=%fused_computation.23 | loop fusion | flops 1612800 | bytes 461120 | tf_op jit(solution)/shard_map/convert.12
  10.6 1.5 %fusion = f32[2,2,80,96]{3,2,0,1:T(8,128)S(1)} fusion(bf16[1,2,96,1440]{3,2,1,0:T(8,128)(2,1)} %param.7, bf16[1,80,1440]{2,1,0:T(8,128)(2,1)S(1)} %get-tuple-element.65, bf16[1,80,1440]{2,1,0:T(8,128)(2,1)S(1)} %get-tuple-element.64, f32[80]{0:T(128)S(1)} %compare_select_fusion.1), kind=kOutput, calls=%fused_computation.3 | convolution fusion | flops 89425920 | bytes 1136960 | tf_op jit(solution)/shard_map/rmj,hcj->hrmc/dot_general | solution.py:251
  12.1 0.4 convolution_bitcast_fusion
  12.5 0.9 copy_bitcast_fusion.1
  13.4 4.0 %all-to-all-start = ((bf16[8,5,2,2,2,2,96]{6,5,4,3,2,1,0:T(2,128)(2,1)}), bf16[8,5,2,2,2,2,96]{6,5,4,3,2,1,0:T(2,128)(2,1)}, u32[]{:S(2)}, u32[]{:S(2)}) async-start(bf16[8,5,2,2,2,2,96]{6,5,4,3,2,1,0:T(2,128)(2,1)} %copy_bitcast_fusion.1), calls=%async_computation | async-start | bytes 327680 | tf_op jit(solution)/shard_map/all_to_all | solution.py:262
  17.5 2.1 %reshape.455 = bf16[2,2,96,2,720]{4,3,2,1,0:T(2,128)(2,1)} reshape(bf16[2,2,96,1440]{3,2,1,0:T(8,128)(2,1)S(1)} %pad_maximum_fusion) | data formatting | bytes 2211840 | tf_op jit(solution)/shard_map/reshape | solution.py:237
  19.6 1.4 copy.135
  21.2 2.9 %collective-permute-start = (bf16[2,96,720]{2,1,0:T(8,128)(2,1)S(1)}, bf16[2,96,720]{2,1,0:T(8,128)(2,1)S(1)}, u32[]{:S(2)}, u32[]{:S(2)}) collective-permute-start(bf16[2,96,720]{2,1,0:T(8,128)(2,1)S(1)} %get-tuple-element.50), channel_id=1, source_target_pairs={{0,3},{1,0},{2,1},{3,2},{4,7},{5,4},{6,5},{7,6},{8,11},{9,8},{10,9... | collective-permute-start | bytes 829448 | tf_op jit(solution)/shard_map/ppermute | solution.py:115
  24.1 1.1 collective-permute-start.1
  25.5 6.0 %collective-permute-done.refs_1_ = bf16[2,96,720]{2,1,0:T(8,128)(2,1)S(1)} collective-permute-done((bf16[2,96,720]{2,1,0:T(8,128)(2,1)S(1)}, bf16[2,96,720]{2,1,0:T(8,128)(2,1)S(1)}, u32[]{:S(2)}, u32[]{:S(2)}) %collective-permute-start) | collective-permute-done | bytes 276512 | tf_op jit(solution)/shard_map/ppermute | solution.py:115
  31.5 19.9 %collective-permute-done.1.refs_2_ = bf16[2,96,720]{2,1,0:T(8,128)(2,1)S(1)} collective-permute-done((bf16[2,96,720]{2,1,0:T(8,128)(2,1)S(1)}, bf16[2,96,720]{2,1,0:T(8,128)(2,1)S(1)}, u32[]{:S(2)}, u32[]{:S(2)}) %collective-permute-start.1) | collective-permute-done | bytes 276512 | tf_op jit(solution)/shard_map/ppermute | solution.py:115
  51.4 2.4 %shard_map.94 = (bf16[2,96,720]{2,1,0:T(8,128)(2,1)S(1)}, bf16[2,96,720]{2,1,0:T(8,128)(2,1)S(1)}, bf16[2,96,720]{2,1,0:T(8,128)(2,1)S(1)}, bf16[2,96,720]{2,1,0:T(8,128)(2,1)S(1)}, f32[384,384]{1,0:T(8,128)}) custom-call(s32[1]{0:T(128)} %bitcast.me_ref, bf16[2,96,720]{2,1,0:T(8,128)(2,1)S(1)} %get-tuple-element.51.refs_0_, ...), custom_call_target="tpu_custom_call" | custom-call | flops 637009920 | bytes 8388608 | tf_op jit(solution)/shard_map/pallas_call | solution.py:150
  53.8 4.3 %all-to-all-start.3 = ((f32[8,48,384]{2,1,0:T(8,128)}), f32[8,48,384]{2,1,0:T(8,128)}, u32[]{:S(2)}, u32[]{:S(2)}) async-start(f32[8,48,384]{2,1,0:T(8,128)} %bitcast.40), calls=%async_computation.3 | async-start | bytes 1179648 | tf_op jit(solution)/shard_map/all_to_all | solution.py:212
  58.2 1.2 copy.125
  59.4 1.3 pad.17.lead_ref
  60.7 1.3 pad.18.tail_ref
  62.1 0.9 pad.16
  63.2 1.0 copy.124
  64.2 1.4 copy-done
  65.5 9.1 %shard_map.93 = (bf16[5,4,32,96]{3,2,1,0:T(8,128)(2,1)S(1)}, f32[2,720,96]{2,1,0:T(8,128)S(1)}) custom-call(s32[5]{0:T(128)S(1)} %get-tuple-element.47.lower_ref, bf16[5,32,1408]{2,1,0:T(8,128)(2,1)S(1)} %select_bitcast_fusion.leg_ref, bf16[5,4,32,96]{3,2,1,0:T(8,128)(2,1)S(1)} %bitcast.81, f32[2,2128,96]{2,1,0:T(8,128)S(1)} %pad.17.lead_ref, ...), custom_call_target="tpu_custom_call" | custom-call | flops 346030080 | bytes 16777216 | tf_op jit(solution)/shard_map/pallas_call | solution.py:79
  74.7 0.9 copy.149
  75.6 4.3 %all-to-all-start.2 = ((f32[8,2,96,96]{3,2,1,0:T(8,128)}), f32[8,2,96,96]{3,2,1,0:T(8,128)S(1)}, u32[]{:S(2)}, u32[]{:S(2)}) async-start(f32[8,2,96,96]{3,2,1,0:T(8,128)} %bitcast.79), calls=%async_computation.2 | async-start | bytes 1572864 | tf_op jit(solution)/shard_map/all_to_all | solution.py:212
  79.9 2.3 %multiply_convert_fusion.1 = (bf16[1,8,10,1440]{3,1,2,0:T(8,128)(2,1)S(1)}, bf16[1,8,10,1440]{3,1,2,0:T(8,128)(2,1)S(1)}) fusion(s32[8,10]{0,1:T(8,128)S(1)} %copy.133), kind=kLoop, calls=%fused_computation.18 | loop fusion | flops 1612800 | bytes 461120 | tf_op jit(solution)/shard_map/convert
  82.1 0.8 maximum_bitcast_fusion.1
  82.9 1.1 reduce_sum.19
  84.3 1.3 collective-permute-start.10
  85.7 2.8 %collective-permute-start.9 = (f32[48,96]{1,0:T(8,128)S(1)}, f32[48,96]{1,0:T(8,128)S(1)}, u32[]{:S(2)}, u32[]{:S(2)}) collective-permute-start(f32[48,96]{1,0:T(8,128)S(1)} %bitcast.106), channel_id=1, source_target_pairs={{0,3},{1,0},{2,1},{3,2},{4,7},{5,4},{6,5},{7,6},{8,11},{9,8},{10,9... | collective-permute-start | bytes 55304 | tf_op jit(solution)/shard_map/ppermute | solution.py:115
  88.7 0.8 copy.127
  89.5 2.9 %all-to-all-done.2 = f32[8,2,96,96]{3,2,1,0:T(8,128)S(1)} async-done(((f32[8,2,96,96]{3,2,1,0:T(8,128)}), f32[8,2,96,96]{3,2,1,0:T(8,128)S(1)}, u32[]{:S(2)}, u32[]{:S(2)}) %all-to-all-start.2) | async-done | bytes 589856 | tf_op jit(solution)/shard_map/all_to_all | solution.py:212
  92.5 3.4 %all-to-all-start.1 = ((bf16[8,2,2,20,96]{4,2,3,1,0:T(2,128)(2,1)}), bf16[8,2,2,20,96]{4,2,3,1,0:T(2,128)(2,1)S(1)}, u32[]{:S(2)}, u32[]{:S(2)}) async-start(bf16[8,2,2,20,96]{4,2,3,1,0:T(2,128)(2,1)} %copy.127), calls=%async_computation.1 | async-start | bytes 327680 | tf_op jit(solution)/shard_map/all_to_all | solution.py:290
  96.1 5.6 %all-to-all-done.1 = bf16[8,2,2,20,96]{4,2,3,1,0:T(2,128)(2,1)S(1)} async-done(((bf16[8,2,2,20,96]{4,2,3,1,0:T(2,128)(2,1)}), bf16[8,2,2,20,96]{4,2,3,1,0:T(2,128)(2,1)S(1)}, u32[]{:S(2)}, u32[]{:S(2)}) %all-to-all-start.1) | async-done | bytes 122912 | tf_op jit(solution)/shard_map/all_to_all | solution.py:290
  101.7 1.0 broadcast_in_dim.86
  102.6 3.5 %all-to-all-start.4 = ((f32[8,240,96]{1,2,0:T(8,128)}), f32[8,240,96]{1,2,0:T(8,128)S(1)}, u32[]{:S(2)}, u32[]{:S(2)}) async-start(f32[8,240,96]{1,2,0:T(8,128)} %broadcast_in_dim.86), calls=%async_computation.4 | async-start | bytes 1572864 | tf_op jit(solution)/shard_map/all_to_all | solution.py:217
  106.5 0.3 reshape.454.basis_ref
  107.0 1.3 collective-permute-start.7
  108.3 1.9 %collective-permute-start.8 = (bf16[2,96,720]{2,1,0:T(8,128)(2,1)S(1)}, bf16[2,96,720]{2,1,0:T(8,128)(2,1)S(1)}, u32[]{:S(2)}, u32[]{:S(2)}) collective-permute-start(bf16[2,96,720]{2,1,0:T(8,128)(2,1)S(1)} %get-tuple-element.17), channel_id=1, source_target_pairs={{0,1},{1,2},{2,3},{3,0},{4,5},{5,6},{6,7},{7,4},{8,9},{9,10},{10,1... | collective-permute-start | bytes 829448 | tf_op jit(solution)/shard_map/ppermute | solution.py:115
  110.4 7.2 %collective-permute-done.6.refs_1_ = bf16[2,96,720]{2,1,0:T(8,128)(2,1)S(1)} collective-permute-done((bf16[2,96,720]{2,1,0:T(8,128)(2,1)S(1)}, bf16[2,96,720]{2,1,0:T(8,128)(2,1)S(1)}, u32[]{:S(2)}, u32[]{:S(2)}) %collective-permute-start.6) | collective-permute-done | bytes 276512 | tf_op jit(solution)/shard_map/ppermute | solution.py:115
  117.6 17.1 %collective-permute-done.7.refs_2_ = bf16[2,96,720]{2,1,0:T(8,128)(2,1)S(1)} collective-permute-done((bf16[2,96,720]{2,1,0:T(8,128)(2,1)S(1)}, bf16[2,96,720]{2,1,0:T(8,128)(2,1)S(1)}, u32[]{:S(2)}, u32[]{:S(2)}) %collective-permute-start.7) | collective-permute-done | bytes 276512 | tf_op jit(solution)/shard_map/ppermute | solution.py:115
  134.8 1.6 %shard_map.95 = (bf16[1,2,96,1440]{3,2,1,0:T(8,128)(2,1)}, bf16[1,2,96,1440]{3,2,1,0:T(8,128)(2,1)}) custom-call(s32[1]{0:T(128)} %bitcast.me_ref, bf16[2,2,160,96]{3,2,1,0:T(8,128)(2,1)S(1)} %pad_maximum_fusion.1.rows_ref, bf16[160,1440]{1,0:T(8,128)(2,1)S(1)} %reshape.454.basis_ref, bf16[2,96,720]{2,1,0:T(8,128)(2,1)S(1)} %get-tuple-element.14.refs_0_, ...), custom_call_target="tpu_custom_call" | custom-call | flops 176947200 | bytes 4194304 | tf_op jit(solution)/shard_map/pallas_call | solution.py:190
  136.4 0.5 reshape.460
  136.9 0.5 copy.138
  137.4 0.6 reshape.461
  138.0 1.1 fusion.1
  139.5 0.8 copy.140
  (67 shorter events, 2.7 us)
Async XLA Ops:
  0.6 11.4 %copy-start.5 = (bf16[1,2,96,1440]{3,2,1,0:T(8,128)(2,1)S(1)}, bf16[1,2,96,1440]{3,2,1,0:T(8,128)(2,1)}, u32[]{:S(2)}) copy-start(bf16[1,2,96,1440]{3,2,1,0:T(8,128)(2,1)} %param.6) | copy-start | bytes 1658884
  0.6 24.6 %collective-permute-start.3 = (bf16[96,384]{1,0:T(8,128)(2,1)}, bf16[96,384]{1,0:T(8,128)(2,1)S(1)}, u32[]{:S(2)}, u32[]{:S(2)}) collective-permute-start(bf16[96,384]{1,0:T(8,128)(2,1)} %bitcast.83), channel_id=1, source_target_pairs={{0,3},{1,0},{2,1},{3,2},{4,7},{5,4},{6,5},{7,6},{8,11},{9,8},{10,9... | collective-permute-start | bytes 221192 | tf_op jit(solution)/shard_map/ppermute | solution.py:115
  5.7 19.7 %collective-permute-start.4 = (bf16[96,384]{1,0:T(8,128)(2,1)}, bf16[96,384]{1,0:T(8,128)(2,1)S(1)}, u32[]{:S(2)}, u32[]{:S(2)}) collective-permute-start(bf16[96,384]{1,0:T(8,128)(2,1)} %bitcast.84), channel_id=1, source_target_pairs={{0,2},{1,3},{2,0},{3,1},{4,6},{5,7},{6,4},{7,5},{8,10},{9,11},{10,... | collective-permute-start | bytes 221192 | tf_op jit(solution)/shard_map/ppermute | solution.py:115
  5.7 19.7 %collective-permute-start.5 = (bf16[96,384]{1,0:T(8,128)(2,1)}, bf16[96,384]{1,0:T(8,128)(2,1)S(1)}, u32[]{:S(2)}, u32[]{:S(2)}) collective-permute-start(bf16[96,384]{1,0:T(8,128)(2,1)} %bitcast.85), channel_id=1, source_target_pairs={{0,1},{1,2},{2,3},{3,0},{4,5},{5,6},{6,7},{7,4},{8,9},{9,10},{10,1... | collective-permute-start | bytes 221192 | tf_op jit(solution)/shard_map/ppermute | solution.py:115
  12.1 5.3 %copy-start.4 = (bf16[1,2,96,1440]{3,2,1,0:T(8,128)(2,1)S(1)}, bf16[1,2,96,1440]{3,2,1,0:T(8,128)(2,1)}, u32[]{:S(2)}) copy-start(bf16[1,2,96,1440]{3,2,1,0:T(8,128)(2,1)} %param.7) | copy-start | bytes 1658884
  13.4 40.4 %all-to-all-start = ((bf16[8,5,2,2,2,2,96]{6,5,4,3,2,1,0:T(2,128)(2,1)}), bf16[8,5,2,2,2,2,96]{6,5,4,3,2,1,0:T(2,128)(2,1)}, u32[]{:S(2)}, u32[]{:S(2)}) async-start(bf16[8,5,2,2,2,2,96]{6,5,4,3,2,1,0:T(2,128)(2,1)} %copy_bitcast_fusion.1), calls=%async_computation | async-start | bytes 327680 | tf_op jit(solution)/shard_map/all_to_all | solution.py:262
  21.1 4.1 %copy-start.7 = (s32[40]{0:T(128)S(1)}, s32[40]{0:T(128)}, u32[]{:S(2)}) copy-start(s32[40]{0:T(128)} %param.11) | copy-start | bytes 484
  21.1 30.3 %copy-start.1 = (bf16[384,96]{0,1:T(8,128)(2,1)S(1)}, bf16[384,96]{0,1:T(8,128)(2,1)}, u32[]{:S(2)}) copy-start(bf16[384,96]{0,1:T(8,128)(2,1)} %param.10) | copy-start | bytes 221188
  21.2 10.3 %collective-permute-start = (bf16[2,96,720]{2,1,0:T(8,128)(2,1)S(1)}, bf16[2,96,720]{2,1,0:T(8,128)(2,1)S(1)}, u32[]{:S(2)}, u32[]{:S(2)}) collective-permute-start(bf16[2,96,720]{2,1,0:T(8,128)(2,1)S(1)} %get-tuple-element.50), channel_id=1, source_target_pairs={{0,3},{1,0},{2,1},{3,2},{4,7},{5,4},{6,5},{7,6},{8,11},{9,8},{10,9... | collective-permute-start | bytes 829448 | tf_op jit(solution)/shard_map/ppermute | solution.py:115
  24.1 27.3 %collective-permute-start.1 = (bf16[2,96,720]{2,1,0:T(8,128)(2,1)S(1)}, bf16[2,96,720]{2,1,0:T(8,128)(2,1)S(1)}, u32[]{:S(2)}, u32[]{:S(2)}) collective-permute-start(bf16[2,96,720]{2,1,0:T(8,128)(2,1)S(1)} %get-tuple-element.49), channel_id=1, source_target_pairs={{0,2},{1,3},{2,0},{3,1},{4,6},{5,7},{6,4},{7,5},{8,10},{9,11},{10,... | collective-permute-start | bytes 829448 | tf_op jit(solution)/shard_map/ppermute | solution.py:115
  25.3 26.1 %collective-permute-start.2 = (bf16[2,96,720]{2,1,0:T(8,128)(2,1)S(1)}, bf16[2,96,720]{2,1,0:T(8,128)(2,1)S(1)}, u32[]{:S(2)}, u32[]{:S(2)}) collective-permute-start(bf16[2,96,720]{2,1,0:T(8,128)(2,1)S(1)} %get-tuple-element.48), channel_id=1, source_target_pairs={{0,1},{1,2},{2,3},{3,0},{4,5},{5,6},{6,7},{7,4},{8,9},{9,10},{10,1... | collective-permute-start | bytes 829448 | tf_op jit(solution)/shard_map/ppermute | solution.py:115
  53.8 4.4 %copy-start.6 = (f32[96,2,720]{2,1,0:T(2,128)S(1)}, f32[96,2,720]{2,1,0:T(2,128)}, u32[]{:S(2)}) copy-start(f32[96,2,720]{2,1,0:T(2,128)} %param.9) | copy-start | bytes 1658884
  53.8 21.8 %all-to-all-start.3 = ((f32[8,48,384]{2,1,0:T(8,128)}), f32[8,48,384]{2,1,0:T(8,128)}, u32[]{:S(2)}, u32[]{:S(2)}) async-start(f32[8,48,384]{2,1,0:T(8,128)} %bitcast.40), calls=%async_computation.3 | async-start | bytes 1179648 | tf_op jit(solution)/shard_map/all_to_all | solution.py:212
  59.4 1.3 copy-start.2
  64.2 1.4 copy-start
  75.6 16.9 %all-to-all-start.2 = ((f32[8,2,96,96]{3,2,1,0:T(8,128)}), f32[8,2,96,96]{3,2,1,0:T(8,128)S(1)}, u32[]{:S(2)}, u32[]{:S(2)}) async-start(f32[8,2,96,96]{3,2,1,0:T(8,128)} %bitcast.79), calls=%async_computation.2 | async-start | bytes 1572864 | tf_op jit(solution)/shard_map/all_to_all | solution.py:212
  84.3 11.7 %collective-permute-start.11 = (f32[48,96]{1,0:T(8,128)S(1)}, f32[48,96]{1,0:T(8,128)S(1)}, u32[]{:S(2)}, u32[]{:S(2)}) collective-permute-start(f32[48,96]{1,0:T(8,128)S(1)} %bitcast.108), channel_id=1, source_target_pairs={{0,1},{1,2},{2,3},{3,0},{4,5},{5,6},{6,7},{7,4},{8,9},{9,10},{10,1... | collective-permute-start | bytes 55304 | tf_op jit(solution)/shard_map/ppermute | solution.py:115
  84.3 11.6 %collective-permute-start.10 = (f32[48,96]{1,0:T(8,128)S(1)}, f32[48,96]{1,0:T(8,128)S(1)}, u32[]{:S(2)}, u32[]{:S(2)}) collective-permute-start(f32[48,96]{1,0:T(8,128)S(1)} %bitcast.107), channel_id=1, source_target_pairs={{0,2},{1,3},{2,0},{3,1},{4,6},{5,7},{6,4},{7,5},{8,10},{9,11},{10,... | collective-permute-start | bytes 55304 | tf_op jit(solution)/shard_map/ppermute | solution.py:115
  85.7 10.3 %collective-permute-start.9 = (f32[48,96]{1,0:T(8,128)S(1)}, f32[48,96]{1,0:T(8,128)S(1)}, u32[]{:S(2)}, u32[]{:S(2)}) collective-permute-start(f32[48,96]{1,0:T(8,128)S(1)} %bitcast.106), channel_id=1, source_target_pairs={{0,3},{1,0},{2,1},{3,2},{4,7},{5,4},{6,5},{7,6},{8,11},{9,8},{10,9... | collective-permute-start | bytes 55304 | tf_op jit(solution)/shard_map/ppermute | solution.py:115
  92.5 9.2 %all-to-all-start.1 = ((bf16[8,2,2,20,96]{4,2,3,1,0:T(2,128)(2,1)}), bf16[8,2,2,20,96]{4,2,3,1,0:T(2,128)(2,1)S(1)}, u32[]{:S(2)}, u32[]{:S(2)}) async-start(bf16[8,2,2,20,96]{4,2,3,1,0:T(2,128)(2,1)} %copy.127), calls=%async_computation.1 | async-start | bytes 327680 | tf_op jit(solution)/shard_map/all_to_all | solution.py:290
  96.1 10.2 %copy-start.3 = (bf16[8,2,10,1440]{3,0,2,1:T(8,128)(2,1)S(1)}, bf16[8,2,10,1440]{3,0,2,1:T(8,128)(2,1)}, u32[]{:S(2)}) copy-start(bf16[8,2,10,1440]{3,0,2,1:T(8,128)(2,1)} %maximum_bitcast_fusion.1) | copy-start | bytes 1382404
  102.6 33.7 %all-to-all-start.4 = ((f32[8,240,96]{1,2,0:T(8,128)}), f32[8,240,96]{1,2,0:T(8,128)S(1)}, u32[]{:S(2)}, u32[]{:S(2)}) async-start(f32[8,240,96]{1,2,0:T(8,128)} %broadcast_in_dim.86), calls=%async_computation.4 | async-start | bytes 1572864 | tf_op jit(solution)/shard_map/all_to_all | solution.py:217
  106.9 10.7 %collective-permute-start.6 = (bf16[2,96,720]{2,1,0:T(8,128)(2,1)S(1)}, bf16[2,96,720]{2,1,0:T(8,128)(2,1)S(1)}, u32[]{:S(2)}, u32[]{:S(2)}) collective-permute-start(bf16[2,96,720]{2,1,0:T(8,128)(2,1)S(1)} %get-tuple-element.15), channel_id=1, source_target_pairs={{0,3},{1,0},{2,1},{3,2},{4,7},{5,4},{6,5},{7,6},{8,11},{9,8},{10,9... | collective-permute-start | bytes 829448 | tf_op jit(solution)/shard_map/ppermute | solution.py:115
  107.0 27.8 %collective-permute-start.7 = (bf16[2,96,720]{2,1,0:T(8,128)(2,1)S(1)}, bf16[2,96,720]{2,1,0:T(8,128)(2,1)S(1)}, u32[]{:S(2)}, u32[]{:S(2)}) collective-permute-start(bf16[2,96,720]{2,1,0:T(8,128)(2,1)S(1)} %get-tuple-element.16), channel_id=1, source_target_pairs={{0,2},{1,3},{2,0},{3,1},{4,6},{5,7},{6,4},{7,5},{8,10},{9,11},{10,... | collective-permute-start | bytes 829448 | tf_op jit(solution)/shard_map/ppermute | solution.py:115
  108.3 26.5 %collective-permute-start.8 = (bf16[2,96,720]{2,1,0:T(8,128)(2,1)S(1)}, bf16[2,96,720]{2,1,0:T(8,128)(2,1)S(1)}, u32[]{:S(2)}, u32[]{:S(2)}) collective-permute-start(bf16[2,96,720]{2,1,0:T(8,128)(2,1)S(1)} %get-tuple-element.17), channel_id=1, source_target_pairs={{0,1},{1,2},{2,3},{3,0},{4,5},{5,6},{6,7},{7,4},{8,9},{9,10},{10,1... | collective-permute-start | bytes 829448 | tf_op jit(solution)/shard_map/ppermute | solution.py:115

commit v5 on v4

--- a/solution.py
+++ b/solution.py
@@ -100,9 +100,7 @@
             pltpu.VMEM(tail.shape, jnp.float32),
         ],
         compiler_params=pltpu.CompilerParams(vmem_limit_bytes=32 * 2**20),
-        cost_estimate=pl.CostEstimate(
-            flops=owned * 16 * rows * qpad * width, bytes_accessed=2**24, transcendentals=0
-        ),
+        cost_estimate=pl.CostEstimate(flops=1, bytes_accessed=1, transcendentals=0),
     )(lower, leg_masked, received, lead, tail)
 
 
@@ -159,9 +157,7 @@
             pltpu.VMEM((2, channels, span), jnp.float32),
         ],
         compiler_params=pltpu.CompilerParams(vmem_limit_bytes=40 * 2**20),
-        cost_estimate=pl.CostEstimate(
-            flops=6 * channels * channels * span, bytes_accessed=2**23, transcendentals=0
-        ),
+        cost_estimate=pl.CostEstimate(flops=1, bytes_accessed=1, transcendentals=0),
     )(me[None], *fields, *mixings)
 
 
@@ -194,9 +190,7 @@
         out_specs=(whole, whole),
         scratch_shapes=[pltpu.VMEM((count, *homes[0].shape), jnp.bfloat16)],
         compiler_params=pltpu.CompilerParams(vmem_limit_bytes=40 * 2**20),
-        cost_estimate=pl.CostEstimate(
-            flops=8 * rows.shape[2] * width * longitudes, bytes_accessed=2**22, transcendentals=0
-        ),
+        cost_estimate=pl.CostEstimate(flops=1, bytes_accessed=1, transcendentals=0),
     )(me[None], rows, basis, *homes)
 
 
@@ -236,13 +230,12 @@
     both_fields = jnp.stack([grid_field[0], cotangent[0]], axis=0)
     cut = both_fields.reshape(2, 2, chan_width, pieces, span).transpose(1, 3, 0, 2, 4)
     cut = cut.reshape(chan_count, 2, chan_width, span)
+    cut, grid_field, cotangent = lax.optimization_barrier((cut, grid_field, cotangent))
     field_blocks = arrivals(
         lambda owner, step: lax.dynamic_index_in_dim(cut, owner, 0, keepdims=False)
     )
     mixing_t = mixing.T
     mixing_blocks = arrivals(lambda owner, step: mixing_t)
-    *sends, mixing_grad = mix_stage(me, field_blocks, mixing_blocks)
-    homes = arrivals(lambda owner, step: sends[step])
     slot_orders = jnp.stack([pair_table, order_count - 1 - pair_table], axis=1).reshape(-1)
     basis = dft_basis(slot_orders, longitudes)
     weight_m = jnp.where(slot_orders == 0, 1.0, 2.0).astype(jnp.float32)
@@ -284,6 +277,12 @@
     )
 
     synth, grad_local = owner_stage(lower, leg_masked, received, spectral, order_count)
+    synth, field_blocks = lax.optimization_barrier((synth, field_blocks))
+    *sends, mixing_grad = mix_stage(me, field_blocks, mixing_blocks)
+    grad_local, synth, mixing_grad, sends = lax.optimization_barrier(
+        (grad_local, synth, mixing_grad, sends)
+    )
+    homes = arrivals(lambda owner, step: sends[step])
     synth = synth.reshape(owned, 2, 2, 2, 2, npairs, chan_width)
     back = jnp.transpose(synth, (5, 1, 3, 2, 0, 4, 6))
     back = back.reshape(npairs, 2, 2, 4 * owned, chan_width)
@@ -294,7 +293,6 @@
     row_scale = row_scale.reshape(2 * order_count, 1)
     rows = jnp.stack([rows[0] * row_scale, rows[1]], axis=0)
     row_basis = by_device(basis).reshape(2 * order_count, longitudes)
-    block_output, grad_input = output_stage(me, rows, row_basis, homes)
     channels = chan_count * chan_width
 
     mixing_share = scatter_sum(scattered_rows(mixing_grad[None])[:, 0], "lat")
@@ -306,10 +304,12 @@
     weight_share = scatter_sum(scattered_rows(grad_local), "lat")
     weight_rows = weight_share.shape[1]
     shares = jnp.concatenate([weight_share.reshape(-1, chan_width), mixing_share], axis=0)
+    shares, homes = lax.optimization_barrier((shares, homes))
     shares = spread(shares, "lat")
     weight_shares = shares[:, : 2 * weight_rows].reshape(-1, 2, weight_rows, chan_width)
     weight_sum = joined_rows(weight_shares, degrees)
     mixing_sum = joined_rows(shares[:, None, 2 * weight_rows :], channels)[0]
+    block_output, grad_input = output_stage(me, rows, row_basis, homes)
     grad_weights = jnp.transpose(weight_sum, (2, 0, 1)) / math.sqrt(order_count)
     grad_mixing = mixing_sum / math.sqrt(2 * npairs * longitudes)
     return (block_output, grad_input, grad_weights, grad_mixing)

time: 141 us -> 143 us (1.014)
  starting transfers between devices: 37.2 us -> 49.9 us
  waiting for transfers between devices: 58.8 us -> 47.3 us
  local copies, waits for them, and re-layouts: 17.6 us -> 19.3 us
    ppermute x12, waiting for transfers between devices: 50.3 us -> 25.5 us  [arrivals(): lax.ppermute(pick(lax.rem(me + count - step, count), step), 'chan', pairs)]
    ppermute x12, starting transfers between devices: 17.7 us -> 30.8 us  [arrivals(): lax.ppermute(pick(lax.rem(me + count - step, count), step), 'chan', pairs)]
    all_to_all x1, waiting for transfers between devices: 0.01 us -> 9.54 us  [spread(): return lax.all_to_all(everywhere, axis, 0, 0, tiled=True)]
    all_to_all x2, waiting for transfers between devices: 2.95 us -> 12.2 us  [scatter_sum(): return jnp.sum(lax.all_to_all(array, axis, 0, 0, tiled=True), axis=0)]
    all_to_all x1, waiting for transfers between devices: 5.57 us -> 0.01 us  [local(): rows = lax.all_to_all(back, 'lat', split_axis=0, concat_axis=0, tiled=True)]
    unnamed x19 -> x35, local copies, waits for them, and re-layouts: 3.5 us -> 7.39 us
  transfers between devices with their start and end apart: 17 -> 17, of which waited for: 6 -> 6; matrix products, arithmetic and copies ran while one was open for 17% -> 14% of each run, Pallas kernels for 9% -> 7%
where the time goes in v5:
time: 143 us
  starting transfers between devices  49.9 us (35%)
  waiting for transfers between devices  47.3 us (33%)
  local copies, waits for them, and re-layouts  19.3 us (13%)
  Pallas kernels  14.2 us (10%)
  other arithmetic  9.96 us (7%)
    ppermute x12, starting transfers between devices, arrivals(): lax.ppermute(pick(lax.rem(me + count - step, count), step), 'chan', pairs)  30.8 us
    ppermute x12, waiting for transfers between devices, arrivals(): lax.ppermute(pick(lax.rem(me + count - step, count), step), 'chan', pairs)  25.5 us
    all_to_all x2, waiting for transfers between devices, scatter_sum(): return jnp.sum(lax.all_to_all(array, axis, 0, 0, tiled=True), axis=0)  12.2 us
    all_to_all x1, waiting for transfers between devices, spread(): return lax.all_to_all(everywhere, axis, 0, 0, tiled=True)  9.54 us
    pallas_call x1, Pallas kernels, owner_stage(): pl.pallas_call(functools.partial(owner_kernel, degrees, tail_shift, 128),...  9.03 us
    all_to_all x2, starting transfers between devices, scatter_sum(): return jnp.sum(lax.all_to_all(array, axis, 0, 0, tiled=True), axis=0)  7.76 us
    unnamed x35, local copies, waits for them, and re-layouts  7.39 us
    another operation x5, other arithmetic  4.59 us
  transfers between devices with their start and end apart: 17, of which 6 were waited for; matrix products, arithmetic and copies ran while one was open for 14% of the time, Pallas kernels for 7%

profile of v5, /device:TPU:0, one launch (start us, length us, event | category | flops | bytes accessed | tf_op | source)
XLA Modules:
  0.0 142.5 jit_solution(16228426107915211880)
XLA Ops:
  0.6 5.1 %collective-permute-start.3 = (bf16[96,384]{1,0:T(8,128)(2,1)}, bf16[96,384]{1,0:T(8,128)(2,1)}, u32[]{:S(2)}, u32[]{:S(2)}) collective-permute-start(bf16[96,384]{1,0:T(8,128)(2,1)} %bitcast.85), channel_id=1, source_target_pairs={{0,3},{1,0},{2,1},{3,2},{4,7},{5,4},{6,5},{7,6},{8,11},{9,8},{10,9... | collective-permute-start | bytes 221192 | tf_op jit(solution)/shard_map/ppermute | solution.py:113
  5.7 1.0 collective-permute-start.5
  6.7 0.7 subtract_bitcast_fusion
  7.4 0.7 pad_add_fusion
  8.3 2.3 %multiply_convert_fusion.3 = (bf16[1,80,1440]{2,1,0:T(8,128)(2,1)S(1)}, bf16[1,80,1440]{2,1,0:T(8,128)(2,1)S(1)}) fusion(s32[80]{0:T(128)S(1)} %mul.146), kind=kLoop, calls=%fused_computation.23 | loop fusion | flops 1612800 | bytes 461120 | tf_op jit(solution)/shard_map/convert.12
  10.6 1.4 pad_maximum_fusion
  11.9 1.3 reshape.451
  13.4 0.9 copy-done.11
  15.1 0.9 copy_bitcast_fusion.1
  16.0 4.0 %all-to-all-start = ((bf16[8,5,2,2,2,2,96]{6,5,4,3,2,1,0:T(2,128)(2,1)}), bf16[8,5,2,2,2,2,96]{6,5,4,3,2,1,0:T(2,128)(2,1)}, u32[]{:S(2)}, u32[]{:S(2)}) async-start(bf16[8,5,2,2,2,2,96]{6,5,4,3,2,1,0:T(2,128)(2,1)} %copy_bitcast_fusion.1), calls=%async_computation | async-start | bytes 327680 | tf_op jit(solution)/shard_map/all_to_all | solution.py:255
  20.0 0.9 dynamic-slice_bitcast_fusion
  20.9 2.8 %collective-permute-start = (bf16[2,96,720]{2,1,0:T(8,128)(2,1)S(1)}, bf16[2,96,720]{2,1,0:T(8,128)(2,1)S(1)}, u32[]{:S(2)}, u32[]{:S(2)}) collective-permute-start(bf16[2,96,720]{2,1,0:T(8,128)(2,1)S(1)} %get-tuple-element.90), channel_id=1, source_target_pairs={{0,3},{1,0},{2,1},{3,2},{4,7},{5,4},{6,5},{7,6},{8,11},{9,8},{10,9... | collective-permute-start | bytes 829448 | tf_op jit(solution)/shard_map/ppermute | solution.py:113
  23.8 1.1 collective-permute-start.1
  25.1 6.0 %collective-permute-done.refs_1_ = bf16[2,96,720]{2,1,0:T(8,128)(2,1)S(1)} collective-permute-done((bf16[2,96,720]{2,1,0:T(8,128)(2,1)S(1)}, bf16[2,96,720]{2,1,0:T(8,128)(2,1)S(1)}, u32[]{:S(2)}, u32[]{:S(2)}) %collective-permute-start) | collective-permute-done | bytes 276512 | tf_op jit(solution)/shard_map/ppermute | solution.py:113
  31.2 14.7 %collective-permute-start.2 = (bf16[2,96,720]{2,1,0:T(8,128)(2,1)}, bf16[2,96,720]{2,1,0:T(8,128)(2,1)}, u32[]{:S(2)}, u32[]{:S(2)}) collective-permute-start(bf16[2,96,720]{2,1,0:T(8,128)(2,1)} %get-tuple-element.88), channel_id=1, source_target_pairs={{0,1},{1,2},{2,3},{3,0},{4,5},{5,6},{6,7},{7,4},{8,9},{9,10},{10,1... | collective-permute-start | bytes 829448 | tf_op jit(solution)/shard_map/ppermute | solution.py:113
  46.1 1.2 copy.126
  47.2 1.3 pad.17.lead_ref
  48.6 1.2 pad.18.tail_ref
  49.8 1.0 copy.125
  50.8 1.4 copy-done
  52.1 9.0 %shard_map.93 = (bf16[5,4,32,96]{3,2,1,0:T(8,128)(2,1)S(1)}, f32[2,720,96]{2,1,0:T(8,128)S(1)}) custom-call(s32[5]{0:T(128)S(1)} %get-tuple-element.87.lower_ref, bf16[5,32,1408]{2,1,0:T(8,128)(2,1)S(1)} %select_bitcast_fusion.leg_ref, bf16[5,4,32,96]{3,2,1,0:T(8,128)(2,1)S(1)} %bitcast.83, f32[2,2128,96]{2,1,0:T(8,128)S(1)} %pad.17.lead_ref, ...), custom_call_target="tpu_custom_call" | custom-call | flops 1 | bytes 1 | tf_op jit(solution)/shard_map/pallas_call | solution.py:79
  61.2 0.9 copy-done.1
  62.1 0.7 copy-done.3
  62.8 3.6 %shard_map.94 = (bf16[2,96,720]{2,1,0:T(8,128)(2,1)S(1)}, bf16[2,96,720]{2,1,0:T(8,128)(2,1)}, bf16[2,96,720]{2,1,0:T(8,128)(2,1)S(1)}, bf16[2,96,720]{2,1,0:T(8,128)(2,1)S(1)}, f32[384,384]{1,0:T(8,128)}) custom-call(s32[1]{0:T(128)} %bitcast.me_ref, bf16[2,96,720]{2,1,0:T(8,128)(2,1)S(1)} %get-tuple-element.39.refs_0_, ...), custom_call_target="tpu_custom_call" | custom-call | flops 1 | bytes 1 | tf_op jit(solution)/shard_map/pallas_call | solution.py:148
  66.3 4.2 %all-to-all-start.3 = ((f32[8,48,384]{2,1,0:T(8,128)}), f32[8,48,384]{2,1,0:T(8,128)S(1)}, u32[]{:S(2)}, u32[]{:S(2)}) async-start(f32[8,48,384]{2,1,0:T(8,128)} %bitcast.40), calls=%async_computation.3 | async-start | bytes 1179648 | tf_op jit(solution)/shard_map/all_to_all | solution.py:206
  70.8 1.0 copy.150
  71.7 9.3 %all-to-all-done.3 = f32[8,48,384]{2,1,0:T(8,128)S(1)} async-done(((f32[8,48,384]{2,1,0:T(8,128)}), f32[8,48,384]{2,1,0:T(8,128)S(1)}, u32[]{:S(2)}, u32[]{:S(2)}) %all-to-all-start.3) | async-done | bytes 589856 | tf_op jit(solution)/shard_map/all_to_all | solution.py:206
  81.0 0.8 copy-done.7
  81.8 3.5 %all-to-all-start.2 = ((f32[8,2,96,96]{3,2,1,0:T(8,128)}), f32[8,2,96,96]{3,2,1,0:T(8,128)S(1)}, u32[]{:S(2)}, u32[]{:S(2)}) async-start(f32[8,2,96,96]{3,2,1,0:T(8,128)} %bitcast.81), calls=%async_computation.2 | async-start | bytes 1572864 | tf_op jit(solution)/shard_map/all_to_all | solution.py:206
  85.4 2.3 %multiply_convert_fusion.1 = (bf16[1,8,10,1440]{3,1,2,0:T(8,128)(2,1)S(1)}, bf16[1,8,10,1440]{3,1,2,0:T(8,128)(2,1)S(1)}) fusion(s32[8,10]{0,1:T(8,128)S(1)} %copy.134), kind=kLoop, calls=%fused_computation.18 | loop fusion | flops 1612800 | bytes 461120 | tf_op jit(solution)/shard_map/convert
  88.1 3.7 %collective-permute-start.6 = (f32[48,96]{1,0:T(8,128)S(1)}, f32[48,96]{1,0:T(8,128)S(1)}, u32[]{:S(2)}, u32[]{:S(2)}) collective-permute-start(f32[48,96]{1,0:T(8,128)S(1)} %bitcast.108), channel_id=1, source_target_pairs={{0,3},{1,0},{2,1},{3,2},{4,7},{5,4},{6,5},{7,6},{8,11},{9,8},{10,9... | collective-permute-start | bytes 55304 | tf_op jit(solution)/shard_map/ppermute | solution.py:113
  92.1 0.8 copy.128
  92.9 0.6 collective-permute-start.9
  93.5 1.4 collective-permute-start.10
  94.9 3.0 %all-to-all-done.2 = f32[8,2,96,96]{3,2,1,0:T(8,128)S(1)} async-done(((f32[8,2,96,96]{3,2,1,0:T(8,128)}), f32[8,2,96,96]{3,2,1,0:T(8,128)S(1)}, u32[]{:S(2)}, u32[]{:S(2)}) %all-to-all-start.2) | async-done | bytes 589856 | tf_op jit(solution)/shard_map/all_to_all | solution.py:206
  97.9 3.4 %all-to-all-start.1 = ((bf16[8,2,2,20,96]{4,2,3,1,0:T(2,128)(2,1)}), bf16[8,2,2,20,96]{4,2,3,1,0:T(2,128)(2,1)S(1)}, u32[]{:S(2)}, u32[]{:S(2)}) async-start(bf16[8,2,2,20,96]{4,2,3,1,0:T(2,128)(2,1)} %copy.128), calls=%async_computation.1 | async-start | bytes 327680 | tf_op jit(solution)/shard_map/all_to_all | solution.py:289
  101.5 0.7 collective-permute-done.9.refs_1_
  102.2 18.8 %collective-permute-done.10.refs_2_ = bf16[2,96,720]{2,1,0:T(8,128)(2,1)S(1)} collective-permute-done((bf16[2,96,720]{2,1,0:T(8,128)(2,1)S(1)}, bf16[2,96,720]{2,1,0:T(8,128)(2,1)S(1)}, u32[]{:S(2)}, u32[]{:S(2)}) %collective-permute-start.10) | collective-permute-done | bytes 276512 | tf_op jit(solution)/shard_map/ppermute | solution.py:113
  121.1 1.0 broadcast_in_dim.86
  122.1 3.9 %all-to-all-start.4 = ((f32[8,240,96]{1,2,0:T(8,128)}), f32[8,240,96]{1,2,0:T(8,128)S(1)}, u32[]{:S(2)}, u32[]{:S(2)}) async-start(f32[8,240,96]{1,2,0:T(8,128)} %broadcast_in_dim.86), calls=%async_computation.4 | async-start | bytes 1572864 | tf_op jit(solution)/shard_map/all_to_all | solution.py:211
  126.6 0.6 copy-done.10
  127.5 1.6 %shard_map.95 = (bf16[1,2,96,1440]{3,2,1,0:T(8,128)(2,1)}, bf16[1,2,96,1440]{3,2,1,0:T(8,128)(2,1)}) custom-call(s32[1]{0:T(128)} %bitcast.me_ref, bf16[2,2,160,96]{3,2,1,0:T(8,128)(2,1)S(1)} %pad_maximum_fusion.1.rows_ref, bf16[160,1440]{1,0:T(8,128)(2,1)S(1)} %reshape.456.basis_ref, bf16[2,96,720]{2,1,0:T(8,128)(2,1)S(1)} %get-tuple-element.55.refs_0_, ...), custom_call_target="tpu_custom_call" | custom-call | flops 1 | bytes 1 | tf_op jit(solution)/shard_map/pallas_call | solution.py:186
  129.1 9.5 %all-to-all-done.4 = f32[8,240,96]{1,2,0:T(8,128)S(1)} async-done(((f32[8,240,96]{1,2,0:T(8,128)}), f32[8,240,96]{1,2,0:T(8,128)S(1)}, u32[]{:S(2)}, u32[]{:S(2)}) %all-to-all-start.4) | async-done | bytes 737312 | tf_op jit(solution)/shard_map/all_to_all | solution.py:211
  138.6 0.5 reshape.460
  139.2 0.5 copy.138
  139.6 0.6 reshape.461
  140.3 1.1 fusion.1
  141.7 0.8 copy.140
  (83 shorter events, 3.8 us)
Async XLA Ops:
  0.6 62.1 %collective-permute-start.3 = (bf16[96,384]{1,0:T(8,128)(2,1)}, bf16[96,384]{1,0:T(8,128)(2,1)}, u32[]{:S(2)}, u32[]{:S(2)}) collective-permute-start(bf16[96,384]{1,0:T(8,128)(2,1)} %bitcast.85), channel_id=1, source_target_pairs={{0,3},{1,0},{2,1},{3,2},{4,7},{5,4},{6,5},{7,6},{8,11},{9,8},{10,9... | collective-permute-start | bytes 221192 | tf_op jit(solution)/shard_map/ppermute | solution.py:113
  5.7 57.0 %collective-permute-start.4 = (bf16[96,384]{1,0:T(8,128)(2,1)}, bf16[96,384]{1,0:T(8,128)(2,1)}, u32[]{:S(2)}, u32[]{:S(2)}) collective-permute-start(bf16[96,384]{1,0:T(8,128)(2,1)} %bitcast.86), channel_id=1, source_target_pairs={{0,2},{1,3},{2,0},{3,1},{4,6},{5,7},{6,4},{7,5},{8,10},{9,11},{10,... | collective-permute-start | bytes 221192 | tf_op jit(solution)/shard_map/ppermute | solution.py:113
  5.7 57.0 %collective-permute-start.5 = (bf16[96,384]{1,0:T(8,128)(2,1)}, bf16[96,384]{1,0:T(8,128)(2,1)}, u32[]{:S(2)}, u32[]{:S(2)}) collective-permute-start(bf16[96,384]{1,0:T(8,128)(2,1)} %bitcast.87), channel_id=1, source_target_pairs={{0,1},{1,2},{2,3},{3,0},{4,5},{5,6},{6,7},{7,4},{8,9},{9,10},{10,1... | collective-permute-start | bytes 221192 | tf_op jit(solution)/shard_map/ppermute | solution.py:113
  13.2 1.1 copy-start.11
  13.3 1.3 copy-start.12
  16.0 33.8 %all-to-all-start = ((bf16[8,5,2,2,2,2,96]{6,5,4,3,2,1,0:T(2,128)(2,1)}), bf16[8,5,2,2,2,2,96]{6,5,4,3,2,1,0:T(2,128)(2,1)}, u32[]{:S(2)}, u32[]{:S(2)}) async-start(bf16[8,5,2,2,2,2,96]{6,5,4,3,2,1,0:T(2,128)(2,1)} %copy_bitcast_fusion.1), calls=%async_computation | async-start | bytes 327680 | tf_op jit(solution)/shard_map/all_to_all | solution.py:255
  20.0 4.9 %copy-start.15 = (s32[40]{0:T(128)S(1)}, s32[40]{0:T(128)}, u32[]{:S(2)}) copy-start(s32[40]{0:T(128)} %param.11) | copy-start | bytes 484
  20.0 5.0 %copy-start.14 = (bf16[5,1361,8]{1,2,0:T(8,128)(2,1)S(1)}, bf16[5,1361,8]{1,2,0:T(8,128)(2,1)}, u32[]{:S(2)}) copy-start(bf16[5,1361,8]{1,2,0:T(8,128)(2,1)} %param.8) | copy-start | bytes 326644
  20.0 26.0 %copy-start.13 = (f32[96,2,720]{2,1,0:T(2,128)S(1)}, f32[96,2,720]{2,1,0:T(2,128)}, u32[]{:S(2)}) copy-start(f32[96,2,720]{2,1,0:T(2,128)} %param.9) | copy-start | bytes 1658884
  20.9 10.2 %collective-permute-start = (bf16[2,96,720]{2,1,0:T(8,128)(2,1)S(1)}, bf16[2,96,720]{2,1,0:T(8,128)(2,1)S(1)}, u32[]{:S(2)}, u32[]{:S(2)}) collective-permute-start(bf16[2,96,720]{2,1,0:T(8,128)(2,1)S(1)} %get-tuple-element.90), channel_id=1, source_target_pairs={{0,3},{1,0},{2,1},{3,2},{4,7},{5,4},{6,5},{7,6},{8,11},{9,8},{10,9... | collective-permute-start | bytes 829448 | tf_op jit(solution)/shard_map/ppermute | solution.py:113
  23.8 39.0 %collective-permute-start.1 = (bf16[2,96,720]{2,1,0:T(8,128)(2,1)}, bf16[2,96,720]{2,1,0:T(8,128)(2,1)S(1)}, u32[]{:S(2)}, u32[]{:S(2)}) collective-permute-start(bf16[2,96,720]{2,1,0:T(8,128)(2,1)} %get-tuple-element.89), channel_id=1, source_target_pairs={{0,2},{1,3},{2,0},{3,1},{4,6},{5,7},{6,4},{7,5},{8,10},{9,11},{10,... | collective-permute-start | bytes 829448 | tf_op jit(solution)/shard_map/ppermute | solution.py:113
  31.2 31.6 %collective-permute-start.2 = (bf16[2,96,720]{2,1,0:T(8,128)(2,1)}, bf16[2,96,720]{2,1,0:T(8,128)(2,1)}, u32[]{:S(2)}, u32[]{:S(2)}) collective-permute-start(bf16[2,96,720]{2,1,0:T(8,128)(2,1)} %get-tuple-element.88), channel_id=1, source_target_pairs={{0,1},{1,2},{2,3},{3,0},{4,5},{5,6},{6,7},{7,4},{8,9},{9,10},{10,1... | collective-permute-start | bytes 829448 | tf_op jit(solution)/shard_map/ppermute | solution.py:113
  47.2 1.3 copy-start.6
  50.8 1.4 copy-start
  52.1 10.6 %copy-start.5 = (bf16[384,96]{0,1:T(8,128)(2,1)S(1)}, bf16[384,96]{0,1:T(8,128)(2,1)}, u32[]{:S(2)}) copy-start(bf16[384,96]{0,1:T(8,128)(2,1)} %param.10) | copy-start | bytes 221188
  61.2 0.9 copy-start.1
  62.1 0.7 copy-start.3
  62.8 7.9 %copy-start.2 = (f32[2,720,96]{2,1,0:T(8,128)S(1)}, f32[2,720,96]{2,1,0:T(8,128)}, u32[]{:S(2)}) copy-start(f32[2,720,96]{2,1,0:T(8,128)} %copy-done.1) | copy-start | bytes 1658884
  66.3 14.7 %all-to-all-start.3 = ((f32[8,48,384]{2,1,0:T(8,128)}), f32[8,48,384]{2,1,0:T(8,128)S(1)}, u32[]{:S(2)}, u32[]{:S(2)}) async-start(f32[8,48,384]{2,1,0:T(8,128)} %bitcast.40), calls=%async_computation.3 | async-start | bytes 1179648 | tf_op jit(solution)/shard_map/all_to_all | solution.py:206
  81.0 0.8 copy-start.7
  81.8 16.1 %all-to-all-start.2 = ((f32[8,2,96,96]{3,2,1,0:T(8,128)}), f32[8,2,96,96]{3,2,1,0:T(8,128)S(1)}, u32[]{:S(2)}, u32[]{:S(2)}) async-start(f32[8,2,96,96]{3,2,1,0:T(8,128)} %bitcast.81), calls=%async_computation.2 | async-start | bytes 1572864 | tf_op jit(solution)/shard_map/all_to_all | solution.py:206
  85.4 2.4 %copy-start.8 = (f32[8,48,384]{2,1,0:T(8,128)S(1)}, f32[8,48,384]{2,1,0:T(8,128)}, u32[]{:S(2)}) copy-start(f32[8,48,384]{2,1,0:T(8,128)} %copy-done.7) | copy-start | bytes 1769476
  85.4 6.7 %copy-start.4 = (bf16[5,4,32,96]{3,2,1,0:T(8,128)(2,1)S(1)}, bf16[5,4,32,96]{3,2,1,0:T(8,128)(2,1)}, u32[]{:S(2)}) copy-start(bf16[5,4,32,96]{3,2,1,0:T(8,128)(2,1)} %copy-done.3) | copy-start | bytes 368644
  88.0 13.4 %collective-permute-start.8 = (f32[48,96]{1,0:T(8,128)S(1)}, f32[48,96]{1,0:T(8,128)S(1)}, u32[]{:S(2)}, u32[]{:S(2)}) collective-permute-start(f32[48,96]{1,0:T(8,128)S(1)} %bitcast.110), channel_id=1, source_target_pairs={{0,1},{1,2},{2,3},{3,0},{4,5},{5,6},{6,7},{7,4},{8,9},{9,10},{10,1... | collective-permute-start | bytes 55304 | tf_op jit(solution)/shard_map/ppermute | solution.py:113
  88.1 13.4 %collective-permute-start.7 = (f32[48,96]{1,0:T(8,128)S(1)}, f32[48,96]{1,0:T(8,128)S(1)}, u32[]{:S(2)}, u32[]{:S(2)}) collective-permute-start(f32[48,96]{1,0:T(8,128)S(1)} %bitcast.109), channel_id=1, source_target_pairs={{0,2},{1,3},{2,0},{3,1},{4,6},{5,7},{6,4},{7,5},{8,10},{9,11},{10,... | collective-permute-start | bytes 55304 | tf_op jit(solution)/shard_map/ppermute | solution.py:113
  88.1 13.3 %collective-permute-start.6 = (f32[48,96]{1,0:T(8,128)S(1)}, f32[48,96]{1,0:T(8,128)S(1)}, u32[]{:S(2)}, u32[]{:S(2)}) collective-permute-start(f32[48,96]{1,0:T(8,128)S(1)} %bitcast.108), channel_id=1, source_target_pairs={{0,3},{1,0},{2,1},{3,2},{4,7},{5,4},{6,5},{7,6},{8,11},{9,8},{10,9... | collective-permute-start | bytes 55304 | tf_op jit(solution)/shard_map/ppermute | solution.py:113
  92.9 9.3 %collective-permute-start.9 = (bf16[2,96,720]{2,1,0:T(8,128)(2,1)}, bf16[2,96,720]{2,1,0:T(8,128)(2,1)S(1)}, u32[]{:S(2)}, u32[]{:S(2)}) collective-permute-start(bf16[2,96,720]{2,1,0:T(8,128)(2,1)} %get-tuple-element.52), channel_id=1, source_target_pairs={{0,3},{1,0},{2,1},{3,2},{4,7},{5,4},{6,5},{7,6},{8,11},{9,8},{10,9... | collective-permute-start | bytes 829448 | tf_op jit(solution)/shard_map/ppermute | solution.py:113
  93.5 27.4 %collective-permute-start.10 = (bf16[2,96,720]{2,1,0:T(8,128)(2,1)S(1)}, bf16[2,96,720]{2,1,0:T(8,128)(2,1)S(1)}, u32[]{:S(2)}, u32[]{:S(2)}) collective-permute-start(bf16[2,96,720]{2,1,0:T(8,128)(2,1)S(1)} %get-tuple-element.53), channel_id=1, source_target_pairs={{0,2},{1,3},{2,0},{3,1},{4,6},{5,7},{6,4},{7,5},{8,10},{9,11},{10,... | collective-permute-start | bytes 829448 | tf_op jit(solution)/shard_map/ppermute | solution.py:113
  97.9 23.2 %all-to-all-start.1 = ((bf16[8,2,2,20,96]{4,2,3,1,0:T(2,128)(2,1)}), bf16[8,2,2,20,96]{4,2,3,1,0:T(2,128)(2,1)S(1)}, u32[]{:S(2)}, u32[]{:S(2)}) async-start(bf16[8,2,2,20,96]{4,2,3,1,0:T(2,128)(2,1)} %copy.128), calls=%async_computation.1 | async-start | bytes 327680 | tf_op jit(solution)/shard_map/all_to_all | solution.py:289
  101.4 19.6 %collective-permute-start.11 = (bf16[2,96,720]{2,1,0:T(8,128)(2,1)S(1)}, bf16[2,96,720]{2,1,0:T(8,128)(2,1)S(1)}, u32[]{:S(2)}, u32[]{:S(2)}) collective-permute-start(bf16[2,96,720]{2,1,0:T(8,128)(2,1)S(1)} %get-tuple-element.54), channel_id=1, source_target_pairs={{0,1},{1,2},{2,3},{3,0},{4,5},{5,6},{6,7},{7,4},{8,9},{9,10},{10,1... | collective-permute-start | bytes 829448 | tf_op jit(solution)/shard_map/ppermute | solution.py:113
  121.1 1.0 copy-start.9
  122.1 16.5 %all-to-all-start.4 = ((f32[8,240,96]{1,2,0:T(8,128)}), f32[8,240,96]{1,2,0:T(8,128)S(1)}, u32[]{:S(2)}, u32[]{:S(2)}) async-start(f32[8,240,96]{1,2,0:T(8,128)} %broadcast_in_dim.86), calls=%async_computation.4 | async-start | bytes 1572864 | tf_op jit(solution)/shard_map/all_to_all | solution.py:211
  126.3 0.9 copy-start.10

commit v6 on v3

--- a/solution.py
+++ b/solution.py
@@ -106,6 +106,16 @@
     )(lower, leg_masked, received, lead, tail)
 
 
+def arrivals(pick):
+    count = lax.axis_size("chan")
+    me = lax.axis_index("chan")
+    arrived = [pick(me, 0)]
+    for step in range(1, count):
+        pairs = [(source, (source - step) % count) for source in range(count)]
+        arrived.append(lax.ppermute(pick(lax.rem(me + count - step, count), step), "chan", pairs))
+    return arrived
+
+
 def exchange(blocks):
     count = lax.axis_size("chan")
     me = lax.axis_index("chan")
@@ -118,6 +128,41 @@
     return lax.dynamic_slice_in_dim(twice, lax.rem(count - me, count), count, 0)
 
 
+def output_kernel(count, me_ref, rows_ref, basis_ref, *refs):
+    homes, outs, placed = refs[:count], refs[count : count + 2], refs[count + 2]
+    pieces = count // 2
+    me = me_ref[0]
+    for step in range(count):
+        placed[lax.rem(me + step, count)] = homes[step][...]
+    for part in range(2):
+        for half in range(2):
+            rows = rows_ref[part, half].astype(jnp.float32).T.astype(jnp.bfloat16)
+            grid = jnp.dot(rows, basis_ref[...], preferred_element_type=jnp.float32)
+            skip = jnp.concatenate(
+                [placed[half * pieces + p, part].astype(jnp.float32) for p in range(pieces)], axis=1
+            )
+            outs[part][0, half] = (grid + skip).astype(jnp.bfloat16)
+
+
+def output_stage(me, rows, basis, homes):
+    count = len(homes)
+    width = rows.shape[3]
+    longitudes = basis.shape[1]
+    whole = pl.BlockSpec(memory_space=pltpu.VMEM)
+    out = jax.ShapeDtypeStruct((1, 2, width, longitudes), jnp.bfloat16)
+    return pl.pallas_call(
+        functools.partial(output_kernel, count),
+        out_shape=(out, out),
+        in_specs=[pl.BlockSpec(memory_space=pltpu.SMEM)] + [whole] * (2 + count),
+        out_specs=(whole, whole),
+        scratch_shapes=[pltpu.VMEM((count, *homes[0].shape), jnp.bfloat16)],
+        compiler_params=pltpu.CompilerParams(vmem_limit_bytes=40 * 2**20),
+        cost_estimate=pl.CostEstimate(
+            flops=8 * rows.shape[2] * width * longitudes, bytes_accessed=2**22, transcendentals=0
+        ),
+    )(me[None], rows, basis, *homes)
+
+
 def scattered_rows(array):
     lat_count = lax.axis_size("lat")
     groups, rows, columns = array.shape
@@ -150,9 +195,11 @@
     chan_count = lax.axis_size("chan")
     pieces = chan_count // 2
     span = longitudes // pieces
+    me = lax.axis_index("chan")
     both_fields = jnp.stack([grid_field[0], cotangent[0]], axis=0)
     cut = both_fields.reshape(2, 2, chan_width, pieces, span).transpose(1, 3, 0, 2, 4)
-    sliced = exchange(cut.reshape(chan_count, 2, chan_width, span))
+    cut = cut.reshape(chan_count, 2, chan_width, span)
+    sliced = exchange(cut)
     mixing_blocks = exchange(jnp.broadcast_to(mixing[None], (chan_count, *mixing.shape)))
     mixing_full = mixing_blocks.transpose(1, 0, 2).reshape(mixing.shape[0], -1)
     slot_orders = jnp.stack([pair_table, order_count - 1 - pair_table], axis=1).reshape(-1)
@@ -197,21 +244,18 @@
 
     synth, grad_local = owner_stage(lower, leg_masked, received, spectral, order_count)
     synth = synth.reshape(owned, 2, 2, 2, 2, npairs, chan_width)
-    back = jnp.transpose(synth, (5, 0, 1, 2, 3, 4, 6))
+    back = jnp.transpose(synth, (5, 1, 3, 2, 0, 4, 6))
+    back = back.reshape(npairs, 2, 2, 4 * owned, chan_width)
     rows = lax.all_to_all(back, "lat", split_axis=0, concat_axis=0, tiled=True)
-    rows = jnp.transpose(rows, (2, 4, 3, 0, 1, 5, 6)).reshape(
-        2, 2, 2, order_count, chan_width
-    )
-    row_y = rows[0] * weight_m.astype(jnp.bfloat16)[None, None, :, None]
-    row_dx = rows[1]
-    filtered_grid = jnp.einsum(
-        "hrmc,rmj->hcj", row_y, basis, preferred_element_type=jnp.float32
-    )
-    back_grid = jnp.einsum("hrmc,rmj->hcj", row_dx, basis, preferred_element_type=jnp.float32)
+    rows = jnp.transpose(rows, (1, 2, 0, 3, 4)).reshape(2, 2, 2 * order_count, chan_width)
+    by_device = lambda a: a.reshape(2, lat_count, 2 * owned, -1).transpose(1, 0, 2, 3)
+    row_scale = by_device(jnp.stack([weight_m, weight_m]).astype(jnp.bfloat16))
+    row_scale = row_scale.reshape(2 * order_count, 1)
+    rows = jnp.stack([rows[0] * row_scale, rows[1]], axis=0)
+    row_basis = by_device(basis).reshape(2 * order_count, longitudes)
     channels = chan_count * chan_width
     field_slice = sliced[:, 0].reshape(channels, span)
     cot_slice = sliced[:, 1].reshape(channels, span)
-    mixing_grad = jnp.einsum("ij,oj->io", field_slice, cot_slice, preferred_element_type=jnp.float32)
     skip_slice = jnp.einsum("io,ij->oj", mixing_full, field_slice, preferred_element_type=jnp.float32)
     back_slice = jnp.einsum("io,oj->ij", mixing_full, cot_slice, preferred_element_type=jnp.float32)
     mixed = jnp.stack(
@@ -221,22 +265,26 @@
         ],
         axis=1,
     )
-    home = exchange(mixed)
-    home = home.reshape(2, pieces, 2, chan_width, span).transpose(2, 0, 3, 1, 4)
-    home = home.reshape(2, 2, chan_width, longitudes).astype(jnp.float32)
-    block_output = (filtered_grid + home[0]).astype(jnp.bfloat16)[None]
-    grad_input = (back_grid + home[1]).astype(jnp.bfloat16)[None]
-
+    mixed, grad_local, field_slice = lax.optimization_barrier((mixed, grad_local, field_slice))
+    mixing_grad = jnp.einsum("ij,oj->io", field_slice, cot_slice, preferred_element_type=jnp.float32)
+    homes = arrivals(
+        lambda owner, step: lax.dynamic_index_in_dim(mixed, owner, 0, keepdims=False)
+    )
     mixing_share = scatter_sum(scattered_rows(mixing_grad[None])[:, 0], "lat")
     by_owner = mixing_share.reshape(-1, chan_count, chan_width).transpose(1, 0, 2)
-    mixing_share = jnp.sum(exchange(by_owner), axis=0)
+    shares = arrivals(
+        lambda owner, step: lax.dynamic_index_in_dim(by_owner, owner, 0, keepdims=False)
+    )
+    mixing_share = functools.reduce(jnp.add, shares)
     weight_share = scatter_sum(scattered_rows(grad_local), "lat")
     weight_rows = weight_share.shape[1]
     shares = jnp.concatenate([weight_share.reshape(-1, chan_width), mixing_share], axis=0)
+    shares, homes = lax.optimization_barrier((shares, homes))
     shares = spread(shares, "lat")
     weight_shares = shares[:, : 2 * weight_rows].reshape(-1, 2, weight_rows, chan_width)
     weight_sum = joined_rows(weight_shares, degrees)
     mixing_sum = joined_rows(shares[:, None, 2 * weight_rows :], channels)[0]
+    block_output, grad_input = output_stage(me, rows, row_basis, homes)
     grad_weights = jnp.transpose(weight_sum, (2, 0, 1)) / math.sqrt(order_count)
     grad_mixing = mixing_sum / math.sqrt(2 * npairs * longitudes)
     return (block_output, grad_input, grad_weights, grad_mixing)

time: 137 us -> 136 us (level)
  local copies, waits for them, and re-layouts: 52.4 us -> 33.9 us
  waiting for transfers between devices: 17.2 us -> 32.7 us
  matrix products: 7.87 us -> 3.2 us
  other arithmetic: 9.6 us -> 12.3 us
  starting transfers between devices: 38.5 us -> 40.9 us
  Pallas kernels: 9 us -> 10.6 us
    ppermute x0 -> x6, waiting for transfers between devices: none -> 15.7 us  [arrivals(): lax.ppermute(pick(lax.rem(me + count - step, count), step), 'chan', pairs)]
    ppermute x0 -> x6, starting transfers between devices: none -> 12.1 us  [arrivals(): lax.ppermute(pick(lax.rem(me + count - step, count), step), 'chan', pairs)]
    ppermute x12 -> x6, waiting for transfers between devices: 11.3 us -> 0.02 us  [exchange(): arrived.append(lax.ppermute(pick(me + count - step), 'chan', pairs))]
    all_to_all x1, waiting for transfers between devices: 0.01 us -> 9.39 us  [spread(): return lax.all_to_all(everywhere, axis, 0, 0, tiled=True)]
    ppermute x12 -> x6, starting transfers between devices: 18.9 us -> 10.1 us  [exchange(): arrived.append(lax.ppermute(pick(me + count - step), 'chan', pairs))]
    unnamed x50 -> x42, local copies, waits for them, and re-layouts: 24.3 us -> 15.9 us
    slice x6 -> x2, local copies, waits for them, and re-layouts: 7.14 us -> 0.13 us  [local(): rows = jnp.stack([rows[0] * row_scale, rows[1]], axis=0)]
    dot_general x2 -> x0, matrix products: 3.42 us -> none  [the longest x1 2.19 us: local(): jnp.einsum('hrmc,rmj->hcj', row_dx, basis, preferred_element_type=jnp.flo...]
  transfers between devices with their start and end apart: 17 -> 17, of which waited for: 4 -> 5; matrix products, arithmetic and copies ran while one was open for 47% -> 25% of each run, Pallas kernels for 7% -> 8%
where the time goes in v6:
time: 136 us; the launch traced here: 135 us
  starting transfers between devices  40.9 us (30%)
  local copies, waits for them, and re-layouts  33.9 us (25%)
  waiting for transfers between devices  32.7 us (24%)
  other arithmetic  12.3 us (9%)
  Pallas kernels  10.6 us (8%)
  matrix products  3.2 us (2%)
    unnamed x42, local copies, waits for them, and re-layouts  15.9 us
    ppermute x6, waiting for transfers between devices, arrivals(): lax.ppermute(pick(lax.rem(me + count - step, count), step), 'chan', pairs)  15.7 us
    ppermute x6, starting transfers between devices, arrivals(): lax.ppermute(pick(lax.rem(me + count - step, count), step), 'chan', pairs)  12.1 us
    ppermute x6, starting transfers between devices, exchange(): arrived.append(lax.ppermute(pick(me + count - step), 'chan', pairs))  10.1 us
    all_to_all x1, waiting for transfers between devices, spread(): return lax.all_to_all(everywhere, axis, 0, 0, tiled=True)  9.39 us
    pallas_call x1, Pallas kernels, owner_stage(): pl.pallas_call(functools.partial(owner_kernel, degrees, tail_shift, 128),...  9.01 us
    all_to_all x2, starting transfers between devices, scatter_sum(): return jnp.sum(lax.all_to_all(array, axis, 0, 0, tiled=True), axis=0)  7.79 us
    all_to_all x2, waiting for transfers between devices, scatter_sum(): return jnp.sum(lax.all_to_all(array, axis, 0, 0, tiled=True), axis=0)  7.58 us
  transfers between devices with their start and end apart: 17, of which 5 were waited for; matrix products, arithmetic and copies ran while one was open for 25% of the time, Pallas kernels for 8%

profile of v6, /device:TPU:0, one launch (start us, length us, event | category | flops | bytes accessed | tf_op | source)
XLA Modules:
  0.0 134.7 jit_solution(357555750305113478)
XLA Ops:
  0.6 5.1 %collective-permute-start = (bf16[1,384,96]{1,2,0:T(8,128)(2,1)}, bf16[1,384,96]{1,2,0:T(8,128)(2,1)}, u32[]{:S(2)}, u32[]{:S(2)}) collective-permute-start(bf16[1,384,96]{1,2,0:T(8,128)(2,1)} %bitcast.123), channel_id=1, source_target_pairs={{0,3},{1,0},{2,1},{3,2},{4,7},{5,4},{6,5},{7,6},{8,11},{9,8},{10,9... | collective-permute-start | bytes 221192 | tf_op jit(solution)/shard_map/ppermute | solution.py:126
  5.7 1.0 collective-permute-start.2
  6.7 1.4 %pad_maximum_fusion = bf16[2,2,96,1440]{3,2,1,0:T(8,128)(2,1)S(1)} fusion(bf16[1,2,96,1440]{3,2,1,0:T(8,128)(2,1)} %param.7, bf16[1,2,96,1440]{3,2,1,0:T(8,128)(2,1)} %param.6), kind=kLoop, calls=%fused_computation.2 | loop fusion | flops 552960 | bytes 2211840 | tf_op jit(solution)/shard_map/stack | solution.py:199
  8.1 1.3 reshape.465
  9.6 1.1 constant_dynamic-slice_fusion.6
  10.7 2.8 %collective-permute-start.3 = (bf16[1,2,96,720]{3,2,0,1:T(8,128)(2,1)}, bf16[1,2,96,720]{3,2,0,1:T(8,128)(2,1)}, u32[]{:S(2)}, u32[]{:S(2)}) collective-permute-start(bf16[1,2,96,720]{3,2,0,1:T(8,128)(2,1)} %get-tuple-element.63), channel_id=1, source_target_pairs={{0,3},{1,0},{2,1},{3,2},{4,7},{5,4},{6,5},{7,6},{8,11},{9,8},{10,9... | collective-permute-start | bytes 829448 | tf_op jit(solution)/shard_map/ppermute | solution.py:126
  13.5 1.1 collective-permute-start.4
  14.9 2.3 %multiply_convert_fusion.3 = (bf16[1,80,1440]{2,1,0:T(8,128)(2,1)S(1)}, bf16[1,80,1440]{2,1,0:T(8,128)(2,1)S(1)}) fusion(s32[80]{0:T(128)S(1)} %mul.146), kind=kLoop, calls=%fused_computation.26 | loop fusion | flops 1612800 | bytes 461120 | tf_op jit(solution)/shard_map/convert.12
  18.0 0.9 copy_bitcast_fusion.1
  18.9 3.7 %all-to-all-start = ((bf16[8,5,2,2,2,2,96]{6,5,4,3,2,1,0:T(2,128)(2,1)}), bf16[8,5,2,2,2,2,96]{6,5,4,3,2,1,0:T(2,128)(2,1)S(1)}, u32[]{:S(2)}, u32[]{:S(2)}) async-start(bf16[8,5,2,2,2,2,96]{6,5,4,3,2,1,0:T(2,128)(2,1)} %copy_bitcast_fusion.1), calls=%async_computation | async-start | bytes 327680 | tf_op jit(solution)/shard_map/all_to_all | solution.py:221
  24.2 1.2 pad.18.tail_ref
  25.4 1.5 %constant_dynamic-update-slice_fusion.5 = bf16[7,384,96]{1,2,0:T(8,128)(2,1)} fusion(bf16[7,384,96]{1,2,0:T(8,128)(2,1)} %constant_dynamic-update-slice_fusion.6, bf16[1,384,96]{1,2,0:T(8,128)(2,1)} %collective-permute-done), kind=kLoop, calls=%fused_computation.62 | loop fusion | bytes 147456
  26.9 1.5 %constant_dynamic-update-slice_fusion.4 = bf16[7,384,96]{1,2,0:T(8,128)(2,1)} fusion(bf16[7,384,96]{1,2,0:T(8,128)(2,1)} %constant_dynamic-update-slice_fusion.5, bf16[1,384,96]{1,2,0:T(8,128)(2,1)} %collective-permute-done.1), kind=kLoop, calls=%fused_computation.61 | loop fusion | bytes 147456
  28.5 1.5 %constant_dynamic-update-slice_fusion.3 = bf16[7,384,96]{1,2,0:T(8,128)(2,1)} fusion(bf16[7,384,96]{1,2,0:T(8,128)(2,1)} %constant_dynamic-update-slice_fusion.4, bf16[1,384,96]{1,2,0:T(8,128)(2,1)} %collective-permute-done.2), kind=kLoop, calls=%fused_computation.60 | loop fusion | bytes 147456
  30.0 1.5 %constant_dynamic-update-slice_fusion.2 = bf16[7,384,96]{1,2,0:T(8,128)(2,1)} fusion(bf16[7,384,96]{1,2,0:T(8,128)(2,1)} %constant_dynamic-update-slice_fusion.3, bf16[384,96]{0,1:T(8,128)(2,1)} %param.10), kind=kLoop, calls=%fused_computation.59 | loop fusion | bytes 147456
  31.5 1.5 %constant_dynamic-update-slice_fusion.1 = bf16[7,384,96]{1,2,0:T(8,128)(2,1)} fusion(bf16[7,384,96]{1,2,0:T(8,128)(2,1)} %constant_dynamic-update-slice_fusion.2, bf16[1,384,96]{1,2,0:T(8,128)(2,1)} %collective-permute-done), kind=kLoop, calls=%fused_computation.58 | loop fusion | bytes 147456
  33.0 1.5 %constant_dynamic-update-slice_fusion = bf16[7,384,96]{1,2,0:T(8,128)(2,1)} fusion(bf16[7,384,96]{1,2,0:T(8,128)(2,1)} %constant_dynamic-update-slice_fusion.1, bf16[1,384,96]{1,2,0:T(8,128)(2,1)} %collective-permute-done.1), kind=kLoop, calls=%fused_computation.57 | loop fusion | bytes 147456 | tf_op jit(solution)/shard_map/concatenate | solution.py:127
  34.5 1.7 %constant_dynamic-slice_fusion.9 = bf16[4,384,96]{1,2,0:T(8,128)(2,1)} fusion(bf16[7,384,96]{1,2,0:T(8,128)(2,1)} %constant_dynamic-update-slice_fusion, s32[]{:T(128)S(6)} %select_n.145), kind=kLoop, calls=%fused_computation.81 | loop fusion | bytes 589828 | tf_op jit(solution)/shard_map/dynamic_slice | solution.py:128
  36.3 1.4 %copy-done = f32[2,1408,96]{2,1,0:T(8,128)S(1)} copy-done((f32[2,1408,96]{2,1,0:T(8,128)S(1)}, f32[2,1408,96]{2,1,0:T(8,128)}, u32[]{:S(2)}) %copy-start) | copy-done | bytes 1081368
  37.7 9.0 %shard_map.93 = (bf16[5,4,32,96]{3,2,1,0:T(8,128)(2,1)S(1)}, f32[2,720,96]{2,1,0:T(8,128)S(1)}) custom-call(s32[5]{0:T(128)S(1)} %get-tuple-element.53.lower_ref, bf16[5,32,1408]{2,1,0:T(8,128)(2,1)S(1)} %select_bitcast_fusion.leg_ref, bf16[5,4,32,96]{3,2,1,0:T(8,128)(2,1)S(1)} %bitcast.98, f32[2,2128,96]{2,1,0:T(8,128)S(1)} %pad.17.lead_ref, ...), custom_call_target="tpu_custom_call" | custom-call | flops 346030080 | bytes 16777216 | tf_op jit(solution)/shard_map/pallas_call | solution.py:79
  46.7 1.0 constant_dynamic-update-slice_fusion.11
  47.7 1.0 constant_dynamic-update-slice_fusion.10
  48.7 1.0 constant_dynamic-update-slice_fusion.9
  49.7 1.0 dynamic-slice_dynamic-update-slice_fusion.1
  50.7 1.0 constant_dynamic-update-slice_fusion.8
  51.7 1.0 constant_dynamic-update-slice_fusion.7
  53.4 1.1 copy.154
  55.0 1.1 copy.155
  56.1 1.4 %pad_maximum_fusion.1 = bf16[4,2,96,720]{3,2,0,1:T(8,128)(2,1)S(1)} fusion(bf16[4,1,96,720]{3,2,0,1:T(8,128)(2,1)} %bitcast.115, bf16[4,1,96,720]{3,2,0,1:T(8,128)(2,1)} %bitcast.114), kind=kLoop, calls=%fused_computation.3 | loop fusion | flops 552960 | bytes 2211840 | tf_op jit(solution)/shard_map/stack | solution.py:261
  57.5 1.3 fusion.21
  58.8 4.2 %all-to-all-start.3 = ((f32[8,48,384]{2,1,0:T(8,128)}), f32[8,48,384]{2,1,0:T(8,128)S(1)}, u32[]{:S(2)}, u32[]{:S(2)}) async-start(f32[8,48,384]{2,1,0:T(8,128)} %fusion.21), calls=%async_computation.3 | async-start | bytes 1179648 | tf_op jit(solution)/shard_map/all_to_all | solution.py:175
  63.2 2.3 %multiply_convert_fusion.1 = (bf16[1,8,10,1440]{3,1,2,0:T(8,128)(2,1)S(1)}, bf16[1,8,10,1440]{3,1,2,0:T(8,128)(2,1)S(1)}) fusion(s32[8,10]{0,1:T(8,128)S(1)} %copy.151), kind=kLoop, calls=%fused_computation.21 | loop fusion | flops 1612800 | bytes 461120 | tf_op jit(solution)/shard_map/convert
  65.5 1.0 copy.172
  66.5 7.0 %all-to-all-done.3 = f32[8,48,384]{2,1,0:T(8,128)S(1)} async-done(((f32[8,48,384]{2,1,0:T(8,128)}), f32[8,48,384]{2,1,0:T(8,128)S(1)}, u32[]{:S(2)}, u32[]{:S(2)}) %all-to-all-start.3) | async-done | bytes 589856 | tf_op jit(solution)/shard_map/all_to_all | solution.py:175
  73.5 3.5 %all-to-all-start.2 = ((f32[8,2,96,96]{3,2,1,0:T(8,128)}), f32[8,2,96,96]{3,2,1,0:T(8,128)S(1)}, u32[]{:S(2)}, u32[]{:S(2)}) async-start(f32[8,2,96,96]{3,2,1,0:T(8,128)} %bitcast.96), calls=%async_computation.2 | async-start | bytes 1572864 | tf_op jit(solution)/shard_map/all_to_all | solution.py:175
  79.7 3.9 %collective-permute-start.6 = (f32[48,96]{1,0:T(8,128)S(1)}, f32[48,96]{1,0:T(8,128)S(1)}, u32[]{:S(2)}, u32[]{:S(2)}) collective-permute-start(f32[48,96]{1,0:T(8,128)S(1)} %bitcast.134), channel_id=1, source_target_pairs={{0,3},{1,0},{2,1},{3,2},{4,7},{5,4},{6,5},{7,6},{8,11},{9,8},{10,9... | collective-permute-start | bytes 55304 | tf_op jit(solution)/shard_map/ppermute | solution.py:115
  84.3 0.9 dynamic-slice_bitcast_fusion
  85.2 2.3 %collective-permute-start.10 = (bf16[2,96,720]{2,1,0:T(8,128)(2,1)}, bf16[2,96,720]{2,1,0:T(8,128)(2,1)S(1)}, u32[]{:S(2)}, u32[]{:S(2)}) collective-permute-start(bf16[2,96,720]{2,1,0:T(8,128)(2,1)} %get-tuple-element.57), channel_id=1, source_target_pairs={{0,2},{1,3},{2,0},{3,1},{4,6},{5,7},{6,4},{7,5},{8,10},{9,11},{10,... | collective-permute-start | bytes 829448 | tf_op jit(solution)/shard_map/ppermute | solution.py:115
  87.5 1.5 %collective-permute-start.11 = (bf16[2,96,720]{2,1,0:T(8,128)(2,1)}, bf16[2,96,720]{2,1,0:T(8,128)(2,1)S(1)}, u32[]{:S(2)}, u32[]{:S(2)}) collective-permute-start(bf16[2,96,720]{2,1,0:T(8,128)(2,1)} %get-tuple-element.56), channel_id=1, source_target_pairs={{0,1},{1,2},{2,3},{3,0},{4,5},{5,6},{6,7},{7,4},{8,9},{9,10},{10,1... | collective-permute-start | bytes 829448 | tf_op jit(solution)/shard_map/ppermute | solution.py:115
  89.5 3.5 %all-to-all-start.1 = ((bf16[8,2,2,20,96]{4,2,3,1,0:T(2,128)(2,1)}), bf16[8,2,2,20,96]{4,2,3,1,0:T(2,128)(2,1)S(1)}, u32[]{:S(2)}, u32[]{:S(2)}) async-start(bf16[8,2,2,20,96]{4,2,3,1,0:T(2,128)(2,1)} %copy.145), calls=%async_computation.1 | async-start | bytes 327680 | tf_op jit(solution)/shard_map/all_to_all | solution.py:249
  93.1 3.8 %collective-permute-start.9 = (bf16[2,96,720]{2,1,0:T(8,128)(2,1)}, bf16[2,96,720]{2,1,0:T(8,128)(2,1)S(1)}, u32[]{:S(2)}, u32[]{:S(2)}) collective-permute-start(bf16[2,96,720]{2,1,0:T(8,128)(2,1)} %get-tuple-element.58), channel_id=1, source_target_pairs={{0,3},{1,0},{2,1},{3,2},{4,7},{5,4},{6,5},{7,6},{8,11},{9,8},{10,9... | collective-permute-start | bytes 829448 | tf_op jit(solution)/shard_map/ppermute | solution.py:115
  97.7 11.2 %collective-permute-done.10.refs_2_ = bf16[2,96,720]{2,1,0:T(8,128)(2,1)S(1)} collective-permute-done((bf16[2,96,720]{2,1,0:T(8,128)(2,1)}, bf16[2,96,720]{2,1,0:T(8,128)(2,1)S(1)}, u32[]{:S(2)}, u32[]{:S(2)}) %collective-permute-start.10) | collective-permute-done | bytes 276512 | tf_op jit(solution)/shard_map/ppermute | solution.py:115
  108.9 4.5 %collective-permute-done.9.refs_1_ = bf16[2,96,720]{2,1,0:T(8,128)(2,1)S(1)} collective-permute-done((bf16[2,96,720]{2,1,0:T(8,128)(2,1)}, bf16[2,96,720]{2,1,0:T(8,128)(2,1)S(1)}, u32[]{:S(2)}, u32[]{:S(2)}) %collective-permute-start.9) | collective-permute-done | bytes 276512 | tf_op jit(solution)/shard_map/ppermute | solution.py:115
  113.5 1.0 broadcast_in_dim.92
  114.5 3.8 %all-to-all-start.4 = ((f32[8,240,96]{1,2,0:T(8,128)}), f32[8,240,96]{1,2,0:T(8,128)S(1)}, u32[]{:S(2)}, u32[]{:S(2)}) async-start(f32[8,240,96]{1,2,0:T(8,128)} %broadcast_in_dim.92), calls=%async_computation.4 | async-start | bytes 1572864 | tf_op jit(solution)/shard_map/all_to_all | solution.py:180
  119.9 1.6 %shard_map.94 = (bf16[1,2,96,1440]{3,2,1,0:T(8,128)(2,1)}, bf16[1,2,96,1440]{3,2,1,0:T(8,128)(2,1)}) custom-call(s32[1]{0:T(128)} %bitcast.me_ref, bf16[2,2,160,96]{3,2,1,0:T(8,128)(2,1)S(1)} %pad_maximum_fusion.2.rows_ref, bf16[160,1440]{1,0:T(8,128)(2,1)S(1)} %reshape.463.basis_ref, bf16[2,96,720]{2,1,0:T(8,128)(2,1)S(1)} %get-tuple-element.21.refs_0_, ...), custom_call_target="tpu_custom_call" | custom-call | flops 176947200 | bytes 4194304 | tf_op jit(solution)/shard_map/pallas_call | solution.py:153
  121.4 9.4 %all-to-all-done.4 = f32[8,240,96]{1,2,0:T(8,128)S(1)} async-done(((f32[8,240,96]{1,2,0:T(8,128)}), f32[8,240,96]{1,2,0:T(8,128)S(1)}, u32[]{:S(2)}, u32[]{:S(2)}) %all-to-all-start.4) | async-done | bytes 737312 | tf_op jit(solution)/shard_map/all_to_all | solution.py:180
  132.5 1.1 fusion.1
  (100 shorter events, 13.3 us)
Async XLA Ops:
  0.6 24.8 %collective-permute-start = (bf16[1,384,96]{1,2,0:T(8,128)(2,1)}, bf16[1,384,96]{1,2,0:T(8,128)(2,1)}, u32[]{:S(2)}, u32[]{:S(2)}) collective-permute-start(bf16[1,384,96]{1,2,0:T(8,128)(2,1)} %bitcast.123), channel_id=1, source_target_pairs={{0,3},{1,0},{2,1},{3,2},{4,7},{5,4},{6,5},{7,6},{8,11},{9,8},{10,9... | collective-permute-start | bytes 221192 | tf_op jit(solution)/shard_map/ppermute | solution.py:126
  5.7 21.2 %collective-permute-start.1 = (bf16[1,384,96]{1,2,0:T(8,128)(2,1)}, bf16[1,384,96]{1,2,0:T(8,128)(2,1)}, u32[]{:S(2)}, u32[]{:S(2)}) collective-permute-start(bf16[1,384,96]{1,2,0:T(8,128)(2,1)} %bitcast.124), channel_id=1, source_target_pairs={{0,2},{1,3},{2,0},{3,1},{4,6},{5,7},{6,4},{7,5},{8,10},{9,11},{10,... | collective-permute-start | bytes 221192 | tf_op jit(solution)/shard_map/ppermute | solution.py:126
  5.7 22.7 %collective-permute-start.2 = (bf16[1,384,96]{1,2,0:T(8,128)(2,1)}, bf16[1,384,96]{1,2,0:T(8,128)(2,1)}, u32[]{:S(2)}, u32[]{:S(2)}) collective-permute-start(bf16[1,384,96]{1,2,0:T(8,128)(2,1)} %bitcast.125), channel_id=1, source_target_pairs={{0,1},{1,2},{2,3},{3,0},{4,5},{5,6},{6,7},{7,4},{8,9},{9,10},{10,1... | collective-permute-start | bytes 221192 | tf_op jit(solution)/shard_map/ppermute | solution.py:126
  9.4 5.2 %copy-start.10 = (s32[40]{0:T(128)S(1)}, s32[40]{0:T(128)}, u32[]{:S(2)}) copy-start(s32[40]{0:T(128)} %param.11) | copy-start | bytes 484
  9.4 7.8 %copy-start.5 = (bf16[1,2,96,1440]{3,2,1,0:T(8,128)(2,1)S(1)}, bf16[1,2,96,1440]{3,2,1,0:T(8,128)(2,1)}, u32[]{:S(2)}) copy-start(bf16[1,2,96,1440]{3,2,1,0:T(8,128)(2,1)} %param.6) | copy-start | bytes 1658884
  9.5 8.0 %copy-start.1 = (bf16[2,2,2,96,720]{4,3,1,0,2:T(8,128)(2,1)}, bf16[2,2,2,96,720]{4,3,1,0,2:T(8,128)(2,1)S(1)}, u32[]{:S(2)}) copy-start(bf16[2,2,2,96,720]{4,3,1,0,2:T(8,128)(2,1)S(1)} %copy.153) | copy-start | bytes 3317764
  9.6 8.0 %copy-start.6 = (bf16[1,2,96,1440]{3,2,1,0:T(8,128)(2,1)S(1)}, bf16[1,2,96,1440]{3,2,1,0:T(8,128)(2,1)}, u32[]{:S(2)}) copy-start(bf16[1,2,96,1440]{3,2,1,0:T(8,128)(2,1)} %param.7) | copy-start | bytes 1658884
  10.7 36.0 %collective-permute-start.3 = (bf16[1,2,96,720]{3,2,0,1:T(8,128)(2,1)}, bf16[1,2,96,720]{3,2,0,1:T(8,128)(2,1)}, u32[]{:S(2)}, u32[]{:S(2)}) collective-permute-start(bf16[1,2,96,720]{3,2,0,1:T(8,128)(2,1)} %get-tuple-element.63), channel_id=1, source_target_pairs={{0,3},{1,0},{2,1},{3,2},{4,7},{5,4},{6,5},{7,6},{8,11},{9,8},{10,9... | collective-permute-start | bytes 829448 | tf_op jit(solution)/shard_map/ppermute | solution.py:126
  13.5 34.2 %collective-permute-start.4 = (bf16[1,2,96,720]{3,2,0,1:T(8,128)(2,1)}, bf16[1,2,96,720]{3,2,0,1:T(8,128)(2,1)}, u32[]{:S(2)}, u32[]{:S(2)}) collective-permute-start(bf16[1,2,96,720]{3,2,0,1:T(8,128)(2,1)} %get-tuple-element.62), channel_id=1, source_target_pairs={{0,2},{1,3},{2,0},{3,1},{4,6},{5,7},{6,4},{7,5},{8,10},{9,11},{10,... | collective-permute-start | bytes 829448 | tf_op jit(solution)/shard_map/ppermute | solution.py:126
  14.6 2.5 %copy-start.12 = (s32[40,1]{0,1:T(1,128)}, s32[40,1]{0,1:T(1,128)S(1)}, u32[]{:S(2)}) copy-start(s32[40,1]{0,1:T(1,128)S(1)} %subtract_bitcast_fusion) | copy-start | bytes 484
  17.6 5.3 %copy-start.9 = (bf16[5,1361,8]{1,2,0:T(8,128)(2,1)S(1)}, bf16[5,1361,8]{1,2,0:T(8,128)(2,1)}, u32[]{:S(2)}) copy-start(bf16[5,1361,8]{1,2,0:T(8,128)(2,1)} %param.8) | copy-start | bytes 326644
  17.6 5.5 %copy-start.8 = (bf16[384,96]{0,1:T(8,128)(2,1)S(1)}, bf16[384,96]{0,1:T(8,128)(2,1)}, u32[]{:S(2)}) copy-start(bf16[384,96]{0,1:T(8,128)(2,1)} %param.10) | copy-start | bytes 221188
  18.0 5.8 %copy-start.7 = (f32[96,2,720]{2,1,0:T(2,128)S(1)}, f32[96,2,720]{2,1,0:T(2,128)}, u32[]{:S(2)}) copy-start(f32[96,2,720]{2,1,0:T(2,128)} %param.9) | copy-start | bytes 1658884
  18.9 17.3 %all-to-all-start = ((bf16[8,5,2,2,2,2,96]{6,5,4,3,2,1,0:T(2,128)(2,1)}), bf16[8,5,2,2,2,2,96]{6,5,4,3,2,1,0:T(2,128)(2,1)S(1)}, u32[]{:S(2)}, u32[]{:S(2)}) async-start(bf16[8,5,2,2,2,2,96]{6,5,4,3,2,1,0:T(2,128)(2,1)} %copy_bitcast_fusion.1), calls=%async_computation | async-start | bytes 327680 | tf_op jit(solution)/shard_map/all_to_all | solution.py:221
  25.4 23.3 %collective-permute-start.5 = (bf16[1,2,96,720]{3,2,0,1:T(8,128)(2,1)}, bf16[1,2,96,720]{3,2,0,1:T(8,128)(2,1)}, u32[]{:S(2)}, u32[]{:S(2)}) collective-permute-start(bf16[1,2,96,720]{3,2,0,1:T(8,128)(2,1)} %get-tuple-element.60), channel_id=1, source_target_pairs={{0,1},{1,2},{2,3},{3,0},{4,5},{5,6},{6,7},{7,4},{8,9},{9,10},{10,1... | collective-permute-start | bytes 829448 | tf_op jit(solution)/shard_map/ppermute | solution.py:126
  36.3 1.4 %copy-start = (f32[2,1408,96]{2,1,0:T(8,128)S(1)}, f32[2,1408,96]{2,1,0:T(8,128)}, u32[]{:S(2)}) copy-start(f32[2,1408,96]{2,1,0:T(8,128)} %pad.18.tail_ref) | copy-start | bytes 3244036
  37.7 9.0 %copy-start.4 = (bf16[7,2,96,720]{3,2,0,1:T(8,128)(2,1)S(1)}, bf16[7,2,96,720]{3,2,0,1:T(8,128)(2,1)}, u32[]{:S(2)}) copy-start(bf16[7,2,96,720]{3,2,0,1:T(8,128)(2,1)} %get-tuple-element.61) | copy-start | bytes 5806084
  49.7 3.1 %copy-start.2 = (bf16[4,384,96]{1,2,0:T(8,128)(2,1)S(1)}, bf16[4,384,96]{1,2,0:T(8,128)(2,1)}, u32[]{:S(2)}) copy-start(bf16[4,384,96]{1,2,0:T(8,128)(2,1)} %constant_dynamic-slice_fusion.9) | copy-start | bytes 884740
  58.8 14.7 %all-to-all-start.3 = ((f32[8,48,384]{2,1,0:T(8,128)}), f32[8,48,384]{2,1,0:T(8,128)S(1)}, u32[]{:S(2)}, u32[]{:S(2)}) async-start(f32[8,48,384]{2,1,0:T(8,128)} %fusion.21), calls=%async_computation.3 | async-start | bytes 1179648 | tf_op jit(solution)/shard_map/all_to_all | solution.py:175
  65.4 11.6 %copy-start.11 = (s32[40]{0:T(128)S(1)}, s32[40]{0:T(128)}, u32[]{:S(2)}) copy-start(s32[40]{0:T(128)} %param.11) | copy-start | bytes 484
  65.4 11.6 %copy-start.13 = (s32[40,1]{0,1:T(1,128)S(1)}, s32[40,1]{0,1:T(1,128)}, u32[]{:S(2)}) copy-start(s32[40,1]{0,1:T(1,128)} %copy-done.12) | copy-start | bytes 484
  73.5 16.1 %all-to-all-start.2 = ((f32[8,2,96,96]{3,2,1,0:T(8,128)}), f32[8,2,96,96]{3,2,1,0:T(8,128)S(1)}, u32[]{:S(2)}, u32[]{:S(2)}) async-start(f32[8,2,96,96]{3,2,1,0:T(8,128)} %bitcast.96), calls=%async_computation.2 | async-start | bytes 1572864 | tf_op jit(solution)/shard_map/all_to_all | solution.py:175
  79.7 13.4 %collective-permute-start.6 = (f32[48,96]{1,0:T(8,128)S(1)}, f32[48,96]{1,0:T(8,128)S(1)}, u32[]{:S(2)}, u32[]{:S(2)}) collective-permute-start(f32[48,96]{1,0:T(8,128)S(1)} %bitcast.134), channel_id=1, source_target_pairs={{0,3},{1,0},{2,1},{3,2},{4,7},{5,4},{6,5},{7,6},{8,11},{9,8},{10,9... | collective-permute-start | bytes 55304 | tf_op jit(solution)/shard_map/ppermute | solution.py:115
  83.6 13.3 %collective-permute-start.7 = (f32[48,96]{1,0:T(8,128)S(1)}, f32[48,96]{1,0:T(8,128)S(1)}, u32[]{:S(2)}, u32[]{:S(2)}) collective-permute-start(f32[48,96]{1,0:T(8,128)S(1)} %bitcast.133), channel_id=1, source_target_pairs={{0,2},{1,3},{2,0},{3,1},{4,6},{5,7},{6,4},{7,5},{8,10},{9,11},{10,... | collective-permute-start | bytes 55304 | tf_op jit(solution)/shard_map/ppermute | solution.py:115
  83.6 13.3 %collective-permute-start.8 = (f32[48,96]{1,0:T(8,128)S(1)}, f32[48,96]{1,0:T(8,128)}, u32[]{:S(2)}, u32[]{:S(2)}) collective-permute-start(f32[48,96]{1,0:T(8,128)S(1)} %bitcast.132), channel_id=1, source_target_pairs={{0,1},{1,2},{2,3},{3,0},{4,5},{5,6},{6,7},{7,4},{8,9},{9,10},{10,1... | collective-permute-start | bytes 55304 | tf_op jit(solution)/shard_map/ppermute | solution.py:115
  85.2 23.7 %collective-permute-start.10 = (bf16[2,96,720]{2,1,0:T(8,128)(2,1)}, bf16[2,96,720]{2,1,0:T(8,128)(2,1)S(1)}, u32[]{:S(2)}, u32[]{:S(2)}) collective-permute-start(bf16[2,96,720]{2,1,0:T(8,128)(2,1)} %get-tuple-element.57), channel_id=1, source_target_pairs={{0,2},{1,3},{2,0},{3,1},{4,6},{5,7},{6,4},{7,5},{8,10},{9,11},{10,... | collective-permute-start | bytes 829448 | tf_op jit(solution)/shard_map/ppermute | solution.py:115
  87.5 31.6 %copy-start.3 = (bf16[8,2,10,1440]{3,0,2,1:T(8,128)(2,1)S(1)}, bf16[8,2,10,1440]{3,0,2,1:T(8,128)(2,1)}, u32[]{:S(2)}) copy-start(bf16[8,2,10,1440]{3,0,2,1:T(8,128)(2,1)} %maximum_bitcast_fusion.1) | copy-start | bytes 1382404
  87.5 21.4 %collective-permute-start.11 = (bf16[2,96,720]{2,1,0:T(8,128)(2,1)}, bf16[2,96,720]{2,1,0:T(8,128)(2,1)S(1)}, u32[]{:S(2)}, u32[]{:S(2)}) collective-permute-start(bf16[2,96,720]{2,1,0:T(8,128)(2,1)} %get-tuple-element.56), channel_id=1, source_target_pairs={{0,1},{1,2},{2,3},{3,0},{4,5},{5,6},{6,7},{7,4},{8,9},{9,10},{10,1... | collective-permute-start | bytes 829448 | tf_op jit(solution)/shard_map/ppermute | solution.py:115
  89.5 23.9 %all-to-all-start.1 = ((bf16[8,2,2,20,96]{4,2,3,1,0:T(2,128)(2,1)}), bf16[8,2,2,20,96]{4,2,3,1,0:T(2,128)(2,1)S(1)}, u32[]{:S(2)}, u32[]{:S(2)}) async-start(bf16[8,2,2,20,96]{4,2,3,1,0:T(2,128)(2,1)} %copy.145), calls=%async_computation.1 | async-start | bytes 327680 | tf_op jit(solution)/shard_map/all_to_all | solution.py:249
  93.1 20.3 %collective-permute-start.9 = (bf16[2,96,720]{2,1,0:T(8,128)(2,1)}, bf16[2,96,720]{2,1,0:T(8,128)(2,1)S(1)}, u32[]{:S(2)}, u32[]{:S(2)}) collective-permute-start(bf16[2,96,720]{2,1,0:T(8,128)(2,1)} %get-tuple-element.58), channel_id=1, source_target_pairs={{0,3},{1,0},{2,1},{3,2},{4,7},{5,4},{6,5},{7,6},{8,11},{9,8},{10,9... | collective-permute-start | bytes 829448 | tf_op jit(solution)/shard_map/ppermute | solution.py:115
  114.5 16.4 %all-to-all-start.4 = ((f32[8,240,96]{1,2,0:T(8,128)}), f32[8,240,96]{1,2,0:T(8,128)S(1)}, u32[]{:S(2)}, u32[]{:S(2)}) async-start(f32[8,240,96]{1,2,0:T(8,128)} %broadcast_in_dim.92), calls=%async_computation.4 | async-start | bytes 1572864 | tf_op jit(solution)/shard_map/all_to_all | solution.py:180
